TPU v7x, 128 devices: a whole 4x4x4 slice. The times are simulated.
128 devices in a mesh: req: 16 (over y, x), tp: 8 (over z, core).
Axes of the slice: x: 4, y: 4, z: 4, core: 2. Of those that a mesh axis runs over, the one named last changes fastest.
Arguments:
- tokens: bfloat16 [16, 384, 8192], P('req', 'tp'), may hold values from -6 to 6
- norm_gain: bfloat16 [8192], replicated, may hold values from 0.099609375 to 1.8984375
- w_query: bfloat16 [8192, 8192], P(None, 'tp'), may hold values from -3 to 3
- w_key: bfloat16 [8192, 1024], P(None, 'tp'), may hold values from -1 to 1
- w_value: bfloat16 [8192, 1024], P(None, 'tp'), may hold values from -0.0625 to 0.0625
- store_keys: bfloat16 [64, 512, 8, 128], P('req', None, 'tp'), may hold values from -6 to 6
- store_values: bfloat16 [64, 512, 8, 128], P('req', None, 'tp'), may hold values from -6 to 6
- block_slot: int32 [64], replicated, may hold values from 0 to 63, as said below
- retrieval: int32 [16, 8], replicated, may hold values from 0 to 63, as said below
- sel_index: int32 [16, 384], P('req'), may hold values from 0 to 4095, as said below
Outputs:
- attended: bfloat16 [16, 384, 8192], P('req', None, 'tp')
Inputs may be any that keep to these rules, and one draw needn't show every extreme that they name: `block_slot`: a permutation: slots 4 * s to 4 * s + 3 lie on store device s. `retrieval`: a request's 8 blocks lie on 8 different store devices. `sel_index`: a request's positions rise strictly, the first is 0 and the last 4095.
All inputs are finite; a program needn't handle non-finite values.
Results may differ from a plain program's by a relative error of at most 0.0064.
Values may be sent and summed in bfloat16 or wider, within the bound.
No kernel may reach another device: no remote copies, remote signals or barrier semaphores. Data moves between devices by JAX's collectives and lax.ppermute only.
A program may use at most 192 MiB of HBM per device.

v0:
```python
import jax
import jax.numpy as jnp
from jax import lax
from jax.sharding import PartitionSpec as P


def rotate(values, positions):
    half_dim = values.shape[-1] // 2
    frequency = 500000.0 ** (-(2.0 / values.shape[-1]) * jnp.arange(half_dim).astype(jnp.float32))
    angles = positions.astype(jnp.float32)[:, None] * frequency[None, :]
    cosine = jnp.cos(angles)[:, None, :]
    sines = jnp.sin(angles)[:, None, :]
    first = values[..., :half_dim]
    second = values[..., half_dim:]
    return jnp.concatenate(
        [first * cosine - second * sines, second * cosine + first * sines], axis=-1
    )


def on_device(
    tokens,
    norm_gain,
    w_query,
    w_key,
    w_value,
    store_keys,
    store_values,
    block_slot,
    retrieval,
    sel_index,
):
    block_len = store_keys.shape[1]
    kv_local = store_keys.shape[2]
    head_dim = store_keys.shape[3]
    q_width = w_query.shape[1]
    kv_width = w_key.shape[1]
    group = q_width // head_dim // kv_local
    hidden = lax.all_gather(tokens, "tp", axis=1, tiled=True)[0].astype(jnp.float32)
    scale_rows = lax.rsqrt(jnp.mean(hidden * hidden, axis=-1, keepdims=True) + 1e-05)
    normed = (hidden * scale_rows * norm_gain.astype(jnp.float32)).astype(jnp.bfloat16)
    joined = jnp.concatenate(
        [
            jnp.dot(normed, w_query, preferred_element_type=jnp.float32),
            jnp.dot(normed, w_key, preferred_element_type=jnp.float32),
            jnp.dot(normed, w_value, preferred_element_type=jnp.float32),
        ],
        axis=1,
    )
    projected = joined[None][0]
    sel_rows = projected.shape[0]
    positions = sel_index[0]
    query_raw = projected[:, :q_width].reshape(sel_rows, kv_local * group, head_dim)
    new_keys = (
        projected[:, q_width : q_width + kv_width]
        .astype(jnp.bfloat16)
        .reshape(sel_rows, kv_local, head_dim)
    )
    new_values = (
        projected[:, q_width + kv_width :]
        .astype(jnp.bfloat16)
        .reshape(sel_rows, kv_local, head_dim)
    )
    queries = rotate(query_raw, positions).astype(jnp.bfloat16)
    own_group = lax.axis_index("req")
    wanted = lax.dynamic_slice_in_dim(retrieval, own_group, 1, 0)[0]
    chosen = block_slot[wanted]
    all_keys, all_values = (
        lax.all_gather(store_keys, "req", axis=0, tiled=True),
        lax.all_gather(store_values, "req", axis=0, tiled=True),
    )
    ctx_keys = all_keys[chosen]
    ctx_values = all_values[chosen]
    context = ctx_keys.shape[0] * block_len
    ctx_keys = ctx_keys.reshape(context, kv_local, head_dim).at[positions].set(new_keys)
    ctx_values = ctx_values.reshape(context, kv_local, head_dim).at[positions].set(new_values)
    everywhere = jnp.arange(context)
    rot_keys = rotate(ctx_keys.astype(jnp.float32), everywhere).astype(jnp.bfloat16)
    grouped = queries.reshape(sel_rows, kv_local, group, head_dim)
    scores = jnp.einsum("sngd,cnd->ngsc", grouped, rot_keys, preferred_element_type=jnp.float32)
    scores = scores / jnp.sqrt(jnp.float32(head_dim))
    visible = everywhere[None, :] <= positions[:, None]
    scores = jnp.where(visible[None, None], scores, -jnp.inf)
    highest = jnp.max(scores, axis=-1, keepdims=True)
    expos = jnp.exp(scores - highest)
    weights = (expos / jnp.sum(expos, axis=-1, keepdims=True)).astype(jnp.bfloat16)
    mixed = jnp.einsum("ngsc,cnd->sngd", weights, ctx_values, preferred_element_type=jnp.float32)
    return mixed.reshape(1, sel_rows, q_width).astype(jnp.bfloat16)


def solution(mesh):
    placed = (
        P("req", "tp", None),
        P(),
        P(None, "tp"),
        P(None, "tp"),
        P(None, "tp"),
        P("req", None, "tp", None),
        P("req", None, "tp", None),
        P(),
        P(),
        P("req", None),
    )
    return jax.shard_map(
        on_device, mesh=mesh, in_specs=placed, out_specs=P("req", None, "tp"), check_vma=False
    )
```

profile of v0, /device:TPU:1, one launch (start us, length us, event | category | flops | bytes accessed | tf_op | source)
XLA Modules:
  0.0 291.5 jit_solution(17016376717909668846)
XLA Ops:
  6.5 0.7 all-gather.6.cloned.1.call-update
  7.3 0.7 all-gather.8.cloned.1.call-update
  8.1 0.7 all-gather.4.cloned.1.call-update
  8.7 0.7 reduce.4
  9.5 0.7 convert_element_type.97
  10.2 21.4 %copy.30 = bf16[1024,8192]{1,0:T(8,128)(2,1)} copy(bf16[1024,8192]{0,1:T(8,128)(2,1)} %bitcast.83) | data formatting | bytes 33554432 | tf_op jit(solution)/shard_map/dot_general | solution.py:43
  34.0 2.3 iota_compare_fusion
  36.4 17.5 %all-gather.6.cloned.1.call-done = bf16[1,384,8192]{2,1,0:T(8,128)(2,1)} async-done(((bf16[1,48,8192]{2,1,0:T(8,128)(2,1)}), bf16[1,384,8192]{2,1,0:T(8,128)(2,1)}) %all-gather.6.cloned.1.call-update) | async-done | bytes 6291472 | tf_op jit(solution)/shard_map/all_gather | solution.py:38
  53.8 4.3 %fusion.6 = f32[384]{0:T(512)S(1)} fusion(bf16[1,384,8192]{2,1,0:T(8,128)(2,1)} %all-gather.6.cloned.1.call-done), kind=kLoop, calls=%fused_computation.16 | loop fusion | flops 9436800 | bytes 6292992 | tf_op jit(solution)/shard_map/reduce_sum | solution.py:39
  58.1 14.0 %fusion.12 = f32[384,8,128]{0,2,1:T(8,128)S(1)} fusion(bf16[8,128,8192]{2,1,0:T(8,128)(2,1)} %bitcast.84, bf16[1,384,8192]{2,1,0:T(8,128)(2,1)} %all-gather.6.cloned.1.call-done, f32[8192]{0:T(1024)S(1)} %convert_element_type.97, f32[384]{0:T(512)S(1)} %add_rsqrt_fusion), kind=kOutput, calls=%fused_computation.22 | convolution fusion | flops 6455033856 | bytes 24675840 | tf_op jit(solution)/shard_map/dot_general | solution.py:43
  72.1 1.0 subtract_convert_fusion
  73.1 2.5 fusion.34
  75.7 2.5 fusion.31
  78.2 48.0 %all-gather.8.cloned.1.call-done = bf16[64,512,1,128]{3,1,2,0:T(8,128)(2,1)} async-done(((bf16[4,512,1,128]{3,1,2,0:T(8,128)(2,1)}), bf16[64,512,1,128]{3,1,2,0:T(8,128)(2,1)}) %all-gather.8.cloned.1.call-update) | async-done | bytes 8388624 | tf_op jit(solution)/shard_map/all_gather | solution.py:68
  126.1 4.2 %gather_fusion.2 = bf16[8,512,128]{2,1,0:T(8,128)(2,1)S(1)} fusion(bf16[64,512,128]{2,1,0:T(8,128)(2,1)} %bitcast.90, s32[1024]{0:T(1024)} %pad_clamp_fusion), kind=kCustom, calls=%fused_computation.2 | custom fusion | bytes 2097184 | tf_op jit(solution)/shard_map/gather | solution.py:71
  130.4 68.2 %all-gather.4.cloned.1.call-done = bf16[64,512,1,128]{3,1,2,0:T(8,128)(2,1)} async-done(((bf16[4,512,1,128]{3,1,2,0:T(8,128)(2,1)}), bf16[64,512,1,128]{3,1,2,0:T(8,128)(2,1)}) %all-gather.4.cloned.1.call-update) | async-done | bytes 8388624 | tf_op jit(solution)/shard_map/all_gather | solution.py:69
  198.6 5.2 %gather_fusion.1 = bf16[8,512,128]{2,1,0:T(8,128)(2,1)} fusion(bf16[64,512,128]{2,1,0:T(8,128)(2,1)} %bitcast.91, s32[1024]{0:T(1024)} %pad_clamp_fusion), kind=kCustom, calls=%fused_computation.1 | custom fusion | bytes 2097184 | tf_op jit(solution)/shard_map/gather | solution.py:72
  203.8 2.3 scatter_fusion.1
  206.2 4.2 %scatter_fusion = bf16[4096,128]{1,0:T(8,128)(2,1)} fusion(bf16[4096,128]{1,0:T(8,128)(2,1)} %bitcast.88, s32[384]{0:T(512)} %fusion.46, bf16[384,128]{1,0:T(8,128)(2,1)} %fusion.31), kind=kCustom, calls=%fused_computation.3 | custom fusion | bytes 296448 | tf_op jit(solution)/shard_map/scatter | solution.py:75
  210.4 10.2 %fusion.42 = (bf16[4096,64]{1,0:T(8,128)(2,1)S(1)}, bf16[4096,64]{1,0:T(8,128)(2,1)}) fusion(f32[4096,1,128]{2,0,1:T(8,128)S(1)} %bitcast_convert_fusion, f32[64]{0:T(128)} %copy-done.10, f32[4096]{0:T(1024)S(1)} %iota_convert_fusion), kind=kLoop, calls=%fused_computation.48 | loop fusion | flops 2359296 | bytes 3162368 | tf_op jit(solution)/shard_map/concatenate | solution.py:15
  220.5 21.4 %fusion.1 = (f32[8,384]{1,0:T(8,128)S(1)}, f32[4096,384,8]{1,0,2:T(8,128)}) fusion(pred[384,4096]{0,1:T(8,128)(4,1)} %iota_compare_fusion, bf16[384,8,64]{0,2,1:T(8,128)(2,1)} %get-tuple-element.8, bf16[384,8,64]{0,2,1:T(8,128)(2,1)S(1)} %get-tuple-element.7, bf16[4096,64]{1,0:T(8,128)(2,1)} %get-tuple-element.6, bf16[4096,64]{1,0:T(8,128)(2,1)S(1)} %get-tuple-element.5), kind=kOutput, calls=%fused_computation.9 | convolution fusion | flops 3262641152 | bytes 53751808 | tf_op jit(solution)/shard_map/sngd,cnd->ngsc/dot_general | solution.py:79
  241.9 21.1 %fusion = f32[8,384]{1,0:T(8,128)S(1)} fusion(f32[4096,384,8]{1,0,2:T(8,128)} %get-tuple-element.12, f32[8,384]{1,0:T(8,128)S(1)} %get-tuple-element.11, pred[384,4096]{0,1:T(8,128)(4,1)S(1)} %copy-done.3), kind=kLoop, calls=%fused_computation.8 | loop fusion | flops 50328576 | bytes 51929088 | tf_op jit(solution)/shard_map/reduce_sum | solution.py:85
  263.1 20.7 %fusion.28 = bf16[128,8,384]{2,0,1:T(8,128)(2,1)S(1)} fusion(f32[8,384]{1,0:T(8,128)S(1)} %fusion, f32[8,384]{1,0:T(8,128)S(1)} %get-tuple-element.11, f32[4096,384,8]{1,0,2:T(8,128)} %get-tuple-element.12, pred[384,4096]{0,1:T(8,128)(4,1)S(1)} %copy-done.4, bf16[4096,128]{1,0:T(8,128)(2,1)S(1)} %copy-done.5), kind=kOutput, calls=%fused_computation.38 | convolution fusion | flops 3284533248 | bytes 53764096 | tf_op jit(solution)/shard_map/ngsc,cnd->sngd/dot_general | solution.py:86
  283.8 1.2 copy.25
  (45 shorter events, 2.7 us)
Async XLA Ops:
  6.5 66.6 %copy-start = (bf16[8192,128]{1,0:T(8,128)(2,1)S(1)}, bf16[8192,128]{1,0:T(8,128)(2,1)}, u32[]{:S(2)}) copy-start(bf16[8192,128]{1,0:T(8,128)(2,1)} %param.13) | copy-start | bytes 6291460
  6.5 47.3 %all-gather.6.cloned.1.call-start = ((), (), s32[]{:S(2)}) async-start(), calls=%async_computation.1 | async-start | bytes 7077888 | tf_op jit(solution)/shard_map/all_gather | solution.py:38
  7.3 118.9 %all-gather.8.cloned.1.call-start = ((), (), s32[]{:S(2)}) async-start(), calls=%async_computation.2 | async-start | bytes 8912896 | tf_op jit(solution)/shard_map/all_gather | solution.py:68
  8.0 190.6 %all-gather.4.cloned.1.call-start = ((), (), s32[]{:S(2)}) async-start(), calls=%async_computation | async-start | bytes 8912896 | tf_op jit(solution)/shard_map/all_gather | solution.py:69
  10.2 21.4 %copy-start.9 = (s32[16,8]{0,1:T(8,128)S(1)}, s32[16,8]{0,1:T(8,128)}, u32[]{:S(2)}) copy-start(s32[16,8]{0,1:T(8,128)} %param.18) | copy-start | bytes 1540
  10.2 21.6 %copy-start.2 = (s32[64]{0:T(128)S(1)}, s32[64]{0:T(128)}, u32[]{:S(2)}) copy-start(s32[64]{0:T(128)} %param.17) | copy-start | bytes 772
  10.2 22.8 %copy-start.8 = (s32[1,384]{1,0:T(1,128)S(1)}, s32[1,384]{1,0:T(1,128)}, u32[]{:S(2)}) copy-start(s32[1,384]{1,0:T(1,128)} %param.19) | copy-start | bytes 4612
  32.4 39.7 %copy-start.10 = (f32[64]{0:T(128)}, f32[64]{0:T(128)S(1)}, u32[]{:S(2)}) copy-start(f32[64]{0:T(128)S(1)} %multiply_power_fusion) | copy-start | bytes 772
  53.8 19.3 %slice-start = ((s8[6291456]{0:T(1024)(128)(4,1)}), s8[4194304]{0:T(1024)(128)(4,1)S(1)}, s32[]{:S(2)}) async-start(s8[6291456]{0:T(1024)(128)(4,1)} %bitcast.86), calls=%async_computation.3 | async-start | bytes 8388608
  58.1 15.0 %slice-start.1 = ((s8[6291456]{0:T(1024)(128)(4,1)}), s8[2097152]{0:T(1024)(128)(4,1)S(1)}, s32[]{:S(2)}) async-start(s8[6291456]{0:T(1024)(128)(4,1)} %bitcast.86), calls=%async_computation.4 | async-start | bytes 4194304
  72.1 3.5 %copy-start.11 = (bf16[8192,128]{1,0:T(8,128)(2,1)S(1)}, bf16[8192,128]{1,0:T(8,128)(2,1)}, u32[]{:S(2)}) copy-start(bf16[8192,128]{1,0:T(8,128)(2,1)} %param.14) | copy-start | bytes 6291460
  75.7 128.1 %copy-start.6 = (bf16[384,128]{1,0:T(8,128)(2,1)S(1)}, bf16[384,128]{1,0:T(8,128)(2,1)}, u32[]{:S(2)}) copy-start(bf16[384,128]{1,0:T(8,128)(2,1)} %fusion.34) | copy-start | bytes 294916
  75.7 128.1 %copy-start.7 = (s32[384]{0:T(512)S(1)}, s32[384]{0:T(512)}, u32[]{:S(2)}) copy-start(s32[384]{0:T(512)} %fusion.46) | copy-start | bytes 4612
  220.5 21.4 %copy-start.3 = (pred[384,4096]{0,1:T(8,128)(4,1)S(1)}, pred[384,4096]{0,1:T(8,128)(4,1)}, u32[]{:S(2)}) copy-start(pred[384,4096]{0,1:T(8,128)(4,1)} %iota_compare_fusion) | copy-start | bytes 4718596
  241.9 21.1 %copy-start.4 = (pred[384,4096]{0,1:T(8,128)(4,1)S(1)}, pred[384,4096]{0,1:T(8,128)(4,1)}, u32[]{:S(2)}) copy-start(pred[384,4096]{0,1:T(8,128)(4,1)} %iota_compare_fusion) | copy-start | bytes 4718596
  241.9 21.2 %copy-start.5 = (bf16[4096,128]{1,0:T(8,128)(2,1)S(1)}, bf16[4096,128]{1,0:T(8,128)(2,1)}, u32[]{:S(2)}) copy-start(bf16[4096,128]{1,0:T(8,128)(2,1)} %scatter_fusion) | copy-start | bytes 3145732
  263.1 21.9 %copy-start.1 = (bf16[8192,128]{1,0:T(8,128)(2,1)S(1)}, bf16[8192,128]{1,0:T(8,128)(2,1)}, u32[]{:S(2)}) copy-start(bf16[8192,128]{1,0:T(8,128)(2,1)} %param.13) | copy-start | bytes 6291460
Sparse Core Ops, SparseCore 0:
  9.0 44.7 all-gather.5
  56.0 70.0 all-gather.7
  128.3 70.3 all-gather.3
where the time goes:
time: 293 us; the launch traced here: 292 us
  waiting for transfers between devices  136 us (46%)
  matrix products  61.1 us (21%)
  other arithmetic  42.1 us (14%)
  local copies, waits for them, and re-layouts  39.2 us (13%)
  between operations  13.3 us (5%)
    all_gather x1, waiting for transfers between devices, on_device(): lax.all_gather(store_values, 'req', axis=0, tiled=True)  68.2 us
    all_gather x1, waiting for transfers between devices, on_device(): lax.all_gather(store_keys, 'req', axis=0, tiled=True)  48 us
    dot_general x1, matrix products, on_device(): jnp.einsum('sngd,cnd->ngsc', grouped, rot_keys, preferred_element_type=jn...  21.4 us
    dot_general x1, local copies, waits for them, and re-layouts, on_device(): jnp.dot(normed, w_query, preferred_element_type=jnp.float32)  21.4 us
    reduce_sum x1, other arithmetic, on_device(): jnp.sum(expos, axis=-1, keepdims=True)  21.1 us
    dot_general x1, matrix products, on_device(): jnp.einsum('ngsc,cnd->sngd', weights, ctx_values, preferred_element_type=...  20.7 us
    all_gather x1, waiting for transfers between devices, on_device(): lax.all_gather(tokens, 'tp', axis=1, tiled=True)[0].astype(jnp.float32)  17.5 us
    dot_general x1, matrix products, on_device(): jnp.dot(normed, w_query, preferred_element_type=jnp.float32)  14 us
  transfers between devices with their start and end apart: 3, of which 3 were waited for; matrix products, arithmetic and copies ran while one was open for 19% of the time, Pallas kernels for 0%

commit v1 on v0

v1 whole, which is shorter than its diff:
```python
import functools

import jax
import jax.numpy as jnp
from jax import lax
from jax.experimental import pallas as pl
from jax.experimental.pallas import tpu as pltpu
from jax.sharding import PartitionSpec as P

BF16 = jnp.bfloat16
F32 = jnp.float32
SIDE = 4
ROWS = 64
THETA = 500000.0
EPS = 1e-05
HIDDEN_POS = 1 << 30
MIB = 1 << 20


def move(value, step):
    pairs = []
    for y in range(SIDE):
        for x in range(SIDE):
            for z in range(SIDE):
                for core in range(2):
                    ty, tx, tz, tc = step(y, x, z, core)
                    source = ((y * SIDE + x) * SIDE + z) * 2 + core
                    target = (((ty % SIDE) * SIDE + tx % SIDE) * SIDE + tz % SIDE) * 2 + tc
                    pairs.append((source, target))
    return lax.ppermute(value, ("req", "tp"), pairs)


def way(core):
    return 1 if core == 0 else -1


def along_x(value, sign):
    return move(value, lambda y, x, z, c: (y, x + sign * way(c), z, c))


def along_y(value, sign):
    return move(value, lambda y, x, z, c: (y + sign * way(c), x, z, c))


def along_z(value):
    return move(value, lambda y, x, z, c: (y, x, z + way(c), c))


def other_core(value):
    return move(value, lambda y, x, z, c: (y, x, z, 1 - c))


def norm_kernel(tokens_ref, gain_ref, out_ref):
    hidden = tokens_ref[...].astype(F32)
    scale = lax.rsqrt(jnp.mean(hidden * hidden, axis=-1, keepdims=True) + EPS)
    out_ref[...] = (hidden * scale * gain_ref[...].astype(F32)).astype(BF16)


def normalise(tokens, gain):
    return pl.pallas_call(
        norm_kernel,
        out_shape=jax.ShapeDtypeStruct(tokens.shape, BF16),
        compiler_params=pltpu.CompilerParams(vmem_limit_bytes=24 * MIB),
        name="norm",
    )(tokens, gain.reshape(1, -1))


def pick_kernel(index_ref, *refs):
    sources, (k_fwd, k_back, v_fwd, v_back), sems = refs[:8], refs[8:12], refs[12]
    copies = []
    for tensor, (fwd, back) in enumerate(((k_fwd, k_back), (v_fwd, v_back))):
        for target in range(3):
            for slot in range(4):
                dest = fwd.at[target * 4 + slot] if target < 2 else back.at[slot]
                n = tensor * 12 + target * 4 + slot
                copies.append(
                    pltpu.make_async_copy(
                        sources[tensor * 4 + slot].at[index_ref[n]], dest, sems.at[n]
                    )
                )
    for copy in copies:
        copy.start()
    for copy in copies:
        copy.wait()


def pick(index, keys, values):
    _, tokens, dim = keys[0].shape
    any_spec = pl.BlockSpec(memory_space=pl.ANY)
    shapes = [jax.ShapeDtypeStruct((n, tokens, dim), BF16) for n in (8, 4, 8, 4)]
    return pl.pallas_call(
        pick_kernel,
        out_shape=shapes,
        in_specs=[pl.BlockSpec(memory_space=pltpu.SMEM)] + [any_spec] * 8,
        out_specs=[any_spec] * 4,
        scratch_shapes=[pltpu.SemaphoreType.DMA((24,))],
        compiler_params=pltpu.CompilerParams(vmem_limit_bytes=2 * MIB),
        cost_estimate=pl.CostEstimate(flops=0, bytes_accessed=6 * MIB, transcendentals=0),
        name="pick",
    )(index, *keys, *values)


def rope(values, cosine, sine):
    return values * cosine + pltpu.roll(values, 64, 1) * sine


def project_kernel(
    place_ref, p0, p1, p2, p3, p4, p5, p6, p7, wq_ref, wk_hbm, wv_hbm, cos_ref, sin_ref,
    q_ref, nk_ref, nv_ref, x_buf, wk_buf, wv_buf, x_sems, w_sems,
):
    step = pl.program_id(0)
    pieces = (p0, p1, p2, p3, p4, p5, p6, p7)
    rows = p0.shape[0]

    def piece_copy(n):
        at = pl.multiple_of(place_ref[n] * rows, 16)
        return pltpu.make_async_copy(pieces[n], x_buf.at[pl.ds(at, rows)], x_sems.at[n])

    k_copy = pltpu.make_async_copy(wk_hbm, wk_buf, w_sems.at[0])
    v_copy = pltpu.make_async_copy(wv_hbm, wv_buf, w_sems.at[1])

    @pl.when(step == 0)
    def _():
        for n in range(8):
            piece_copy(n).start()
        k_copy.start()
        v_copy.start()
        for n in range(8):
            piece_copy(n).wait()

    cosine = cos_ref[...]
    sine = sin_ref[...]

    @pl.when(step < 4)
    def _():
        raw = jnp.dot(x_buf[...], wq_ref[...], preferred_element_type=F32)
        for h in range(2):
            q_ref[h] = rope(raw[:, h * 128 : (h + 1) * 128], cosine, sine).astype(BF16)

    @pl.when(step == 4)
    def _():
        k_copy.wait()
        v_copy.wait()
        new_k = jnp.dot(x_buf[...], wk_buf[...], preferred_element_type=F32).astype(BF16)
        nk_ref[...] = rope(new_k.astype(F32), cosine, sine).astype(BF16)
        nv_ref[...] = jnp.dot(x_buf[...], wv_buf[...], preferred_element_type=F32).astype(BF16)


def project(place, pieces, w_query, w_key, w_value, cosine, sine):
    rows, width = pieces[0].shape
    sel = 8 * rows
    any_spec = pl.BlockSpec(memory_space=pl.ANY)
    whole = pl.BlockSpec((sel, 128), lambda i: (0, 0))
    last = lambda i: jnp.minimum(i, 3)
    return pl.pallas_call(
        project_kernel,
        grid=(5,),
        out_shape=[
            jax.ShapeDtypeStruct((8, sel, 128), BF16),
            jax.ShapeDtypeStruct((sel, 128), BF16),
            jax.ShapeDtypeStruct((sel, 128), BF16),
        ],
        in_specs=[pl.BlockSpec(memory_space=pltpu.SMEM)]
        + [any_spec] * 8
        + [pl.BlockSpec((width, 256), lambda i: (0, last(i))), any_spec, any_spec, whole, whole],
        out_specs=[pl.BlockSpec((2, sel, 128), lambda i: (last(i), 0, 0)), whole, whole],
        scratch_shapes=[
            pltpu.VMEM((sel, width), BF16),
            pltpu.VMEM((width, 128), BF16),
            pltpu.VMEM((width, 128), BF16),
            pltpu.SemaphoreType.DMA((8,)),
            pltpu.SemaphoreType.DMA((2,)),
        ],
        compiler_params=pltpu.CompilerParams(vmem_limit_bytes=40 * MIB),
        cost_estimate=pl.CostEstimate(
            flops=2 * sel * width * 1280, bytes_accessed=30 * MIB, transcendentals=0
        ),
        name="project",
    )(place, *pieces, w_query, w_key, w_value, cosine, sine)


def attend_kernel(
    where_ref, count_ref, q_ref, nk_ref, nv_ref, qpos_ref, kpos_ref, npos_ref, cos_ref, sin_ref, *refs
):
    keys, values, out_ref = refs[:7], refs[7:14], refs[14]
    k_buf, v_buf, nv_buf, s_buf, m_buf, acc, sems = refs[15:]
    block = k_buf.shape[1]
    blocks = k_buf.shape[0]
    heads, sel, dim = q_ref.shape
    ctx = block * blocks
    tall = heads * ROWS
    factor = 1.4426950408889634 / (dim ** 0.5)

    def k_dest(j):
        return k_buf.at[j]

    def v_dest(j):
        return v_buf.at[pl.ds(j * block, block), pl.ds(0, dim)]

    for j in range(blocks):
        for n in range(7):

            @pl.when(where_ref[0, j] == n)
            def _():
                pltpu.make_async_copy(keys[n].at[where_ref[1, j]], k_dest(j), sems.at[0, j]).start()

            @pl.when(where_ref[2, j] == n)
            def _():
                pltpu.make_async_copy(values[n].at[where_ref[3, j]], v_dest(j), sems.at[1, j]).start()

    v_buf[:, dim:] = jnp.ones((ctx, dim), BF16)
    nv_buf[:, dim:] = jnp.ones((sel, dim), BF16)
    nv_buf[:, :dim] = nv_ref[...]

    for j in range(blocks):
        pltpu.make_async_copy(keys[0].at[0], k_dest(j), sems.at[0, j]).wait()
        at = pl.ds(j * block, block)
        k_buf[j] = rope(k_buf[j].astype(F32), cos_ref[at, :], sin_ref[at, :]).astype(BF16)
    for j in range(blocks):
        pltpu.make_async_copy(values[0].at[0], v_dest(j), sems.at[1, j]).wait()

    def masked_scores(queries, key_block, key_pos, query_pos):
        width = key_block.shape[0]
        scores = lax.dot_general(
            queries, key_block, (((1,), (1,)), ((), ())), preferred_element_type=F32
        )
        reps = width // 128
        seen = key_pos <= jnp.concatenate([query_pos] * reps, axis=1)
        scores = jnp.where(seen[None], scores.reshape(heads, ROWS, width), -jnp.inf)
        scores = scores.reshape(tall, width)
        most = scores[:, :128]
        for n in range(1, reps):
            most = jnp.maximum(most, scores[:, n * 128 : (n + 1) * 128])
        return scores, most

    def tile(i, carry):
        rows = pl.ds(pl.multiple_of(i * ROWS, ROWS), ROWS)
        queries = q_ref[:, rows, :].reshape(tall, dim)
        query_pos = qpos_ref[rows, :]
        scores, most = masked_scores(queries, nk_ref[...], npos_ref[...], query_pos)
        s_buf[:, ctx:] = scores
        m_buf[...] = most
        count = count_ref[i]

        def first(j, carry):
            scores, most = masked_scores(
                q_ref[:, rows, :].reshape(tall, dim), k_buf[j], kpos_ref[pl.ds(j, 1), :], qpos_ref[rows, :]
            )
            s_buf[:, pl.ds(pl.multiple_of(j * block, block), block)] = scores
            m_buf[...] = jnp.maximum(m_buf[...], most)
            return carry

        lax.fori_loop(0, count, first, 0)
        m_buf[...] = jnp.broadcast_to(jnp.max(m_buf[...], axis=1, keepdims=True), (tall, 128))

        def expos(scores):
            most = jnp.concatenate([m_buf[...]] * (scores.shape[1] // 128), axis=1)
            return jnp.exp2((scores - most) * factor).astype(BF16)

        acc[...] = jnp.dot(expos(s_buf[:, ctx:]), nv_buf[...], preferred_element_type=F32)

        def second(j, carry):
            at = pl.ds(pl.multiple_of(j * block, block), block)
            acc[...] += jnp.dot(expos(s_buf[:, at]), v_buf[at, :], preferred_element_type=F32)
            return carry

        lax.fori_loop(0, count, second, 0)
        result = (acc[:, :dim] / acc[:, dim:]).astype(BF16)
        for h in range(heads):
            out_ref[rows, h * dim : (h + 1) * dim] = result[h * ROWS : (h + 1) * ROWS]
        return carry

    lax.fori_loop(0, sel // ROWS, tile, 0)


def attend(where, count, queries, new_k, new_v, qpos, kpos, npos, cosine, sine, keys, values):
    heads, sel, dim = queries.shape
    _, block, _ = keys[0].shape
    blocks = kpos.shape[0]
    ctx = block * blocks
    smem = pl.BlockSpec(memory_space=pltpu.SMEM)
    vmem = pl.BlockSpec(memory_space=pltpu.VMEM)
    any_spec = pl.BlockSpec(memory_space=pl.ANY)
    tall = heads * ROWS
    return pl.pallas_call(
        attend_kernel,
        out_shape=jax.ShapeDtypeStruct((sel, heads * dim), BF16),
        in_specs=[smem] * 2 + [vmem] * 8 + [any_spec] * 14,
        out_specs=vmem,
        scratch_shapes=[
            pltpu.VMEM((blocks, block, dim), BF16),
            pltpu.VMEM((ctx, 2 * dim), BF16),
            pltpu.VMEM((sel, 2 * dim), BF16),
            pltpu.VMEM((tall, ctx + sel), F32),
            pltpu.VMEM((tall, 128), F32),
            pltpu.VMEM((tall, 2 * dim), F32),
            pltpu.SemaphoreType.DMA((2, blocks)),
        ],
        compiler_params=pltpu.CompilerParams(vmem_limit_bytes=40 * MIB),
        cost_estimate=pl.CostEstimate(
            flops=4 * heads * sel * ctx * dim, bytes_accessed=8 * MIB, transcendentals=heads * sel * ctx
        ),
        name="attend",
    )(where, count, queries, new_k, new_v, qpos, kpos, npos, cosine, sine, *keys, *values)


def tables(positions):
    frequency = THETA ** (-(2.0 / 128) * jnp.arange(64).astype(F32))
    angles = positions.astype(F32)[:, None] * frequency[None, :]
    cosine, sine = jnp.cos(angles), jnp.sin(angles)
    return jnp.concatenate([cosine, cosine], axis=1), jnp.concatenate([-sine, sine], axis=1)


def order_of(offset, sign):
    return jnp.where(
        offset == 0, 0, jnp.where(offset == 2, 3, jnp.where(offset == (-sign) % SIDE, 1, 2))
    )


def on_device(
    tokens, norm_gain, w_query, w_key, w_value, store_keys, store_values, block_slot, retrieval, sel_index
):
    held, block, _, dim = store_keys.shape
    requests, chosen_count = retrieval.shape
    stores = block_slot.shape[0] // held
    req, tp = lax.axis_index("req"), lax.axis_index("tp")
    y, x = req // SIDE, req % SIDE
    z, core = tp // 2, tp % 2
    sign = 1 - 2 * core

    own_k = store_keys.reshape(held, block, dim)
    own_v = store_values.reshape(held, block, dim)
    k_one, k_two = along_x(own_k, 1), along_x(own_k, -1)
    v_one, v_two = along_y(own_v, 1), along_y(own_v, -1)
    normed = normalise(tokens[0], norm_gain)
    z_one = along_z(normed)
    k_far, v_far = along_x(k_one, 1), along_y(v_one, 1)
    z_two = along_z(z_one)
    z_far = along_z(z_two)
    mine = [normed, z_one, z_two, z_far]
    theirs = [other_core(piece) for piece in mine]
    row_k = [own_k, k_one, k_two, k_far]
    column_v = [own_v, v_one, v_two, v_far]

    hot = retrieval[:, :, None] == jnp.arange(block_slot.shape[0])[None, None, :]
    slots = jnp.sum(jnp.where(hot, block_slot[None, None, :], 0), axis=2)
    at_store = (slots // held)[:, :, None] == jnp.arange(stores)[None, None, :]
    wanted = jnp.sum(jnp.where(at_store, (slots % held)[:, :, None], 0), axis=1).reshape(-1)
    arrivals = [0, -sign, sign, 2]
    targets = [sign, 2, -sign]

    def node(yy, xx):
        return ((yy + SIDE) % SIDE) * SIDE + (xx + SIDE) % SIDE

    picks = [node(y + t, x) * stores + node(y, x + a) for t in targets for a in arrivals]
    picks += [node(y, x + t) * stores + node(y + a, x) for t in targets for a in arrivals]
    pick_at = jnp.stack(picks)
    entries = pick_at[:, None] == jnp.arange(requests * stores)[None, :]
    index = jnp.sum(jnp.where(entries, wanted[None, :], 0), axis=1).astype(jnp.int32)

    k_fwd, k_back, v_fwd, v_back = pick(index, row_k, column_v)
    k_fwd, k_back = along_y(k_fwd, 1), along_y(k_back, -1)
    v_fwd, v_back = along_x(v_fwd, 1), along_x(v_back, -1)
    k_last, v_last = along_y(k_fwd[4:], 1), along_x(v_fwd[4:], 1)
    keys = row_k + [k_fwd, k_back, k_last]
    values = column_v + [v_fwd, v_back, v_last]

    own_slots = jnp.sum(jnp.where((jnp.arange(requests) == req)[:, None], slots, 0), axis=0)
    store, local = own_slots // held, own_slots % held
    order_y = order_of((store // SIDE - y) % SIDE, sign)
    order_x = order_of((store % SIDE - x) % SIDE, sign)
    where = jnp.stack(
        [
            jnp.where(order_y == 0, order_x, 3 + order_y),
            jnp.where(order_y == 0, local, order_x),
            jnp.where(order_x == 0, order_y, 3 + order_x),
            jnp.where(order_x == 0, local, order_y),
        ]
    ).astype(jnp.int32)

    positions = sel_index[0]
    sel = positions.shape[0]
    ctx = chosen_count * block
    everywhere = jnp.arange(ctx, dtype=jnp.int32)
    replaced = jnp.any(positions[:, None] == everywhere[None, :], axis=0)
    kpos = jnp.where(replaced, HIDDEN_POS, everywhere).reshape(chosen_count, block)
    qpos = jnp.broadcast_to(positions[:, None], (sel, 128))
    count = positions[ROWS - 1 :: ROWS] // block + 1
    q_cos, q_sin = tables(positions)
    k_cos, k_sin = tables(everywhere)

    place = jnp.stack(
        [((z + s * sign + SIDE) % SIDE) * 2 + core for s in (0, -1, 2, 1)]
        + [((z + s * sign + SIDE) % SIDE) * 2 + 1 - core for s in (0, 1, 2, -1)]
    ).astype(jnp.int32)
    queries, new_k, new_v = project(place, mine + theirs, w_query, w_key, w_value, q_cos, q_sin)
    mixed = attend(
        where, count, queries, new_k, new_v, qpos, kpos, positions[None], k_cos, k_sin, keys, values
    )
    return mixed[None]


def solution(mesh):
    placed = (
        P("req", "tp", None),
        P(),
        P(None, "tp"),
        P(None, "tp"),
        P(None, "tp"),
        P("req", None, "tp", None),
        P("req", None, "tp", None),
        P(),
        P(),
        P("req", None),
    )
    return jax.shard_map(
        on_device, mesh=mesh, in_specs=placed, out_specs=P("req", None, "tp"), check_vma=False
    )
```

time: 293 us -> 121 us (0.41)
  waiting for transfers between devices: 136 us -> 14.3 us
  matrix products: 61.1 us -> 0 us
  Pallas kernels: 0 us -> 53.9 us
  local copies, waits for them, and re-layouts: 39.2 us -> 7.31 us
  starting transfers between devices: 0.08 us -> 26 us
  other arithmetic: 42.1 us -> 18.1 us
  between operations: 13.3 us -> 0.63 us
    all_gather x3 -> x0, waiting for transfers between devices: 134 us -> none  [the longest x1 68.2 us: on_device(): lax.all_gather(store_values, 'req', axis=0, tiled=True)]
    dot_general x5 -> x0, matrix products: 61.1 us -> none  [the longest x1 21.4 us: on_device(): jnp.einsum('sngd,cnd->ngsc', grouped, rot_keys, preferred_element_type=jn...]
    pallas_call x0 -> x4, Pallas kernels: none -> 53.9 us  [the longest x1 26.7 us: attend(): pl.pallas_call(attend_kernel, out_shape=jax.ShapeDtypeStruct((sel, heads...]
    ppermute x0 -> x19, starting transfers between devices: none -> 26 us  [move(): return lax.ppermute(value, ('req', 'tp'), pairs)]
    reduce_sum x2 -> x3, other arithmetic: 25.4 us -> 0.7 us  [the longest x1 0.41 us: on_device(): slots = jnp.sum(jnp.where(hot, block_slot[None, None, :], 0), axis=2)]
    dot_general x1 -> x0, local copies, waits for them, and re-layouts: 21.4 us -> none  [on_device(): jnp.dot(normed, w_query, preferred_element_type=jnp.float32)]
    ppermute x0 -> x19, waiting for transfers between devices: none -> 14.3 us  [move(): return lax.ppermute(value, ('req', 'tp'), pairs)]
    neg x0 -> x2, other arithmetic: none -> 10.6 us  [tables(): -sine]
  transfers between devices with their start and end apart: 3 -> 19, of which waited for: 3 -> 3; matrix products, arithmetic and copies ran while one was open for 19% -> 18% of each run, Pallas kernels for 0% -> 23%
where the time goes in v1:
time: 121 us; the launch traced here: 120 us
  Pallas kernels  53.9 us (45%)
  starting transfers between devices  26 us (21%)
  other arithmetic  18.1 us (15%)
  waiting for transfers between devices  14.3 us (12%)
  local copies, waits for them, and re-layouts  7.31 us (6%)
    pallas_call x1, Pallas kernels, attend(): pl.pallas_call(attend_kernel, out_shape=jax.ShapeDtypeStruct((sel, heads...  26.7 us
    ppermute x19, starting transfers between devices, move(): return lax.ppermute(value, ('req', 'tp'), pairs)  26 us
    pallas_call x1, Pallas kernels, project(): pl.pallas_call(project_kernel, grid=(5,), out_shape=[jax.ShapeDtypeStruct...  16.8 us
    ppermute x19, waiting for transfers between devices, move(): return lax.ppermute(value, ('req', 'tp'), pairs)  14.3 us
    neg x2, other arithmetic, tables(): -sine  10.6 us
    pallas_call x1, Pallas kernels, pick(): pl.pallas_call(pick_kernel, out_shape=shapes, in_specs=[pl.BlockSpec(memo...  9.84 us
    concatenate x2, other arithmetic, tables(): jnp.concatenate([cosine, cosine], axis=1)  5.68 us
    unnamed x31, local copies, waits for them, and re-layouts  3.85 us
  transfers between devices with their start and end apart: 19, of which 3 were waited for; matrix products, arithmetic and copies ran while one was open for 18% of the time, Pallas kernels for 23%

profile of v1, /device:TPU:1, one launch (start us, length us, event | category | flops | bytes accessed | tf_op | source)
XLA Modules:
  0.0 120.2 jit_solution(11599968784283820121)
XLA Ops:
  0.0 3.3 %collective-permute-start.7 = (bf16[4,512,128]{2,1,0:T(8,128)(2,1)}, bf16[4,512,128]{2,1,0:T(8,128)(2,1)S(1)}, u32[]{:S(2)}, u32[]{:S(2)}) collective-permute-start(bf16[4,512,128]{2,1,0:T(8,128)(2,1)} %bitcast.66), channel_id=1, source_target_pairs={{0,8},{1,25},{2,10},{3,27},{4,12},{5,29},{6,14},{7,31},{8,16},{9,1... | collective-permute-start | bytes 1572872 | tf_op jit(solution)/shard_map/ppermute | solution.py:30
  3.3 2.7 %collective-permute-start.10 = (bf16[4,512,128]{2,1,0:T(8,128)(2,1)}, bf16[4,512,128]{2,1,0:T(8,128)(2,1)S(1)}, u32[]{:S(2)}, u32[]{:S(2)}) collective-permute-start(bf16[4,512,128]{2,1,0:T(8,128)(2,1)} %bitcast.70), channel_id=1, source_target_pairs={{0,32},{1,97},{2,34},{3,99},{4,36},{5,101},{6,38},{7,103},{8,40},{... | collective-permute-start | bytes 1572872 | tf_op jit(solution)/shard_map/ppermute | solution.py:30
  6.8 1.1 copy-done
  8.4 3.8 %collective-permute-start = (bf16[48,8192]{1,0:T(8,128)(2,1)S(1)}, bf16[48,8192]{1,0:T(8,128)(2,1)}, u32[]{:S(2)}, u32[]{:S(2)}) collective-permute-start(bf16[48,8192]{1,0:T(8,128)(2,1)S(1)} %norm.1.p0), channel_id=1, source_target_pairs={{0,2},{1,7},{2,4},{3,1},{4,6},{5,3},{6,0},{7,5},{8,10},{9,15},{10,... | collective-permute-start | bytes 2359304 | tf_op jit(solution)/shard_map/ppermute | solution.py:30
  12.3 9.8 %fusion.1 = (f32[4096,64]{1,0:T(8,128)}, f32[4096,64]{1,0:T(8,128)}, f32[4096,64]{1,0:T(8,128)}) fusion(f32[64]{0:T(128)S(1)} %multiply_power_fusion, f32[4096]{0:T(1024)S(1)} %iota_convert_fusion), kind=kLoop, calls=%fused_computation.6 | loop fusion | flops 524288 | bytes 3162368 | tf_op jit(solution)/shard_map/neg | solution.py:311
  22.6 2.7 %collective-permute-start.9 = (bf16[4,512,128]{2,1,0:T(8,128)(2,1)S(1)}, bf16[4,512,128]{2,1,0:T(8,128)(2,1)}, u32[]{:S(2)}, u32[]{:S(2)}) collective-permute-start(bf16[4,512,128]{2,1,0:T(8,128)(2,1)S(1)} %collective-permute-done.7.refs_1_), channel_id=1, source_target_pairs={{0,8},{1,25},{2,10},{3,27},{4,12},{5,29},{6,14},{7,31},{8,16},{9,1... | collective-permute-start | bytes 1572872 | tf_op jit(solution)/shard_map/ppermute | solution.py:30
  25.4 2.7 %collective-permute-start.12 = (bf16[4,512,128]{2,1,0:T(8,128)(2,1)S(1)}, bf16[4,512,128]{2,1,0:T(8,128)(2,1)}, u32[]{:S(2)}, u32[]{:S(2)}) collective-permute-start(bf16[4,512,128]{2,1,0:T(8,128)(2,1)S(1)} %collective-permute-done.10.refs_5_.refs_8_), channel_id=1, source_target_pairs={{0,32},{1,97},{2,34},{3,99},{4,36},{5,101},{6,38},{7,103},{8,40},{... | collective-permute-start | bytes 1572872 | tf_op jit(solution)/shard_map/ppermute | solution.py:30
  28.9 2.6 %collective-permute-done.9.refs_3_ = bf16[4,512,128]{2,1,0:T(8,128)(2,1)} collective-permute-done((bf16[4,512,128]{2,1,0:T(8,128)(2,1)S(1)}, bf16[4,512,128]{2,1,0:T(8,128)(2,1)}, u32[]{:S(2)}, u32[]{:S(2)}) %collective-permute-start.9) | collective-permute-done | bytes 524320 | tf_op jit(solution)/shard_map/ppermute | solution.py:30
  31.5 2.7 %collective-permute-done.12.refs_7_.refs_10_ = bf16[4,512,128]{2,1,0:T(8,128)(2,1)} collective-permute-done((bf16[4,512,128]{2,1,0:T(8,128)(2,1)S(1)}, bf16[4,512,128]{2,1,0:T(8,128)(2,1)}, u32[]{:S(2)}, u32[]{:S(2)}) %collective-permute-start.12) | collective-permute-done | bytes 524320 | tf_op jit(solution)/shard_map/ppermute | solution.py:30
  34.2 9.8 %pick.1 = (bf16[8,512,128]{2,1,0:T(8,128)(2,1)}, bf16[4,512,128]{2,1,0:T(8,128)(2,1)S(1)}, bf16[8,512,128]{2,1,0:T(8,128)(2,1)S(1)}, bf16[4,512,128]{2,1,0:T(8,128)(2,1)S(1)}) custom-call(s32[24]{0:T(128)S(1)} %select_reduce_fusion.2.index_ref, bf16[4,512,128]{2,1,0:T(8,128)(2,1)S(1)} %bitcast.68, bf16[4,512,128]{2,1,0:T(8,128)(2,1)S(1)} %collective-permute-done.7.refs_1_, ...), custom_call_target="tpu_custom_call" | custom-call | bytes 6291456 | tf_op jit(solution)/shard_map/pick/pallas_call | solution.py:91
  44.0 1.0 copy-done.8
  45.0 0.8 copy-done.9
  46.6 3.5 %collective-permute-start.13 = (bf16[8,512,128]{2,1,0:T(8,128)(2,1)}, bf16[8,512,128]{2,1,0:T(8,128)(2,1)}, u32[]{:S(2)}, u32[]{:S(2)}) collective-permute-start(bf16[8,512,128]{2,1,0:T(8,128)(2,1)} %get-tuple-element.15), channel_id=1, source_target_pairs={{0,32},{1,97},{2,34},{3,99},{4,36},{5,101},{6,38},{7,103},{8,40},{... | collective-permute-start | bytes 3145736 | tf_op jit(solution)/shard_map/ppermute | solution.py:30
  51.4 0.9 fusion
  52.3 0.9 pad_maximum_fusion.2
  53.2 9.0 %collective-permute-done.13.refs_4_ = bf16[8,512,128]{2,1,0:T(8,128)(2,1)} collective-permute-done((bf16[8,512,128]{2,1,0:T(8,128)(2,1)}, bf16[8,512,128]{2,1,0:T(8,128)(2,1)}, u32[]{:S(2)}, u32[]{:S(2)}) %collective-permute-start.13) | collective-permute-done | bytes 1048608 | tf_op jit(solution)/shard_map/ppermute | solution.py:30
  63.0 4.8 %pad_maximum_fusion = (f32[4096,128]{1,0:T(8,128)S(1)}, f32[4096,128]{1,0:T(8,128)S(1)}) fusion(f32[4096,64]{1,0:T(8,128)} %get-tuple-element.24, f32[4096,64]{1,0:T(8,128)} %get-tuple-element.23, f32[4096,64]{1,0:T(8,128)} %get-tuple-element.22), kind=kLoop, calls=%fused_computation.4 | loop fusion | flops 1048576 | bytes 7340032 | tf_op jit(solution)/shard_map/concatenate | solution.py:311
  67.8 1.2 slice.12
  69.0 1.1 slice.13
  70.2 0.9 collective-permute-start.17
  71.1 2.7 %collective-permute-start.15 = (bf16[4,512,128]{2,1,0:T(8,128)(2,1)S(1)}, bf16[4,512,128]{2,1,0:T(8,128)(2,1)S(1)}, u32[]{:S(2)}, u32[]{:S(2)}) collective-permute-start(bf16[4,512,128]{2,1,0:T(8,128)(2,1)S(1)} %slice.12), channel_id=1, source_target_pairs={{0,32},{1,97},{2,34},{3,99},{4,36},{5,101},{6,38},{7,103},{8,40},{... | collective-permute-start | bytes 1572872 | tf_op jit(solution)/shard_map/ppermute | solution.py:30
  73.7 2.6 %collective-permute-start.18 = (bf16[4,512,128]{2,1,0:T(8,128)(2,1)S(1)}, bf16[4,512,128]{2,1,0:T(8,128)(2,1)S(1)}, u32[]{:S(2)}, u32[]{:S(2)}) collective-permute-start(bf16[4,512,128]{2,1,0:T(8,128)(2,1)S(1)} %slice.13), channel_id=1, source_target_pairs={{0,8},{1,25},{2,10},{3,27},{4,12},{5,29},{6,14},{7,31},{8,16},{9,1... | collective-permute-start | bytes 1572872 | tf_op jit(solution)/shard_map/ppermute | solution.py:30
  76.3 16.8 %project.1 = (bf16[8,384,128]{2,1,0:T(8,128)(2,1)S(1)}, bf16[384,128]{1,0:T(8,128)(2,1)S(1)}, bf16[384,128]{1,0:T(8,128)(2,1)S(1)}) custom-call(s32[8]{0:T(128)S(1)} %stack.118.place_ref, bf16[48,8192]{1,0:T(8,128)(2,1)S(1)} %norm.1.p0, bf16[48,8192]{1,0:T(8,128)(2,1)} %collective-permute-done.p1, bf16[48,8192]{1,0:T(8,128)(2,1)} %collective-permute-done.1.p2, ...), custom_call_target="tpu_custom_call" | custom-call | flops 8053063680 | bytes 31457280 | tf_op jit(solution)/shard_map/project/pallas_call | solution.py:155
  93.3 26.7 %attend.1 = bf16[384,1024]{1,0:T(8,128)(2,1)} custom-call(s32[4,8]{1,0:T(4,128)S(1)} %pad_add_fusion.where_ref, s32[6]{0:T(128)S(1)} %fusion.8.count_ref, bf16[8,384,128]{2,1,0:T(8,128)(2,1)S(1)} %get-tuple-element.12.q_ref, bf16[384,128]{1,0:T(8,128)(2,1)S(1)} %get-tuple-element.13.nk_ref, bf16[384,128]{1,0:T(8,128)(2,1)S(1)} %get-tuple-element.14.nv_ref, ...), custom_call_target="tpu_custom_call" | custom-call | flops 6442450944 | bytes 8388608 | tf_op jit(solution)/shard_map/attend/pallas_call | solution.py:285
  (77 shorter events, 5.4 us)
Async XLA Ops:
  0.0 22.6 %collective-permute-start.7 = (bf16[4,512,128]{2,1,0:T(8,128)(2,1)}, bf16[4,512,128]{2,1,0:T(8,128)(2,1)S(1)}, u32[]{:S(2)}, u32[]{:S(2)}) collective-permute-start(bf16[4,512,128]{2,1,0:T(8,128)(2,1)} %bitcast.66), channel_id=1, source_target_pairs={{0,8},{1,25},{2,10},{3,27},{4,12},{5,29},{6,14},{7,31},{8,16},{9,1... | collective-permute-start | bytes 1572872 | tf_op jit(solution)/shard_map/ppermute | solution.py:30
  3.3 25.5 %collective-permute-start.8 = (bf16[4,512,128]{2,1,0:T(8,128)(2,1)}, bf16[4,512,128]{2,1,0:T(8,128)(2,1)S(1)}, u32[]{:S(2)}, u32[]{:S(2)}) collective-permute-start(bf16[4,512,128]{2,1,0:T(8,128)(2,1)} %bitcast.67), channel_id=1, source_target_pairs={{0,24},{1,9},{2,26},{3,11},{4,28},{5,13},{6,30},{7,15},{8,0},{9,17... | collective-permute-start | bytes 1572872 | tf_op jit(solution)/shard_map/ppermute | solution.py:30
  3.3 22.1 %collective-permute-start.10 = (bf16[4,512,128]{2,1,0:T(8,128)(2,1)}, bf16[4,512,128]{2,1,0:T(8,128)(2,1)S(1)}, u32[]{:S(2)}, u32[]{:S(2)}) collective-permute-start(bf16[4,512,128]{2,1,0:T(8,128)(2,1)} %bitcast.70), channel_id=1, source_target_pairs={{0,32},{1,97},{2,34},{3,99},{4,36},{5,101},{6,38},{7,103},{8,40},{... | collective-permute-start | bytes 1572872 | tf_op jit(solution)/shard_map/ppermute | solution.py:30
  6.0 22.8 %collective-permute-start.11 = (bf16[4,512,128]{2,1,0:T(8,128)(2,1)}, bf16[4,512,128]{2,1,0:T(8,128)(2,1)}, u32[]{:S(2)}, u32[]{:S(2)}) collective-permute-start(bf16[4,512,128]{2,1,0:T(8,128)(2,1)} %bitcast.71), channel_id=1, source_target_pairs={{0,96},{1,33},{2,98},{3,35},{4,100},{5,37},{6,102},{7,39},{8,104},... | collective-permute-start | bytes 1572872 | tf_op jit(solution)/shard_map/ppermute | solution.py:30
  8.4 19.6 %collective-permute-start = (bf16[48,8192]{1,0:T(8,128)(2,1)S(1)}, bf16[48,8192]{1,0:T(8,128)(2,1)}, u32[]{:S(2)}, u32[]{:S(2)}) collective-permute-start(bf16[48,8192]{1,0:T(8,128)(2,1)S(1)} %norm.1.p0), channel_id=1, source_target_pairs={{0,2},{1,7},{2,4},{3,1},{4,6},{5,3},{6,0},{7,5},{8,10},{9,15},{10,... | collective-permute-start | bytes 2359304 | tf_op jit(solution)/shard_map/ppermute | solution.py:30
  12.3 21.9 %copy-start.1 = (bf16[4,512,1,128]{3,1,2,0:T(8,128)(2,1)S(1)}, bf16[4,512,1,128]{3,1,2,0:T(8,128)(2,1)}, u32[]{:S(2)}) copy-start(bf16[4,512,1,128]{3,1,2,0:T(8,128)(2,1)} %param.15) | copy-start | bytes 1572868
  12.3 21.9 %copy-start.2 = (bf16[4,512,1,128]{3,1,2,0:T(8,128)(2,1)S(1)}, bf16[4,512,1,128]{3,1,2,0:T(8,128)(2,1)}, u32[]{:S(2)}) copy-start(bf16[4,512,1,128]{3,1,2,0:T(8,128)(2,1)} %param.16) | copy-start | bytes 1572868
  22.6 8.9 %collective-permute-start.9 = (bf16[4,512,128]{2,1,0:T(8,128)(2,1)S(1)}, bf16[4,512,128]{2,1,0:T(8,128)(2,1)}, u32[]{:S(2)}, u32[]{:S(2)}) collective-permute-start(bf16[4,512,128]{2,1,0:T(8,128)(2,1)S(1)} %collective-permute-done.7.refs_1_), channel_id=1, source_target_pairs={{0,8},{1,25},{2,10},{3,27},{4,12},{5,29},{6,14},{7,31},{8,16},{9,1... | collective-permute-start | bytes 1572872 | tf_op jit(solution)/shard_map/ppermute | solution.py:30
  25.4 8.8 %collective-permute-start.12 = (bf16[4,512,128]{2,1,0:T(8,128)(2,1)S(1)}, bf16[4,512,128]{2,1,0:T(8,128)(2,1)}, u32[]{:S(2)}, u32[]{:S(2)}) collective-permute-start(bf16[4,512,128]{2,1,0:T(8,128)(2,1)S(1)} %collective-permute-done.10.refs_5_.refs_8_), channel_id=1, source_target_pairs={{0,32},{1,97},{2,34},{3,99},{4,36},{5,101},{6,38},{7,103},{8,40},{... | collective-permute-start | bytes 1572872 | tf_op jit(solution)/shard_map/ppermute | solution.py:30
  28.1 22.2 %collective-permute-start.1 = (bf16[48,8192]{1,0:T(8,128)(2,1)}, bf16[48,8192]{1,0:T(8,128)(2,1)}, u32[]{:S(2)}, u32[]{:S(2)}) collective-permute-start(bf16[48,8192]{1,0:T(8,128)(2,1)} %collective-permute-done.p1), channel_id=1, source_target_pairs={{0,2},{1,7},{2,4},{3,1},{4,6},{5,3},{6,0},{7,5},{8,10},{9,15},{10,... | collective-permute-start | bytes 2359304 | tf_op jit(solution)/shard_map/ppermute | solution.py:30
  28.8 21.4 %copy-start.5 = (s32[1,384]{1,0:T(1,128)S(1)}, s32[1,384]{1,0:T(1,128)}, u32[]{:S(2)}) copy-start(s32[1,384]{1,0:T(1,128)} %npos_ref.1) | copy-start | bytes 4612
  28.8 41.4 %collective-permute-start.3 = (bf16[48,8192]{1,0:T(8,128)(2,1)S(1)}, bf16[48,8192]{1,0:T(8,128)(2,1)}, u32[]{:S(2)}, u32[]{:S(2)}) collective-permute-start(bf16[48,8192]{1,0:T(8,128)(2,1)S(1)} %norm.1.p0), channel_id=1, source_target_pairs={{0,1},{1,0},{2,3},{3,2},{4,5},{5,4},{6,7},{7,6},{8,9},{9,8},{10,11... | collective-permute-start | bytes 2359304 | tf_op jit(solution)/shard_map/ppermute | solution.py:30
  46.6 15.6 %collective-permute-start.13 = (bf16[8,512,128]{2,1,0:T(8,128)(2,1)}, bf16[8,512,128]{2,1,0:T(8,128)(2,1)}, u32[]{:S(2)}, u32[]{:S(2)}) collective-permute-start(bf16[8,512,128]{2,1,0:T(8,128)(2,1)} %get-tuple-element.15), channel_id=1, source_target_pairs={{0,32},{1,97},{2,34},{3,99},{4,36},{5,101},{6,38},{7,103},{8,40},{... | collective-permute-start | bytes 3145736 | tf_op jit(solution)/shard_map/ppermute | solution.py:30
  50.3 12.0 %collective-permute-start.2 = (bf16[48,8192]{1,0:T(8,128)(2,1)}, bf16[48,8192]{1,0:T(8,128)(2,1)}, u32[]{:S(2)}, u32[]{:S(2)}) collective-permute-start(bf16[48,8192]{1,0:T(8,128)(2,1)} %collective-permute-done.1.p2), channel_id=1, source_target_pairs={{0,2},{1,7},{2,4},{3,1},{4,6},{5,3},{6,0},{7,5},{8,10},{9,15},{10,... | collective-permute-start | bytes 2359304 | tf_op jit(solution)/shard_map/ppermute | solution.py:30
  51.2 17.7 %collective-permute-start.16 = (bf16[8,512,128]{2,1,0:T(8,128)(2,1)}, bf16[8,512,128]{2,1,0:T(8,128)(2,1)}, u32[]{:S(2)}, u32[]{:S(2)}) collective-permute-start(bf16[8,512,128]{2,1,0:T(8,128)(2,1)} %copy-done.8), channel_id=1, source_target_pairs={{0,8},{1,25},{2,10},{3,27},{4,12},{5,29},{6,14},{7,31},{8,16},{9,1... | collective-permute-start | bytes 3145736 | tf_op jit(solution)/shard_map/ppermute | solution.py:30
  53.2 17.9 %collective-permute-start.4 = (bf16[48,8192]{1,0:T(8,128)(2,1)}, bf16[48,8192]{1,0:T(8,128)(2,1)}, u32[]{:S(2)}, u32[]{:S(2)}) collective-permute-start(bf16[48,8192]{1,0:T(8,128)(2,1)} %collective-permute-done.p1), channel_id=1, source_target_pairs={{0,1},{1,0},{2,3},{3,2},{4,5},{5,4},{6,7},{7,6},{8,9},{9,8},{10,11... | collective-permute-start | bytes 2359304 | tf_op jit(solution)/shard_map/ppermute | solution.py:30
  62.2 11.5 %collective-permute-start.5 = (bf16[48,8192]{1,0:T(8,128)(2,1)}, bf16[48,8192]{1,0:T(8,128)(2,1)}, u32[]{:S(2)}, u32[]{:S(2)}) collective-permute-start(bf16[48,8192]{1,0:T(8,128)(2,1)} %collective-permute-done.1.p2), channel_id=1, source_target_pairs={{0,1},{1,0},{2,3},{3,2},{4,5},{5,4},{6,7},{7,6},{8,9},{9,8},{10,11... | collective-permute-start | bytes 2359304 | tf_op jit(solution)/shard_map/ppermute | solution.py:30
  62.4 14.0 %collective-permute-start.6 = (bf16[48,8192]{1,0:T(8,128)(2,1)}, bf16[48,8192]{1,0:T(8,128)(2,1)}, u32[]{:S(2)}, u32[]{:S(2)}) collective-permute-start(bf16[48,8192]{1,0:T(8,128)(2,1)} %collective-permute-done.2.p3), channel_id=1, source_target_pairs={{0,1},{1,0},{2,3},{3,2},{4,5},{5,4},{6,7},{7,6},{8,9},{9,8},{10,11... | collective-permute-start | bytes 2359304 | tf_op jit(solution)/shard_map/ppermute | solution.py:30
  63.0 13.4 %copy-start.6 = (bf16[8192,128]{1,0:T(8,128)(2,1)S(1)}, bf16[8192,128]{1,0:T(8,128)(2,1)}, u32[]{:S(2)}) copy-start(bf16[8192,128]{1,0:T(8,128)(2,1)} %wk_hbm.1) | copy-start | bytes 6291460
  63.0 13.3 %copy-start.7 = (bf16[8192,128]{1,0:T(8,128)(2,1)S(1)}, bf16[8192,128]{1,0:T(8,128)(2,1)}, u32[]{:S(2)}) copy-start(bf16[8192,128]{1,0:T(8,128)(2,1)} %wv_hbm.1) | copy-start | bytes 6291460
  69.0 24.2 %collective-permute-start.14 = (bf16[4,512,128]{2,1,0:T(8,128)(2,1)S(1)}, bf16[4,512,128]{2,1,0:T(8,128)(2,1)S(1)}, u32[]{:S(2)}, u32[]{:S(2)}) collective-permute-start(bf16[4,512,128]{2,1,0:T(8,128)(2,1)S(1)} %copy-done.12), channel_id=1, source_target_pairs={{0,96},{1,33},{2,98},{3,35},{4,100},{5,37},{6,102},{7,39},{8,104},... | collective-permute-start | bytes 1572872 | tf_op jit(solution)/shard_map/ppermute | solution.py:30
  70.2 23.0 %collective-permute-start.17 = (bf16[4,512,128]{2,1,0:T(8,128)(2,1)S(1)}, bf16[4,512,128]{2,1,0:T(8,128)(2,1)S(1)}, u32[]{:S(2)}, u32[]{:S(2)}) collective-permute-start(bf16[4,512,128]{2,1,0:T(8,128)(2,1)S(1)} %copy-done.10), channel_id=1, source_target_pairs={{0,24},{1,9},{2,26},{3,11},{4,28},{5,13},{6,30},{7,15},{8,0},{9,17... | collective-permute-start | bytes 1572872 | tf_op jit(solution)/shard_map/ppermute | solution.py:30
  71.1 22.1 %collective-permute-start.15 = (bf16[4,512,128]{2,1,0:T(8,128)(2,1)S(1)}, bf16[4,512,128]{2,1,0:T(8,128)(2,1)S(1)}, u32[]{:S(2)}, u32[]{:S(2)}) collective-permute-start(bf16[4,512,128]{2,1,0:T(8,128)(2,1)S(1)} %slice.12), channel_id=1, source_target_pairs={{0,32},{1,97},{2,34},{3,99},{4,36},{5,101},{6,38},{7,103},{8,40},{... | collective-permute-start | bytes 1572872 | tf_op jit(solution)/shard_map/ppermute | solution.py:30
  73.7 19.5 %collective-permute-start.18 = (bf16[4,512,128]{2,1,0:T(8,128)(2,1)S(1)}, bf16[4,512,128]{2,1,0:T(8,128)(2,1)S(1)}, u32[]{:S(2)}, u32[]{:S(2)}) collective-permute-start(bf16[4,512,128]{2,1,0:T(8,128)(2,1)S(1)} %slice.13), channel_id=1, source_target_pairs={{0,8},{1,25},{2,10},{3,27},{4,12},{5,29},{6,14},{7,31},{8,16},{9,1... | collective-permute-start | bytes 1572872 | tf_op jit(solution)/shard_map/ppermute | solution.py:30
  (10 other events, 49.0 us)

commit v2 on v1

--- a/solution.py
+++ b/solution.py
@@ -10,7 +10,8 @@
 BF16 = jnp.bfloat16
 F32 = jnp.float32
 SIDE = 4
-ROWS = 64
+ROWS = 128
+STEP = 2
 THETA = 500000.0
 EPS = 1e-05
 HIDDEN_POS = 1 << 30
@@ -60,41 +61,33 @@
     return pl.pallas_call(
         norm_kernel,
         out_shape=jax.ShapeDtypeStruct(tokens.shape, BF16),
-        compiler_params=pltpu.CompilerParams(vmem_limit_bytes=24 * MIB),
+        compiler_params=pltpu.CompilerParams(vmem_limit_bytes=8 * MIB),
         name="norm",
     )(tokens, gain.reshape(1, -1))
 
 
 def pick_kernel(index_ref, *refs):
-    sources, (k_fwd, k_back, v_fwd, v_back), sems = refs[:8], refs[8:12], refs[12]
-    copies = []
+    sources, (k_fwd, k_back, v_fwd, v_back) = refs[:8], refs[8:]
     for tensor, (fwd, back) in enumerate(((k_fwd, k_back), (v_fwd, v_back))):
         for target in range(3):
             for slot in range(4):
-                dest = fwd.at[target * 4 + slot] if target < 2 else back.at[slot]
-                n = tensor * 12 + target * 4 + slot
-                copies.append(
-                    pltpu.make_async_copy(
-                        sources[tensor * 4 + slot].at[index_ref[n]], dest, sems.at[n]
-                    )
-                )
-    for copy in copies:
-        copy.start()
-    for copy in copies:
-        copy.wait()
+                chosen = sources[tensor * 4 + slot][index_ref[tensor * 12 + target * 4 + slot]]
+                if target < 2:
+                    fwd[target * 4 + slot] = chosen
+                else:
+                    back[slot] = chosen
 
 
 def pick(index, keys, values):
     _, tokens, dim = keys[0].shape
-    any_spec = pl.BlockSpec(memory_space=pl.ANY)
+    vmem = pl.BlockSpec(memory_space=pltpu.VMEM)
     shapes = [jax.ShapeDtypeStruct((n, tokens, dim), BF16) for n in (8, 4, 8, 4)]
     return pl.pallas_call(
         pick_kernel,
         out_shape=shapes,
-        in_specs=[pl.BlockSpec(memory_space=pltpu.SMEM)] + [any_spec] * 8,
-        out_specs=[any_spec] * 4,
-        scratch_shapes=[pltpu.SemaphoreType.DMA((24,))],
-        compiler_params=pltpu.CompilerParams(vmem_limit_bytes=2 * MIB),
+        in_specs=[pl.BlockSpec(memory_space=pltpu.SMEM)] + [vmem] * 8,
+        out_specs=[vmem] * 4,
+        compiler_params=pltpu.CompilerParams(vmem_limit_bytes=10 * MIB),
         cost_estimate=pl.CostEstimate(flops=0, bytes_accessed=6 * MIB, transcendentals=0),
         name="pick",
     )(index, *keys, *values)
@@ -171,7 +164,7 @@
             pltpu.SemaphoreType.DMA((8,)),
             pltpu.SemaphoreType.DMA((2,)),
         ],
-        compiler_params=pltpu.CompilerParams(vmem_limit_bytes=40 * MIB),
+        compiler_params=pltpu.CompilerParams(vmem_limit_bytes=24 * MIB),
         cost_estimate=pl.CostEstimate(
             flops=2 * sel * width * 1280, bytes_accessed=30 * MIB, transcendentals=0
         ),
@@ -180,7 +173,7 @@
 
 
 def attend_kernel(
-    where_ref, count_ref, q_ref, nk_ref, nv_ref, qpos_ref, kpos_ref, npos_ref, cos_ref, sin_ref, *refs
+    where_ref, count_ref, q_ref, nk_ref, nv_ref, qpos_ref, kpos_ref, npos_ref, cos_ref, sin_ref, far_cos_ref, far_sin_ref, *refs
 ):
     keys, values, out_ref = refs[:7], refs[7:14], refs[14]
     k_buf, v_buf, nv_buf, s_buf, m_buf, acc, sems = refs[15:]
@@ -214,8 +207,10 @@
 
     for j in range(blocks):
         pltpu.make_async_copy(keys[0].at[0], k_dest(j), sems.at[0, j]).wait()
-        at = pl.ds(j * block, block)
-        k_buf[j] = rope(k_buf[j].astype(F32), cos_ref[at, :], sin_ref[at, :]).astype(BF16)
+        far_cos, far_sin = far_cos_ref[j : j + 1, :], far_sin_ref[j : j + 1, :]
+        cosine = far_cos * cos_ref[...] - far_sin * sin_ref[...]
+        sine = far_sin * cos_ref[...] + far_cos * sin_ref[...]
+        k_buf[j] = rope(k_buf[j].astype(F32), cosine, sine).astype(BF16)
     for j in range(blocks):
         pltpu.make_async_copy(values[0].at[0], v_dest(j), sems.at[1, j]).wait()
 
@@ -240,13 +235,17 @@
         scores, most = masked_scores(queries, nk_ref[...], npos_ref[...], query_pos)
         s_buf[:, ctx:] = scores
         m_buf[...] = most
-        count = count_ref[i]
+        count = (count_ref[i] + STEP - 1) // STEP
+        span = STEP * block
 
         def first(j, carry):
             scores, most = masked_scores(
-                q_ref[:, rows, :].reshape(tall, dim), k_buf[j], kpos_ref[pl.ds(j, 1), :], qpos_ref[rows, :]
+                q_ref[:, rows, :].reshape(tall, dim),
+                k_buf[pl.ds(j * STEP, STEP)].reshape(span, dim),
+                jnp.concatenate([kpos_ref[pl.ds(j * STEP + n, 1), :] for n in range(STEP)], axis=1),
+                qpos_ref[rows, :],
             )
-            s_buf[:, pl.ds(pl.multiple_of(j * block, block), block)] = scores
+            s_buf[:, pl.ds(pl.multiple_of(j * span, span), span)] = scores
             m_buf[...] = jnp.maximum(m_buf[...], most)
             return carry
 
@@ -260,7 +259,7 @@
         acc[...] = jnp.dot(expos(s_buf[:, ctx:]), nv_buf[...], preferred_element_type=F32)
 
         def second(j, carry):
-            at = pl.ds(pl.multiple_of(j * block, block), block)
+            at = pl.ds(pl.multiple_of(j * span, span), span)
             acc[...] += jnp.dot(expos(s_buf[:, at]), v_buf[at, :], preferred_element_type=F32)
             return carry
 
@@ -273,7 +272,7 @@
     lax.fori_loop(0, sel // ROWS, tile, 0)
 
 
-def attend(where, count, queries, new_k, new_v, qpos, kpos, npos, cosine, sine, keys, values):
+def attend(where, count, queries, new_k, new_v, qpos, kpos, npos, angles, keys, values):
     heads, sel, dim = queries.shape
     _, block, _ = keys[0].shape
     blocks = kpos.shape[0]
@@ -285,7 +284,7 @@
     return pl.pallas_call(
         attend_kernel,
         out_shape=jax.ShapeDtypeStruct((sel, heads * dim), BF16),
-        in_specs=[smem] * 2 + [vmem] * 8 + [any_spec] * 14,
+        in_specs=[smem] * 2 + [vmem] * 10 + [any_spec] * 14,
         out_specs=vmem,
         scratch_shapes=[
             pltpu.VMEM((blocks, block, dim), BF16),
@@ -301,7 +300,7 @@
             flops=4 * heads * sel * ctx * dim, bytes_accessed=8 * MIB, transcendentals=heads * sel * ctx
         ),
         name="attend",
-    )(where, count, queries, new_k, new_v, qpos, kpos, npos, cosine, sine, *keys, *values)
+    )(where, count, queries, new_k, new_v, qpos, kpos, npos, *angles, *keys, *values)
 
 
 def tables(positions):
@@ -387,7 +386,7 @@
     qpos = jnp.broadcast_to(positions[:, None], (sel, 128))
     count = positions[ROWS - 1 :: ROWS] // block + 1
     q_cos, q_sin = tables(positions)
-    k_cos, k_sin = tables(everywhere)
+    angles = (*tables(everywhere[:block]), *tables(everywhere[::block]))
 
     place = jnp.stack(
         [((z + s * sign + SIDE) % SIDE) * 2 + core for s in (0, -1, 2, 1)]
@@ -395,7 +394,7 @@
     ).astype(jnp.int32)
     queries, new_k, new_v = project(place, mine + theirs, w_query, w_key, w_value, q_cos, q_sin)
     mixed = attend(
-        where, count, queries, new_k, new_v, qpos, kpos, positions[None], k_cos, k_sin, keys, values
+        where, count, queries, new_k, new_v, qpos, kpos, positions[None], angles, keys, values
     )
     return mixed[None]
 

time: 121 us -> 122 us (level)
  local copies, waits for them, and re-layouts: 7.31 us -> 28.8 us
  Pallas kernels: 53.9 us -> 38.8 us
  other arithmetic: 18.1 us -> 5.48 us
  waiting for transfers between devices: 14.3 us -> 19.2 us
  starting transfers between devices: 26 us -> 28.7 us
    unnamed x31 -> x49, local copies, waits for them, and re-layouts: 3.85 us -> 26.4 us
    neg x2 -> x3, other arithmetic: 10.6 us -> 1.86 us  [tables(): -sine]
    pallas_call x1, Pallas kernels: 9.84 us -> 2.21 us  [pick(): pl.pallas_call(pick_kernel, out_shape=shapes, in_specs=[pl.BlockSpec(memo...]
    pallas_call x1, Pallas kernels: 26.7 us -> 20.9 us  [attend(): pl.pallas_call(attend_kernel, out_shape=jax.ShapeDtypeStruct((sel, heads...]
    concatenate x2 -> x3, other arithmetic: 5.68 us -> 0.45 us  [tables(): jnp.concatenate([cosine, cosine], axis=1)]
    ppermute x19, waiting for transfers between devices: 14.3 us -> 19.2 us  [move(): return lax.ppermute(value, ('req', 'tp'), pairs)]
    ppermute x19, starting transfers between devices: 26 us -> 28.7 us  [move(): return lax.ppermute(value, ('req', 'tp'), pairs)]
    pallas_call x1, Pallas kernels: 16.8 us -> 15.2 us  [project(): pl.pallas_call(project_kernel, grid=(5,), out_shape=[jax.ShapeDtypeStruct...]
  transfers between devices with their start and end apart: 19 -> 19, of which waited for: 3 -> 4; matrix products, arithmetic and copies ran while one was open for 18% -> 6% of each run, Pallas kernels for 23% -> 14%
where the time goes in v2:
time: 122 us
  Pallas kernels  38.8 us (32%)
  local copies, waits for them, and re-layouts  28.8 us (24%)
  starting transfers between devices  28.7 us (24%)
  waiting for transfers between devices  19.2 us (16%)
  other arithmetic  5.48 us (4%)
    ppermute x19, starting transfers between devices, move(): return lax.ppermute(value, ('req', 'tp'), pairs)  28.7 us
    unnamed x49, local copies, waits for them, and re-layouts  26.4 us
    pallas_call x1, Pallas kernels, attend(): pl.pallas_call(attend_kernel, out_shape=jax.ShapeDtypeStruct((sel, heads...  20.9 us
    ppermute x19, waiting for transfers between devices, move(): return lax.ppermute(value, ('req', 'tp'), pairs)  19.2 us
    pallas_call x1, Pallas kernels, project(): pl.pallas_call(project_kernel, grid=(5,), out_shape=[jax.ShapeDtypeStruct...  15.2 us
  transfers between devices with their start and end apart: 19, of which 4 were waited for; matrix products, arithmetic and copies ran while one was open for 6% of the time, Pallas kernels for 14%

profile of v2, /device:TPU:1, one launch (start us, length us, event | category | flops | bytes accessed | tf_op | source)
XLA Modules:
  0.0 121.6 jit_solution(7026571501060783367)
XLA Ops:
  0.8 1.1 copy-done
  2.4 4.7 %collective-permute-start = (bf16[48,8192]{1,0:T(8,128)(2,1)S(1)}, bf16[48,8192]{1,0:T(8,128)(2,1)}, u32[]{:S(2)}, u32[]{:S(2)}) collective-permute-start(bf16[48,8192]{1,0:T(8,128)(2,1)S(1)} %norm.1.p0), channel_id=1, source_target_pairs={{0,2},{1,7},{2,4},{3,1},{4,6},{5,3},{6,0},{7,5},{8,10},{9,15},{10,... | collective-permute-start | bytes 2359304 | tf_op jit(solution)/shard_map/ppermute | solution.py:31
  7.0 2.5 %collective-permute-start.7 = (bf16[4,512,128]{2,1,0:T(8,128)(2,1)}, bf16[4,512,128]{2,1,0:T(8,128)(2,1)S(1)}, u32[]{:S(2)}, u32[]{:S(2)}) collective-permute-start(bf16[4,512,128]{2,1,0:T(8,128)(2,1)} %bitcast.66), channel_id=1, source_target_pairs={{0,8},{1,25},{2,10},{3,27},{4,12},{5,29},{6,14},{7,31},{8,16},{9,1... | collective-permute-start | bytes 1572872 | tf_op jit(solution)/shard_map/ppermute | solution.py:31
  9.5 2.7 %collective-permute-start.10 = (bf16[4,512,128]{2,1,0:T(8,128)(2,1)}, bf16[4,512,128]{2,1,0:T(8,128)(2,1)S(1)}, u32[]{:S(2)}, u32[]{:S(2)}) collective-permute-start(bf16[4,512,128]{2,1,0:T(8,128)(2,1)} %bitcast.70), channel_id=1, source_target_pairs={{0,32},{1,97},{2,34},{3,99},{4,36},{5,101},{6,38},{7,103},{8,40},{... | collective-permute-start | bytes 1572872 | tf_op jit(solution)/shard_map/ppermute | solution.py:31
  13.0 1.1 select_reduce_fusion.1
  14.7 6.7 %collective-permute-done.7.refs_1_ = bf16[4,512,128]{2,1,0:T(8,128)(2,1)S(1)} collective-permute-done((bf16[4,512,128]{2,1,0:T(8,128)(2,1)}, bf16[4,512,128]{2,1,0:T(8,128)(2,1)S(1)}, u32[]{:S(2)}, u32[]{:S(2)}) %collective-permute-start.7) | collective-permute-done | bytes 524320 | tf_op jit(solution)/shard_map/ppermute | solution.py:31
  21.4 3.1 %collective-permute-start.9 = (bf16[4,512,128]{2,1,0:T(8,128)(2,1)S(1)}, bf16[4,512,128]{2,1,0:T(8,128)(2,1)S(1)}, u32[]{:S(2)}, u32[]{:S(2)}) collective-permute-start(bf16[4,512,128]{2,1,0:T(8,128)(2,1)S(1)} %collective-permute-done.7.refs_1_), channel_id=1, source_target_pairs={{0,8},{1,25},{2,10},{3,27},{4,12},{5,29},{6,14},{7,31},{8,16},{9,1... | collective-permute-start | bytes 1572872 | tf_op jit(solution)/shard_map/ppermute | solution.py:31
  24.4 3.0 %collective-permute-start.12 = (bf16[4,512,128]{2,1,0:T(8,128)(2,1)S(1)}, bf16[4,512,128]{2,1,0:T(8,128)(2,1)}, u32[]{:S(2)}, u32[]{:S(2)}) collective-permute-start(bf16[4,512,128]{2,1,0:T(8,128)(2,1)S(1)} %collective-permute-done.10.refs_5_.refs_8_), channel_id=1, source_target_pairs={{0,32},{1,97},{2,34},{3,99},{4,36},{5,101},{6,38},{7,103},{8,40},{... | collective-permute-start | bytes 1572872 | tf_op jit(solution)/shard_map/ppermute | solution.py:31
  29.4 1.2 collective-permute-done.9.refs_3_
  30.6 3.0 %collective-permute-done.12.refs_7_.refs_10_ = bf16[4,512,128]{2,1,0:T(8,128)(2,1)} collective-permute-done((bf16[4,512,128]{2,1,0:T(8,128)(2,1)S(1)}, bf16[4,512,128]{2,1,0:T(8,128)(2,1)}, u32[]{:S(2)}, u32[]{:S(2)}) %collective-permute-start.12) | collective-permute-done | bytes 524320 | tf_op jit(solution)/shard_map/ppermute | solution.py:31
  35.6 2.2 %pick.1 = (bf16[8,512,128]{2,1,0:T(8,128)(2,1)}, bf16[4,512,128]{2,1,0:T(8,128)(2,1)S(1)}, bf16[8,512,128]{2,1,0:T(8,128)(2,1)S(1)}, bf16[4,512,128]{2,1,0:T(8,128)(2,1)S(1)}) custom-call(s32[24]{0:T(128)S(1)} %select_reduce_fusion.2.index_ref, bf16[4,512,128]{2,1,0:T(8,128)(2,1)S(1)} %bitcast.68, bf16[4,512,128]{2,1,0:T(8,128)(2,1)S(1)} %collective-permute-done.7.refs_1_, ...), custom_call_target="tpu_custom_call" | custom-call | bytes 6291456 | tf_op jit(solution)/shard_map/pick/pallas_call | solution.py:85
  40.4 3.5 %collective-permute-start.13 = (bf16[8,512,128]{2,1,0:T(8,128)(2,1)}, bf16[8,512,128]{2,1,0:T(8,128)(2,1)}, u32[]{:S(2)}, u32[]{:S(2)}) collective-permute-start(bf16[8,512,128]{2,1,0:T(8,128)(2,1)} %get-tuple-element.15), channel_id=1, source_target_pairs={{0,32},{1,97},{2,34},{3,99},{4,36},{5,101},{6,38},{7,103},{8,40},{... | collective-permute-start | bytes 3145736 | tf_op jit(solution)/shard_map/ppermute | solution.py:31
  45.2 2.1 %collective-permute-start.16 = (bf16[8,512,128]{2,1,0:T(8,128)(2,1)}, bf16[8,512,128]{2,1,0:T(8,128)(2,1)S(1)}, u32[]{:S(2)}, u32[]{:S(2)}) collective-permute-start(bf16[8,512,128]{2,1,0:T(8,128)(2,1)} %copy-done.9), channel_id=1, source_target_pairs={{0,8},{1,25},{2,10},{3,27},{4,12},{5,29},{6,14},{7,31},{8,16},{9,1... | collective-permute-start | bytes 3145736 | tf_op jit(solution)/shard_map/ppermute | solution.py:31
  47.6 8.4 %collective-permute-done.13.refs_4_ = bf16[8,512,128]{2,1,0:T(8,128)(2,1)} collective-permute-done((bf16[8,512,128]{2,1,0:T(8,128)(2,1)}, bf16[8,512,128]{2,1,0:T(8,128)(2,1)}, u32[]{:S(2)}, u32[]{:S(2)}) %collective-permute-start.13) | collective-permute-done | bytes 1048608 | tf_op jit(solution)/shard_map/ppermute | solution.py:31
  56.0 1.3 %collective-permute-start.5 = (bf16[48,8192]{1,0:T(8,128)(2,1)}, bf16[48,8192]{1,0:T(8,128)(2,1)S(1)}, u32[]{:S(2)}, u32[]{:S(2)}) collective-permute-start(bf16[48,8192]{1,0:T(8,128)(2,1)} %collective-permute-done.1.p2), channel_id=1, source_target_pairs={{0,1},{1,0},{2,3},{3,2},{4,5},{5,4},{6,7},{7,6},{8,9},{9,8},{10,11... | collective-permute-start | bytes 2359304 | tf_op jit(solution)/shard_map/ppermute | solution.py:31
  58.5 1.1 slice.32
  59.9 2.7 %collective-permute-start.15 = (bf16[4,512,128]{2,1,0:T(8,128)(2,1)S(1)}, bf16[4,512,128]{2,1,0:T(8,128)(2,1)S(1)}, u32[]{:S(2)}, u32[]{:S(2)}) collective-permute-start(bf16[4,512,128]{2,1,0:T(8,128)(2,1)S(1)} %slice.32), channel_id=1, source_target_pairs={{0,32},{1,97},{2,34},{3,99},{4,36},{5,101},{6,38},{7,103},{8,40},{... | collective-permute-start | bytes 1572872 | tf_op jit(solution)/shard_map/ppermute | solution.py:31
  62.6 2.7 %collective-permute-start.18 = (bf16[4,512,128]{2,1,0:T(8,128)(2,1)S(1)}, bf16[4,512,128]{2,1,0:T(8,128)(2,1)S(1)}, u32[]{:S(2)}, u32[]{:S(2)}) collective-permute-start(bf16[4,512,128]{2,1,0:T(8,128)(2,1)S(1)} %slice.33), channel_id=1, source_target_pairs={{0,8},{1,25},{2,10},{3,27},{4,12},{5,29},{6,14},{7,31},{8,16},{9,1... | collective-permute-start | bytes 1572872 | tf_op jit(solution)/shard_map/ppermute | solution.py:31
  65.3 5.8 %copy-done.6 = bf16[8192,1024]{1,0:T(8,128)(2,1)S(1)} copy-done((bf16[8192,1024]{1,0:T(8,128)(2,1)S(1)}, bf16[8192,1024]{1,0:T(8,128)(2,1)}, u32[]{:S(2)}) %copy-start.6) | copy-done | bytes 16777240
  71.1 1.6 %copy-done.7 = bf16[8192,128]{1,0:T(8,128)(2,1)S(1)} copy-done((bf16[8192,128]{1,0:T(8,128)(2,1)S(1)}, bf16[8192,128]{1,0:T(8,128)(2,1)}, u32[]{:S(2)}) %copy-start.7) | copy-done | bytes 2097176
  72.6 1.6 %copy-done.8 = bf16[8192,128]{1,0:T(8,128)(2,1)S(1)} copy-done((bf16[8192,128]{1,0:T(8,128)(2,1)S(1)}, bf16[8192,128]{1,0:T(8,128)(2,1)}, u32[]{:S(2)}) %copy-start.8) | copy-done | bytes 2097176
  74.2 15.2 %project.1 = (bf16[8,384,128]{2,1,0:T(8,128)(2,1)S(1)}, bf16[384,128]{1,0:T(8,128)(2,1)S(1)}, bf16[384,128]{1,0:T(8,128)(2,1)S(1)}) custom-call(s32[8]{0:T(128)S(1)} %stack.118.place_ref, bf16[48,8192]{1,0:T(8,128)(2,1)S(1)} %norm.1.p0, bf16[48,8192]{1,0:T(8,128)(2,1)} %collective-permute-done.p1, bf16[48,8192]{1,0:T(8,128)(2,1)} %collective-permute-done.1.p2, ...), custom_call_target="tpu_custom_call" | custom-call | flops 8053063680 | bytes 31457280 | tf_op jit(solution)/shard_map/project/pallas_call | solution.py:148
  98.5 1.1 copy-done.21
  100.5 20.9 %attend.1 = bf16[384,1024]{1,0:T(8,128)(2,1)} custom-call(s32[4,8]{1,0:T(4,128)S(1)} %pad_add_fusion.where_ref, s32[3]{0:T(128)S(1)} %fusion.9.count_ref, bf16[8,384,128]{2,1,0:T(8,128)(2,1)S(1)} %copy-done.21, bf16[384,128]{1,0:T(8,128)(2,1)S(1)} %get-tuple-element.13.nk_ref, bf16[384,128]{1,0:T(8,128)(2,1)S(1)} %copy-done.23, ...), custom_call_target="tpu_custom_call" | custom-call | flops 6442450944 | bytes 8388608 | tf_op jit(solution)/shard_map/attend/pallas_call | solution.py:284
  (100 shorter events, 21.9 us)
Async XLA Ops:
  2.4 25.0 %collective-permute-start = (bf16[48,8192]{1,0:T(8,128)(2,1)S(1)}, bf16[48,8192]{1,0:T(8,128)(2,1)}, u32[]{:S(2)}, u32[]{:S(2)}) collective-permute-start(bf16[48,8192]{1,0:T(8,128)(2,1)S(1)} %norm.1.p0), channel_id=1, source_target_pairs={{0,2},{1,7},{2,4},{3,1},{4,6},{5,3},{6,0},{7,5},{8,10},{9,15},{10,... | collective-permute-start | bytes 2359304 | tf_op jit(solution)/shard_map/ppermute | solution.py:31
  7.0 14.3 %collective-permute-start.7 = (bf16[4,512,128]{2,1,0:T(8,128)(2,1)}, bf16[4,512,128]{2,1,0:T(8,128)(2,1)S(1)}, u32[]{:S(2)}, u32[]{:S(2)}) collective-permute-start(bf16[4,512,128]{2,1,0:T(8,128)(2,1)} %bitcast.66), channel_id=1, source_target_pairs={{0,8},{1,25},{2,10},{3,27},{4,12},{5,29},{6,14},{7,31},{8,16},{9,1... | collective-permute-start | bytes 1572872 | tf_op jit(solution)/shard_map/ppermute | solution.py:31
  9.5 19.7 %collective-permute-start.8 = (bf16[4,512,128]{2,1,0:T(8,128)(2,1)}, bf16[4,512,128]{2,1,0:T(8,128)(2,1)S(1)}, u32[]{:S(2)}, u32[]{:S(2)}) collective-permute-start(bf16[4,512,128]{2,1,0:T(8,128)(2,1)} %bitcast.67), channel_id=1, source_target_pairs={{0,24},{1,9},{2,26},{3,11},{4,28},{5,13},{6,30},{7,15},{8,0},{9,17... | collective-permute-start | bytes 1572872 | tf_op jit(solution)/shard_map/ppermute | solution.py:31
  9.5 14.9 %collective-permute-start.10 = (bf16[4,512,128]{2,1,0:T(8,128)(2,1)}, bf16[4,512,128]{2,1,0:T(8,128)(2,1)S(1)}, u32[]{:S(2)}, u32[]{:S(2)}) collective-permute-start(bf16[4,512,128]{2,1,0:T(8,128)(2,1)} %bitcast.70), channel_id=1, source_target_pairs={{0,32},{1,97},{2,34},{3,99},{4,36},{5,101},{6,38},{7,103},{8,40},{... | collective-permute-start | bytes 1572872 | tf_op jit(solution)/shard_map/ppermute | solution.py:31
  12.3 17.1 %collective-permute-start.11 = (bf16[4,512,128]{2,1,0:T(8,128)(2,1)}, bf16[4,512,128]{2,1,0:T(8,128)(2,1)S(1)}, u32[]{:S(2)}, u32[]{:S(2)}) collective-permute-start(bf16[4,512,128]{2,1,0:T(8,128)(2,1)} %bitcast.71), channel_id=1, source_target_pairs={{0,96},{1,33},{2,98},{3,35},{4,100},{5,37},{6,102},{7,39},{8,104},... | collective-permute-start | bytes 1572872 | tf_op jit(solution)/shard_map/ppermute | solution.py:31
  21.4 9.2 %collective-permute-start.9 = (bf16[4,512,128]{2,1,0:T(8,128)(2,1)S(1)}, bf16[4,512,128]{2,1,0:T(8,128)(2,1)S(1)}, u32[]{:S(2)}, u32[]{:S(2)}) collective-permute-start(bf16[4,512,128]{2,1,0:T(8,128)(2,1)S(1)} %collective-permute-done.7.refs_1_), channel_id=1, source_target_pairs={{0,8},{1,25},{2,10},{3,27},{4,12},{5,29},{6,14},{7,31},{8,16},{9,1... | collective-permute-start | bytes 1572872 | tf_op jit(solution)/shard_map/ppermute | solution.py:31
  24.4 9.1 %collective-permute-start.12 = (bf16[4,512,128]{2,1,0:T(8,128)(2,1)S(1)}, bf16[4,512,128]{2,1,0:T(8,128)(2,1)}, u32[]{:S(2)}, u32[]{:S(2)}) collective-permute-start(bf16[4,512,128]{2,1,0:T(8,128)(2,1)S(1)} %collective-permute-done.10.refs_5_.refs_8_), channel_id=1, source_target_pairs={{0,32},{1,97},{2,34},{3,99},{4,36},{5,101},{6,38},{7,103},{8,40},{... | collective-permute-start | bytes 1572872 | tf_op jit(solution)/shard_map/ppermute | solution.py:31
  27.4 16.9 %collective-permute-start.1 = (bf16[48,8192]{1,0:T(8,128)(2,1)}, bf16[48,8192]{1,0:T(8,128)(2,1)}, u32[]{:S(2)}, u32[]{:S(2)}) collective-permute-start(bf16[48,8192]{1,0:T(8,128)(2,1)} %collective-permute-done.p1), channel_id=1, source_target_pairs={{0,2},{1,7},{2,4},{3,1},{4,6},{5,3},{6,0},{7,5},{8,10},{9,15},{10,... | collective-permute-start | bytes 2359304 | tf_op jit(solution)/shard_map/ppermute | solution.py:31
  29.3 30.5 %collective-permute-start.3 = (bf16[48,8192]{1,0:T(8,128)(2,1)S(1)}, bf16[48,8192]{1,0:T(8,128)(2,1)}, u32[]{:S(2)}, u32[]{:S(2)}) collective-permute-start(bf16[48,8192]{1,0:T(8,128)(2,1)S(1)} %norm.1.p0), channel_id=1, source_target_pairs={{0,1},{1,0},{2,3},{3,2},{4,5},{5,4},{6,7},{7,6},{8,9},{9,8},{10,11... | collective-permute-start | bytes 2359304 | tf_op jit(solution)/shard_map/ppermute | solution.py:31
  40.4 15.6 %collective-permute-start.13 = (bf16[8,512,128]{2,1,0:T(8,128)(2,1)}, bf16[8,512,128]{2,1,0:T(8,128)(2,1)}, u32[]{:S(2)}, u32[]{:S(2)}) collective-permute-start(bf16[8,512,128]{2,1,0:T(8,128)(2,1)} %get-tuple-element.15), channel_id=1, source_target_pairs={{0,32},{1,97},{2,34},{3,99},{4,36},{5,101},{6,38},{7,103},{8,40},{... | collective-permute-start | bytes 3145736 | tf_op jit(solution)/shard_map/ppermute | solution.py:31
  44.3 13.0 %collective-permute-start.2 = (bf16[48,8192]{1,0:T(8,128)(2,1)}, bf16[48,8192]{1,0:T(8,128)(2,1)S(1)}, u32[]{:S(2)}, u32[]{:S(2)}) collective-permute-start(bf16[48,8192]{1,0:T(8,128)(2,1)} %collective-permute-done.1.p2), channel_id=1, source_target_pairs={{0,2},{1,7},{2,4},{3,1},{4,6},{5,3},{6,0},{7,5},{8,10},{9,15},{10,... | collective-permute-start | bytes 2359304 | tf_op jit(solution)/shard_map/ppermute | solution.py:31
  45.2 14.4 %collective-permute-start.16 = (bf16[8,512,128]{2,1,0:T(8,128)(2,1)}, bf16[8,512,128]{2,1,0:T(8,128)(2,1)S(1)}, u32[]{:S(2)}, u32[]{:S(2)}) collective-permute-start(bf16[8,512,128]{2,1,0:T(8,128)(2,1)} %copy-done.9), channel_id=1, source_target_pairs={{0,8},{1,25},{2,10},{3,27},{4,12},{5,29},{6,14},{7,31},{8,16},{9,1... | collective-permute-start | bytes 3145736 | tf_op jit(solution)/shard_map/ppermute | solution.py:31
  47.5 12.4 %collective-permute-start.4 = (bf16[48,8192]{1,0:T(8,128)(2,1)}, bf16[48,8192]{1,0:T(8,128)(2,1)S(1)}, u32[]{:S(2)}, u32[]{:S(2)}) collective-permute-start(bf16[48,8192]{1,0:T(8,128)(2,1)} %collective-permute-done.p1), channel_id=1, source_target_pairs={{0,1},{1,0},{2,3},{3,2},{4,5},{5,4},{6,7},{7,6},{8,9},{9,8},{10,11... | collective-permute-start | bytes 2359304 | tf_op jit(solution)/shard_map/ppermute | solution.py:31
  56.0 6.6 %collective-permute-start.5 = (bf16[48,8192]{1,0:T(8,128)(2,1)}, bf16[48,8192]{1,0:T(8,128)(2,1)S(1)}, u32[]{:S(2)}, u32[]{:S(2)}) collective-permute-start(bf16[48,8192]{1,0:T(8,128)(2,1)} %collective-permute-done.1.p2), channel_id=1, source_target_pairs={{0,1},{1,0},{2,3},{3,2},{4,5},{5,4},{6,7},{7,6},{8,9},{9,8},{10,11... | collective-permute-start | bytes 2359304 | tf_op jit(solution)/shard_map/ppermute | solution.py:31
  57.3 8.0 %collective-permute-start.6 = (bf16[48,8192]{1,0:T(8,128)(2,1)S(1)}, bf16[48,8192]{1,0:T(8,128)(2,1)S(1)}, u32[]{:S(2)}, u32[]{:S(2)}) collective-permute-start(bf16[48,8192]{1,0:T(8,128)(2,1)S(1)} %collective-permute-done.2.p3), channel_id=1, source_target_pairs={{0,1},{1,0},{2,3},{3,2},{4,5},{5,4},{6,7},{7,6},{8,9},{9,8},{10,11... | collective-permute-start | bytes 2359304 | tf_op jit(solution)/shard_map/ppermute | solution.py:31
  59.6 31.4 %collective-permute-start.14 = (bf16[4,512,128]{2,1,0:T(8,128)(2,1)}, bf16[4,512,128]{2,1,0:T(8,128)(2,1)S(1)}, u32[]{:S(2)}, u32[]{:S(2)}) collective-permute-start(bf16[4,512,128]{2,1,0:T(8,128)(2,1)} %copy-done.11), channel_id=1, source_target_pairs={{0,96},{1,33},{2,98},{3,35},{4,100},{5,37},{6,102},{7,39},{8,104},... | collective-permute-start | bytes 1572872 | tf_op jit(solution)/shard_map/ppermute | solution.py:31
  59.7 32.0 %collective-permute-start.17 = (bf16[4,512,128]{2,1,0:T(8,128)(2,1)}, bf16[4,512,128]{2,1,0:T(8,128)(2,1)S(1)}, u32[]{:S(2)}, u32[]{:S(2)}) collective-permute-start(bf16[4,512,128]{2,1,0:T(8,128)(2,1)} %copy-done.10), channel_id=1, source_target_pairs={{0,24},{1,9},{2,26},{3,11},{4,28},{5,13},{6,30},{7,15},{8,0},{9,17... | collective-permute-start | bytes 1572872 | tf_op jit(solution)/shard_map/ppermute | solution.py:31
  59.9 32.7 %collective-permute-start.15 = (bf16[4,512,128]{2,1,0:T(8,128)(2,1)S(1)}, bf16[4,512,128]{2,1,0:T(8,128)(2,1)S(1)}, u32[]{:S(2)}, u32[]{:S(2)}) collective-permute-start(bf16[4,512,128]{2,1,0:T(8,128)(2,1)S(1)} %slice.32), channel_id=1, source_target_pairs={{0,32},{1,97},{2,34},{3,99},{4,36},{5,101},{6,38},{7,103},{8,40},{... | collective-permute-start | bytes 1572872 | tf_op jit(solution)/shard_map/ppermute | solution.py:31
  62.6 30.8 %collective-permute-start.18 = (bf16[4,512,128]{2,1,0:T(8,128)(2,1)S(1)}, bf16[4,512,128]{2,1,0:T(8,128)(2,1)S(1)}, u32[]{:S(2)}, u32[]{:S(2)}) collective-permute-start(bf16[4,512,128]{2,1,0:T(8,128)(2,1)S(1)} %slice.33), channel_id=1, source_target_pairs={{0,8},{1,25},{2,10},{3,27},{4,12},{5,29},{6,14},{7,31},{8,16},{9,1... | collective-permute-start | bytes 1572872 | tf_op jit(solution)/shard_map/ppermute | solution.py:31
  65.3 5.8 %copy-start.6 = (bf16[8192,1024]{1,0:T(8,128)(2,1)S(1)}, bf16[8192,1024]{1,0:T(8,128)(2,1)}, u32[]{:S(2)}) copy-start(bf16[8192,1024]{1,0:T(8,128)(2,1)} %wq_ref.1) | copy-start | bytes 50331652
  71.0 1.6 %copy-start.7 = (bf16[8192,128]{1,0:T(8,128)(2,1)S(1)}, bf16[8192,128]{1,0:T(8,128)(2,1)}, u32[]{:S(2)}) copy-start(bf16[8192,128]{1,0:T(8,128)(2,1)} %wk_hbm.1) | copy-start | bytes 6291460
  74.2 20.1 %copy-start.2 = (bf16[4,512,1,128]{3,1,2,0:T(8,128)(2,1)S(1)}, bf16[4,512,1,128]{3,1,2,0:T(8,128)(2,1)}, u32[]{:S(2)}) copy-start(bf16[4,512,1,128]{3,1,2,0:T(8,128)(2,1)} %param.15) | copy-start | bytes 1572868
  74.2 20.1 %copy-start.4 = (bf16[4,512,1,128]{3,1,2,0:T(8,128)(2,1)S(1)}, bf16[4,512,1,128]{3,1,2,0:T(8,128)(2,1)}, u32[]{:S(2)}) copy-start(bf16[4,512,1,128]{3,1,2,0:T(8,128)(2,1)} %param.16) | copy-start | bytes 1572868
  74.2 20.1 %copy-start.5 = (s32[1,384]{1,0:T(1,128)S(1)}, s32[1,384]{1,0:T(1,128)}, u32[]{:S(2)}) copy-start(s32[1,384]{1,0:T(1,128)} %npos_ref.1) | copy-start | bytes 4612
  (19 other events, 18.3 us)

commit v3 on v2

--- a/solution.py
+++ b/solution.py
@@ -31,20 +31,20 @@
     return lax.ppermute(value, ("req", "tp"), pairs)
 
 
-def way(core):
-    return 1 if core == 0 else -1
-
-
-def along_x(value, sign):
-    return move(value, lambda y, x, z, c: (y, x + sign * way(c), z, c))
-
-
-def along_y(value, sign):
-    return move(value, lambda y, x, z, c: (y + sign * way(c), x, z, c))
-
-
-def along_z(value):
-    return move(value, lambda y, x, z, c: (y, x, z + way(c), c))
+def first_axis(value, step):
+    return move(value, lambda y, x, z, c: (y, x + step, z, c) if c == 0 else (y + step, x, z, c))
+
+
+def second_axis(value, step):
+    return move(value, lambda y, x, z, c: (y + step, x, z, c) if c == 0 else (y, x + step, z, c))
+
+
+def along_z(value, step):
+    return move(value, lambda y, x, z, c: (y, x, z + step, c))
+
+
+def around_z(value):
+    return move(value, lambda y, x, z, c: (y, x, z + 1 - 2 * c, c))
 
 
 def other_core(value):
@@ -66,31 +66,37 @@
     )(tokens, gain.reshape(1, -1))
 
 
-def pick_kernel(index_ref, *refs):
-    sources, (k_fwd, k_back, v_fwd, v_back) = refs[:8], refs[8:]
-    for tensor, (fwd, back) in enumerate(((k_fwd, k_back), (v_fwd, v_back))):
+def pick_kernel(index_ref, own, before, behind, k_far, v_far, up, down):
+    sources = (own, before, behind)
+    held = k_far.shape[0]
+    for slot in range(4):
         for target in range(3):
-            for slot in range(4):
-                chosen = sources[tensor * 4 + slot][index_ref[tensor * 12 + target * 4 + slot]]
-                if target < 2:
-                    fwd[target * 4 + slot] = chosen
-                else:
-                    back[slot] = chosen
-
-
-def pick(index, keys, values):
-    _, tokens, dim = keys[0].shape
+            n = index_ref[target * 4 + slot]
+            keys = sources[slot].at[n] if slot < 3 else k_far.at[n]
+            values = sources[slot].at[held + n] if slot < 3 else v_far.at[n]
+            if target == 0:
+                up[slot] = keys[...]
+                up[4 + slot] = values[...]
+            elif target == 1:
+                up[8 + slot] = keys[...]
+                down[8 + slot] = values[...]
+            else:
+                down[slot] = keys[...]
+                down[4 + slot] = values[...]
+
+
+def pick(index, own, before, behind, k_far, v_far):
+    _, tokens, dim = own.shape
     vmem = pl.BlockSpec(memory_space=pltpu.VMEM)
-    shapes = [jax.ShapeDtypeStruct((n, tokens, dim), BF16) for n in (8, 4, 8, 4)]
     return pl.pallas_call(
         pick_kernel,
-        out_shape=shapes,
-        in_specs=[pl.BlockSpec(memory_space=pltpu.SMEM)] + [vmem] * 8,
-        out_specs=[vmem] * 4,
+        out_shape=[jax.ShapeDtypeStruct((12, tokens, dim), BF16)] * 2,
+        in_specs=[pl.BlockSpec(memory_space=pltpu.SMEM)] + [vmem] * 5,
+        out_specs=[vmem] * 2,
         compiler_params=pltpu.CompilerParams(vmem_limit_bytes=10 * MIB),
         cost_estimate=pl.CostEstimate(flops=0, bytes_accessed=6 * MIB, transcendentals=0),
         name="pick",
-    )(index, *keys, *values)
+    )(index, own, before, behind, k_far, v_far)
 
 
 def rope(values, cosine, sine):
@@ -98,12 +104,12 @@
 
 
 def project_kernel(
-    place_ref, p0, p1, p2, p3, p4, p5, p6, p7, wq_ref, wk_hbm, wv_hbm, cos_ref, sin_ref,
+    place_ref, p0, p1, p2, p3, near, remote, wq_ref, wk_hbm, wv_hbm, cos_ref, sin_ref,
     q_ref, nk_ref, nv_ref, x_buf, wk_buf, wv_buf, x_sems, w_sems,
 ):
     step = pl.program_id(0)
-    pieces = (p0, p1, p2, p3, p4, p5, p6, p7)
     rows = p0.shape[0]
+    pieces = [p0, p1, p2, p3] + [ref.at[pl.ds(n * rows, rows)] for ref in (near, remote) for n in range(ref.shape[0] // rows)]
 
     def piece_copy(n):
         at = pl.multiple_of(place_ref[n] * rows, 16)
@@ -154,7 +160,7 @@
             jax.ShapeDtypeStruct((sel, 128), BF16),
         ],
         in_specs=[pl.BlockSpec(memory_space=pltpu.SMEM)]
-        + [any_spec] * 8
+        + [any_spec] * 6
         + [pl.BlockSpec((width, 256), lambda i: (0, last(i))), any_spec, any_spec, whole, whole],
         out_specs=[pl.BlockSpec((2, sel, 128), lambda i: (last(i), 0, 0)), whole, whole],
         scratch_shapes=[
@@ -164,7 +170,7 @@
             pltpu.SemaphoreType.DMA((8,)),
             pltpu.SemaphoreType.DMA((2,)),
         ],
-        compiler_params=pltpu.CompilerParams(vmem_limit_bytes=24 * MIB),
+        compiler_params=pltpu.CompilerParams(vmem_limit_bytes=40 * MIB),
         cost_estimate=pl.CostEstimate(
             flops=2 * sel * width * 1280, bytes_accessed=30 * MIB, transcendentals=0
         ),
@@ -175,8 +181,10 @@
 def attend_kernel(
     where_ref, count_ref, q_ref, nk_ref, nv_ref, qpos_ref, kpos_ref, npos_ref, cos_ref, sin_ref, far_cos_ref, far_sin_ref, *refs
 ):
-    keys, values, out_ref = refs[:7], refs[7:14], refs[14]
-    k_buf, v_buf, nv_buf, s_buf, m_buf, acc, sems = refs[15:]
+    own, before, behind, k_far, v_far, up, down, k_last, v_last, out_ref = refs[:10]
+    k_buf, v_buf, nv_buf, s_buf, m_buf, acc, sems = refs[10:]
+    keys = (own, before, behind, k_far, up, down, k_last)
+    values = (own, before, behind, v_far, up, down, v_last)
     block = k_buf.shape[1]
     blocks = k_buf.shape[0]
     heads, sel, dim = q_ref.shape
@@ -272,9 +280,9 @@
     lax.fori_loop(0, sel // ROWS, tile, 0)
 
 
-def attend(where, count, queries, new_k, new_v, qpos, kpos, npos, angles, keys, values):
+def attend(where, count, queries, new_k, new_v, qpos, kpos, npos, angles, arrays):
     heads, sel, dim = queries.shape
-    _, block, _ = keys[0].shape
+    _, block, _ = arrays[0].shape
     blocks = kpos.shape[0]
     ctx = block * blocks
     smem = pl.BlockSpec(memory_space=pltpu.SMEM)
@@ -284,7 +292,7 @@
     return pl.pallas_call(
         attend_kernel,
         out_shape=jax.ShapeDtypeStruct((sel, heads * dim), BF16),
-        in_specs=[smem] * 2 + [vmem] * 10 + [any_spec] * 14,
+        in_specs=[smem] * 2 + [vmem] * 10 + [any_spec] * 9,
         out_specs=vmem,
         scratch_shapes=[
             pltpu.VMEM((blocks, block, dim), BF16),
@@ -300,7 +308,7 @@
             flops=4 * heads * sel * ctx * dim, bytes_accessed=8 * MIB, transcendentals=heads * sel * ctx
         ),
         name="attend",
-    )(where, count, queries, new_k, new_v, qpos, kpos, npos, *angles, *keys, *values)
+    )(where, count, queries, new_k, new_v, qpos, kpos, npos, *angles, *arrays)
 
 
 def tables(positions):
@@ -310,10 +318,8 @@
     return jnp.concatenate([cosine, cosine], axis=1), jnp.concatenate([-sine, sine], axis=1)
 
 
-def order_of(offset, sign):
-    return jnp.where(
-        offset == 0, 0, jnp.where(offset == 2, 3, jnp.where(offset == (-sign) % SIDE, 1, 2))
-    )
+def order_of(offset):
+    return jnp.where(offset == 0, 0, jnp.where(offset == 2, 3, jnp.where(offset == 3, 1, 2)))
 
 
 def on_device(
@@ -325,57 +331,51 @@
     req, tp = lax.axis_index("req"), lax.axis_index("tp")
     y, x = req // SIDE, req % SIDE
     z, core = tp // 2, tp % 2
-    sign = 1 - 2 * core
-
-    own_k = store_keys.reshape(held, block, dim)
-    own_v = store_values.reshape(held, block, dim)
-    k_one, k_two = along_x(own_k, 1), along_x(own_k, -1)
-    v_one, v_two = along_y(own_v, 1), along_y(own_v, -1)
+    own = jnp.concatenate(
+        [store_keys.reshape(held, block, dim), store_values.reshape(held, block, dim)]
+    )
+    before, behind = first_axis(own, 1), first_axis(own, -1)
     normed = normalise(tokens[0], norm_gain)
-    z_one = along_z(normed)
-    k_far, v_far = along_x(k_one, 1), along_y(v_one, 1)
-    z_two = along_z(z_one)
-    z_far = along_z(z_two)
-    mine = [normed, z_one, z_two, z_far]
-    theirs = [other_core(piece) for piece in mine]
-    row_k = [own_k, k_one, k_two, k_far]
-    column_v = [own_v, v_one, v_two, v_far]
+    z_before, z_behind = along_z(normed, 1), along_z(normed, -1)
+    k_far, v_far = first_axis(before[:held], 1), first_axis(behind[held:], -1)
+    z_far = around_z(jnp.where(core == 0, z_before, z_behind))
+    near = other_core(jnp.concatenate([normed, z_before, z_behind]))
+    remote = other_core(z_far)
 
     hot = retrieval[:, :, None] == jnp.arange(block_slot.shape[0])[None, None, :]
     slots = jnp.sum(jnp.where(hot, block_slot[None, None, :], 0), axis=2)
     at_store = (slots // held)[:, :, None] == jnp.arange(stores)[None, None, :]
     wanted = jnp.sum(jnp.where(at_store, (slots % held)[:, :, None], 0), axis=1).reshape(-1)
-    arrivals = [0, -sign, sign, 2]
-    targets = [sign, 2, -sign]
-
-    def node(yy, xx):
-        return ((yy + SIDE) % SIDE) * SIDE + (xx + SIDE) % SIDE
-
-    picks = [node(y + t, x) * stores + node(y, x + a) for t in targets for a in arrivals]
-    picks += [node(y, x + t) * stores + node(y + a, x) for t in targets for a in arrivals]
+
+    def node(first, second):
+        first, second = (first + SIDE) % SIDE, (second + SIDE) % SIDE
+        return jnp.where(core == 0, second * SIDE + first, first * SIDE + second)
+
+    first = jnp.where(core == 0, x, y)
+    second = jnp.where(core == 0, y, x)
+    picks = [
+        node(first, second + target) * stores + node(first + arrival, second)
+        for target in (1, 2, -1)
+        for arrival in (0, -1, 1, 2)
+    ]
     pick_at = jnp.stack(picks)
     entries = pick_at[:, None] == jnp.arange(requests * stores)[None, :]
     index = jnp.sum(jnp.where(entries, wanted[None, :], 0), axis=1).astype(jnp.int32)
 
-    k_fwd, k_back, v_fwd, v_back = pick(index, row_k, column_v)
-    k_fwd, k_back = along_y(k_fwd, 1), along_y(k_back, -1)
-    v_fwd, v_back = along_x(v_fwd, 1), along_x(v_back, -1)
-    k_last, v_last = along_y(k_fwd[4:], 1), along_x(v_fwd[4:], 1)
-    keys = row_k + [k_fwd, k_back, k_last]
-    values = column_v + [v_fwd, v_back, v_last]
+    up, down = pick(index, own, before, behind, k_far, v_far)
+    up, down = second_axis(up, 1), second_axis(down, -1)
+    k_last, v_last = second_axis(up[8:], 1), second_axis(down[8:], -1)
 
     own_slots = jnp.sum(jnp.where((jnp.arange(requests) == req)[:, None], slots, 0), axis=0)
     store, local = own_slots // held, own_slots % held
-    order_y = order_of((store // SIDE - y) % SIDE, sign)
-    order_x = order_of((store % SIDE - x) % SIDE, sign)
-    where = jnp.stack(
-        [
-            jnp.where(order_y == 0, order_x, 3 + order_y),
-            jnp.where(order_y == 0, local, order_x),
-            jnp.where(order_x == 0, order_y, 3 + order_x),
-            jnp.where(order_x == 0, local, order_y),
-        ]
-    ).astype(jnp.int32)
+    store_y, store_x = store // SIDE, store % SIDE
+    one = order_of((jnp.where(core == 0, store_x, store_y) - first) % SIDE)
+    two = order_of((jnp.where(core == 0, store_y, store_x) - second) % SIDE)
+    array = jnp.where(two == 0, one, 3 + two)
+    entry = jnp.where(two == 0, local, one)
+    offset = jnp.where(two == 0, held, 4)
+    shared = (array != 3) & (array != 6)
+    where = jnp.stack([array, entry, array, jnp.where(shared, entry + offset, entry)]).astype(jnp.int32)
 
     positions = sel_index[0]
     sel = positions.shape[0]
@@ -389,12 +389,13 @@
     angles = (*tables(everywhere[:block]), *tables(everywhere[::block]))
 
     place = jnp.stack(
-        [((z + s * sign + SIDE) % SIDE) * 2 + core for s in (0, -1, 2, 1)]
-        + [((z + s * sign + SIDE) % SIDE) * 2 + 1 - core for s in (0, 1, 2, -1)]
+        [((z + s + SIDE) % SIDE) * 2 + core for s in (0, -1, 1, 2)]
+        + [((z + s + SIDE) % SIDE) * 2 + 1 - core for s in (0, -1, 1, 2)]
     ).astype(jnp.int32)
-    queries, new_k, new_v = project(place, mine + theirs, w_query, w_key, w_value, q_cos, q_sin)
+    queries, new_k, new_v = project(place, [normed, z_before, z_behind, z_far, near, remote], w_query, w_key, w_value, q_cos, q_sin)
     mixed = attend(
-        where, count, queries, new_k, new_v, qpos, kpos, positions[None], angles, keys, values
+        where, count, queries, new_k, new_v, qpos, kpos, positions[None], angles,
+        [own, before, behind, k_far, v_far, up, down, k_last, v_last],
     )
     return mixed[None]
 

time: 122 us -> 101 us (0.83)
  local copies, waits for them, and re-layouts: 28.8 us -> 4.79 us
  waiting for transfers between devices: 19.2 us -> 28.5 us
  starting transfers between devices: 28.7 us -> 22 us
    unnamed x49 -> x13, local copies, waits for them, and re-layouts: 26.4 us -> 1.22 us
    ppermute x19 -> x13, waiting for transfers between devices: 19.2 us -> 28.5 us  [move(): return lax.ppermute(value, ('req', 'tp'), pairs)]
    ppermute x19 -> x13, starting transfers between devices: 28.7 us -> 22 us  [move(): return lax.ppermute(value, ('req', 'tp'), pairs)]
    concatenate x0 -> x2, other arithmetic: none -> 1.45 us  [the longest x1 1.29 us: on_device(): jnp.concatenate([store_keys.reshape(held, block, dim), store_values.resha...]
  transfers between devices with their start and end apart: 19 -> 13, of which waited for: 4 -> 4; matrix products, arithmetic and copies ran while one was open for 6% -> 8% of each run, Pallas kernels for 14% -> 16%
where the time goes in v3:
time: 101 us; the launch traced here: 99.4 us
  Pallas kernels  37.9 us (38%)
  waiting for transfers between devices  28.5 us (28%)
  starting transfers between devices  22 us (22%)
  other arithmetic  5.68 us (6%)
  local copies, waits for them, and re-layouts  4.79 us (5%)
    ppermute x13, waiting for transfers between devices, move(): return lax.ppermute(value, ('req', 'tp'), pairs)  28.5 us
    ppermute x13, starting transfers between devices, move(): return lax.ppermute(value, ('req', 'tp'), pairs)  22 us
    pallas_call x1, Pallas kernels, attend(): pl.pallas_call(attend_kernel, out_shape=jax.ShapeDtypeStruct((sel, heads...  21 us
    pallas_call x1, Pallas kernels, project(): pl.pallas_call(project_kernel, grid=(5,), out_shape=[jax.ShapeDtypeStruct...  14.6 us
    slice x2, local copies, waits for them, and re-layouts, on_device(): k_far, v_far = (first_axis(before[:held], 1), first_axis(behind[held:], -1))  2.15 us
  transfers between devices with their start and end apart: 13, of which 4 were waited for; matrix products, arithmetic and copies ran while one was open for 8% of the time, Pallas kernels for 16%

profile of v3, /device:TPU:1, one launch (start us, length us, event | category | flops | bytes accessed | tf_op | source)
XLA Modules:
  0.0 99.4 jit_solution(9129280444911967076)
XLA Ops:
  0.8 1.1 %copy-done = bf16[1,48,8192]{2,1,0:T(8,128)(2,1)S(1)} copy-done((bf16[1,48,8192]{2,1,0:T(8,128)(2,1)S(1)}, bf16[1,48,8192]{2,1,0:T(8,128)(2,1)}, u32[]{:S(2)}) %copy-start) | copy-done | bytes 786456
  2.4 2.5 %collective-permute-start = (bf16[48,8192]{1,0:T(8,128)(2,1)S(1)}, bf16[48,8192]{1,0:T(8,128)(2,1)S(1)}, u32[]{:S(2)}, u32[]{:S(2)}) collective-permute-start(bf16[48,8192]{1,0:T(8,128)(2,1)S(1)} %norm.1.p0), channel_id=1, source_target_pairs={{0,2},{1,3},{2,4},{3,5},{4,6},{5,7},{6,0},{7,1},{8,10},{9,11},{10,... | collective-permute-start | bytes 2359304 | tf_op jit(solution)/shard_map/ppermute | solution.py:31
  5.0 2.2 %collective-permute-start.1 = (bf16[48,8192]{1,0:T(8,128)(2,1)S(1)}, bf16[48,8192]{1,0:T(8,128)(2,1)S(1)}, u32[]{:S(2)}, u32[]{:S(2)}) collective-permute-start(bf16[48,8192]{1,0:T(8,128)(2,1)S(1)} %norm.1.p0), channel_id=1, source_target_pairs={{0,6},{1,7},{2,0},{3,1},{4,2},{5,3},{6,4},{7,5},{8,14},{9,15},{10,... | collective-permute-start | bytes 2359304 | tf_op jit(solution)/shard_map/ppermute | solution.py:31
  7.2 1.3 %pad_maximum_fusion.1.own.refs_0_ = bf16[8,512,128]{2,1,0:T(8,128)(2,1)S(1)} fusion(bf16[4,512,128]{2,1,0:T(8,128)(2,1)} %bitcast.66, bf16[4,512,128]{2,1,0:T(8,128)(2,1)} %bitcast.67), kind=kLoop, calls=%fused_computation.3 | loop fusion | flops 524288 | bytes 2097152 | tf_op jit(solution)/shard_map/concatenate | solution.py:334
  8.5 1.4 %collective-permute-start.5 = (bf16[8,512,128]{2,1,0:T(8,128)(2,1)S(1)}, bf16[8,512,128]{2,1,0:T(8,128)(2,1)}, u32[]{:S(2)}, u32[]{:S(2)}) collective-permute-start(bf16[8,512,128]{2,1,0:T(8,128)(2,1)S(1)} %pad_maximum_fusion.1.own.refs_0_), channel_id=1, source_target_pairs={{0,8},{1,33},{2,10},{3,35},{4,12},{5,37},{6,14},{7,39},{8,16},{9,4... | collective-permute-start | bytes 3145736 | tf_op jit(solution)/shard_map/ppermute | solution.py:31
  9.8 1.5 %collective-permute-start.6 = (bf16[8,512,128]{2,1,0:T(8,128)(2,1)S(1)}, bf16[8,512,128]{2,1,0:T(8,128)(2,1)}, u32[]{:S(2)}, u32[]{:S(2)}) collective-permute-start(bf16[8,512,128]{2,1,0:T(8,128)(2,1)S(1)} %pad_maximum_fusion.1.own.refs_0_), channel_id=1, source_target_pairs={{0,24},{1,97},{2,26},{3,99},{4,28},{5,101},{6,30},{7,103},{8,0},{9... | collective-permute-start | bytes 3145736 | tf_op jit(solution)/shard_map/ppermute | solution.py:31
  13.9 10.6 %collective-permute-done.p1 = bf16[48,8192]{1,0:T(8,128)(2,1)S(1)} collective-permute-done((bf16[48,8192]{1,0:T(8,128)(2,1)S(1)}, bf16[48,8192]{1,0:T(8,128)(2,1)S(1)}, u32[]{:S(2)}, u32[]{:S(2)}) %collective-permute-start) | collective-permute-done | bytes 786464 | tf_op jit(solution)/shard_map/ppermute | solution.py:31
  24.6 1.2 %collective-permute-start.3 = (bf16[144,8192]{1,0:T(8,128)(2,1)S(1)}, bf16[144,8192]{1,0:T(8,128)(2,1)S(1)}, u32[]{:S(2)}, u32[]{:S(2)}) collective-permute-start(bf16[144,8192]{1,0:T(8,128)(2,1)S(1)} %pad_maximum_fusion), channel_id=1, source_target_pairs={{0,1},{1,0},{2,3},{3,2},{4,5},{5,4},{6,7},{7,6},{8,9},{9,8},{10,11... | collective-permute-start | bytes 7077896 | tf_op jit(solution)/shard_map/ppermute | solution.py:31
  25.8 1.1 %slice.40 = bf16[4,512,128]{2,1,0:T(8,128)(2,1)S(1)} slice(bf16[8,512,128]{2,1,0:T(8,128)(2,1)} %collective-permute-done.5.before.refs_1_), slice={[0:4], [0:512], [0:128]} | slice | bytes 1048576 | tf_op jit(solution)/shard_map/slice | solution.py:340
  26.9 1.4 %collective-permute-start.7 = (bf16[4,512,128]{2,1,0:T(8,128)(2,1)S(1)}, bf16[4,512,128]{2,1,0:T(8,128)(2,1)S(1)}, u32[]{:S(2)}, u32[]{:S(2)}) collective-permute-start(bf16[4,512,128]{2,1,0:T(8,128)(2,1)S(1)} %slice.40), channel_id=1, source_target_pairs={{0,8},{1,33},{2,10},{3,35},{4,12},{5,37},{6,14},{7,39},{8,16},{9,4... | collective-permute-start | bytes 1572872 | tf_op jit(solution)/shard_map/ppermute | solution.py:31
  28.3 1.1 %slice.41 = bf16[4,512,128]{2,1,0:T(8,128)(2,1)S(1)} slice(bf16[8,512,128]{2,1,0:T(8,128)(2,1)} %collective-permute-done.6.behind.refs_2_), slice={[4:8], [0:512], [0:128]} | slice | bytes 1048576 | tf_op jit(solution)/shard_map/slice | solution.py:340
  29.4 1.5 %collective-permute-start.8 = (bf16[4,512,128]{2,1,0:T(8,128)(2,1)S(1)}, bf16[4,512,128]{2,1,0:T(8,128)(2,1)S(1)}, u32[]{:S(2)}, u32[]{:S(2)}) collective-permute-start(bf16[4,512,128]{2,1,0:T(8,128)(2,1)S(1)} %slice.41), channel_id=1, source_target_pairs={{0,24},{1,97},{2,26},{3,99},{4,28},{5,101},{6,30},{7,103},{8,0},{9... | collective-permute-start | bytes 1572872 | tf_op jit(solution)/shard_map/ppermute | solution.py:31
  31.0 2.8 %collective-permute-start.2 = (bf16[48,8192]{1,0:T(8,128)(2,1)S(1)}, bf16[48,8192]{1,0:T(8,128)(2,1)S(1)}, u32[]{:S(2)}, u32[]{:S(2)}) collective-permute-start(bf16[48,8192]{1,0:T(8,128)(2,1)S(1)} %broadcast_select_fusion), channel_id=1, source_target_pairs={{0,2},{1,7},{2,4},{3,1},{4,6},{5,3},{6,0},{7,5},{8,10},{9,15},{10,... | collective-permute-start | bytes 2359304 | tf_op jit(solution)/shard_map/ppermute | solution.py:31
  33.8 2.8 %collective-permute-done.7.k_far.refs_3_ = bf16[4,512,128]{2,1,0:T(8,128)(2,1)S(1)} collective-permute-done((bf16[4,512,128]{2,1,0:T(8,128)(2,1)S(1)}, bf16[4,512,128]{2,1,0:T(8,128)(2,1)S(1)}, u32[]{:S(2)}, u32[]{:S(2)}) %collective-permute-start.7) | collective-permute-done | bytes 524320 | tf_op jit(solution)/shard_map/ppermute | solution.py:31
  36.6 1.2 %collective-permute-done.8.v_far.refs_4_ = bf16[4,512,128]{2,1,0:T(8,128)(2,1)S(1)} collective-permute-done((bf16[4,512,128]{2,1,0:T(8,128)(2,1)S(1)}, bf16[4,512,128]{2,1,0:T(8,128)(2,1)S(1)}, u32[]{:S(2)}, u32[]{:S(2)}) %collective-permute-start.8) | collective-permute-done | bytes 524320 | tf_op jit(solution)/shard_map/ppermute | solution.py:31
  37.8 1.8 %pick.1 = (bf16[12,512,128]{2,1,0:T(8,128)(2,1)S(1)}, bf16[12,512,128]{2,1,0:T(8,128)(2,1)S(1)}) custom-call(s32[12]{0:T(128)S(1)} %select_reduce_fusion.2.index_ref, bf16[8,512,128]{2,1,0:T(8,128)(2,1)S(1)} %pad_maximum_fusion.1.own.refs_0_, bf16[8,512,128]{2,1,0:T(8,128)(2,1)} %collective-permute-done.5.before.refs_1_, ...), custom_call_target="tpu_custom_call" | custom-call | bytes 6291456 | tf_op jit(solution)/shard_map/pick/pallas_call | solution.py:91
  39.5 1.3 %collective-permute-start.9 = (bf16[12,512,128]{2,1,0:T(8,128)(2,1)S(1)}, bf16[12,512,128]{2,1,0:T(8,128)(2,1)S(1)}, u32[]{:S(2)}, u32[]{:S(2)}) collective-permute-start(bf16[12,512,128]{2,1,0:T(8,128)(2,1)S(1)} %get-tuple-element.13), channel_id=1, source_target_pairs={{0,32},{1,9},{2,34},{3,11},{4,36},{5,13},{6,38},{7,15},{8,40},{9,1... | collective-permute-start | bytes 4718600 | tf_op jit(solution)/shard_map/ppermute | solution.py:31
  40.8 1.5 %collective-permute-start.10 = (bf16[12,512,128]{2,1,0:T(8,128)(2,1)S(1)}, bf16[12,512,128]{2,1,0:T(8,128)(2,1)S(1)}, u32[]{:S(2)}, u32[]{:S(2)}) collective-permute-start(bf16[12,512,128]{2,1,0:T(8,128)(2,1)S(1)} %get-tuple-element.14), channel_id=1, source_target_pairs={{0,96},{1,25},{2,98},{3,27},{4,100},{5,29},{6,102},{7,31},{8,104},... | collective-permute-start | bytes 4718600 | tf_op jit(solution)/shard_map/ppermute | solution.py:31
  43.5 1.7 %collective-permute-start.4 = (bf16[48,8192]{1,0:T(8,128)(2,1)S(1)}, bf16[48,8192]{1,0:T(8,128)(2,1)S(1)}, u32[]{:S(2)}, u32[]{:S(2)}) collective-permute-start(bf16[48,8192]{1,0:T(8,128)(2,1)S(1)} %collective-permute-done.2.p3), channel_id=1, source_target_pairs={{0,1},{1,0},{2,3},{3,2},{4,5},{5,4},{6,7},{7,6},{8,9},{9,8},{10,11... | collective-permute-start | bytes 2359304 | tf_op jit(solution)/shard_map/ppermute | solution.py:31
  45.2 1.0 fusion.1
  46.4 14.0 %collective-permute-done.9.refs_5_ = bf16[12,512,128]{2,1,0:T(8,128)(2,1)S(1)} collective-permute-done((bf16[12,512,128]{2,1,0:T(8,128)(2,1)S(1)}, bf16[12,512,128]{2,1,0:T(8,128)(2,1)S(1)}, u32[]{:S(2)}, u32[]{:S(2)}) %collective-permute-start.9) | collective-permute-done | bytes 1572896 | tf_op jit(solution)/shard_map/ppermute | solution.py:31
  60.5 2.9 %collective-permute-start.12 = (bf16[4,512,128]{2,1,0:T(8,128)(2,1)S(1)}, bf16[4,512,128]{2,1,0:T(8,128)(2,1)S(1)}, u32[]{:S(2)}, u32[]{:S(2)}) collective-permute-start(bf16[4,512,128]{2,1,0:T(8,128)(2,1)S(1)} %slice.43), channel_id=1, source_target_pairs={{0,96},{1,25},{2,98},{3,27},{4,100},{5,29},{6,102},{7,31},{8,104},... | collective-permute-start | bytes 1572872 | tf_op jit(solution)/shard_map/ppermute | solution.py:31
  63.5 14.6 %project.1 = (bf16[8,384,128]{2,1,0:T(8,128)(2,1)S(1)}, bf16[384,128]{1,0:T(8,128)(2,1)S(1)}, bf16[384,128]{1,0:T(8,128)(2,1)S(1)}) custom-call(s32[8]{0:T(128)S(1)} %stack.82.place_ref, bf16[48,8192]{1,0:T(8,128)(2,1)S(1)} %norm.1.p0, bf16[48,8192]{1,0:T(8,128)(2,1)S(1)} %collective-permute-done.p1, bf16[48,8192]{1,0:T(8,128)(2,1)S(1)} %collective-permute-done.1.p2, ...), custom_call_target="tpu_custom_call" | custom-call | flops 8053063680 | bytes 31457280 | tf_op jit(solution)/shard_map/project/pallas_call | solution.py:154
  78.2 21.0 %attend.1 = bf16[384,1024]{1,0:T(8,128)(2,1)} custom-call(s32[4,8]{1,0:T(4,128)S(1)} %pad_add_fusion.where_ref, s32[3]{0:T(128)S(1)} %fusion.10.count_ref, bf16[8,384,128]{2,1,0:T(8,128)(2,1)S(1)} %get-tuple-element.10.q_ref, bf16[384,128]{1,0:T(8,128)(2,1)S(1)} %get-tuple-element.11.nk_ref, bf16[384,128]{1,0:T(8,128)(2,1)S(1)} %get-tuple-element.12.nv_ref, ...), custom_call_target="tpu_custom_call" | custom-call | flops 6442450944 | bytes 8388608 | tf_op jit(solution)/shard_map/attend/pallas_call | solution.py:292
  (56 shorter events, 5.5 us)
Async XLA Ops:
  0.0 11.4 %copy-start.1 = (s32[1,384]{1,0:T(1,128)S(1)}, s32[1,384]{1,0:T(1,128)}, u32[]{:S(2)}) copy-start(s32[1,384]{1,0:T(1,128)} %npos_ref.1) | copy-start | bytes 4612
  0.0 11.6 %copy-start.4 = (s32[16,8]{0,1:T(8,128)S(1)}, s32[16,8]{0,1:T(8,128)}, u32[]{:S(2)}) copy-start(s32[16,8]{0,1:T(8,128)} %param.18) | copy-start | bytes 1540
  0.0 11.7 %copy-start.5 = (s32[64]{0:T(128)S(1)}, s32[64]{0:T(128)}, u32[]{:S(2)}) copy-start(s32[64]{0:T(128)} %param.17) | copy-start | bytes 772
  0.8 1.1 %copy-start = (bf16[1,48,8192]{2,1,0:T(8,128)(2,1)S(1)}, bf16[1,48,8192]{2,1,0:T(8,128)(2,1)}, u32[]{:S(2)}) copy-start(bf16[1,48,8192]{2,1,0:T(8,128)(2,1)} %param.10) | copy-start | bytes 2359300
  2.4 22.0 %collective-permute-start = (bf16[48,8192]{1,0:T(8,128)(2,1)S(1)}, bf16[48,8192]{1,0:T(8,128)(2,1)S(1)}, u32[]{:S(2)}, u32[]{:S(2)}) collective-permute-start(bf16[48,8192]{1,0:T(8,128)(2,1)S(1)} %norm.1.p0), channel_id=1, source_target_pairs={{0,2},{1,3},{2,4},{3,5},{4,6},{5,7},{6,0},{7,1},{8,10},{9,11},{10,... | collective-permute-start | bytes 2359304 | tf_op jit(solution)/shard_map/ppermute | solution.py:31
  5.0 19.5 %collective-permute-start.1 = (bf16[48,8192]{1,0:T(8,128)(2,1)S(1)}, bf16[48,8192]{1,0:T(8,128)(2,1)S(1)}, u32[]{:S(2)}, u32[]{:S(2)}) collective-permute-start(bf16[48,8192]{1,0:T(8,128)(2,1)S(1)} %norm.1.p0), channel_id=1, source_target_pairs={{0,6},{1,7},{2,0},{3,1},{4,2},{5,3},{6,4},{7,5},{8,14},{9,15},{10,... | collective-permute-start | bytes 2359304 | tf_op jit(solution)/shard_map/ppermute | solution.py:31
  8.5 17.4 %collective-permute-start.5 = (bf16[8,512,128]{2,1,0:T(8,128)(2,1)S(1)}, bf16[8,512,128]{2,1,0:T(8,128)(2,1)}, u32[]{:S(2)}, u32[]{:S(2)}) collective-permute-start(bf16[8,512,128]{2,1,0:T(8,128)(2,1)S(1)} %pad_maximum_fusion.1.own.refs_0_), channel_id=1, source_target_pairs={{0,8},{1,33},{2,10},{3,35},{4,12},{5,37},{6,14},{7,39},{8,16},{9,4... | collective-permute-start | bytes 3145736 | tf_op jit(solution)/shard_map/ppermute | solution.py:31
  9.8 18.5 %collective-permute-start.6 = (bf16[8,512,128]{2,1,0:T(8,128)(2,1)S(1)}, bf16[8,512,128]{2,1,0:T(8,128)(2,1)}, u32[]{:S(2)}, u32[]{:S(2)}) collective-permute-start(bf16[8,512,128]{2,1,0:T(8,128)(2,1)S(1)} %pad_maximum_fusion.1.own.refs_0_), channel_id=1, source_target_pairs={{0,24},{1,97},{2,26},{3,99},{4,28},{5,101},{6,30},{7,103},{8,0},{9... | collective-permute-start | bytes 3145736 | tf_op jit(solution)/shard_map/ppermute | solution.py:31
  24.6 38.8 %collective-permute-start.3 = (bf16[144,8192]{1,0:T(8,128)(2,1)S(1)}, bf16[144,8192]{1,0:T(8,128)(2,1)S(1)}, u32[]{:S(2)}, u32[]{:S(2)}) collective-permute-start(bf16[144,8192]{1,0:T(8,128)(2,1)S(1)} %pad_maximum_fusion), channel_id=1, source_target_pairs={{0,1},{1,0},{2,3},{3,2},{4,5},{5,4},{6,7},{7,6},{8,9},{9,8},{10,11... | collective-permute-start | bytes 7077896 | tf_op jit(solution)/shard_map/ppermute | solution.py:31
  26.9 9.7 %collective-permute-start.7 = (bf16[4,512,128]{2,1,0:T(8,128)(2,1)S(1)}, bf16[4,512,128]{2,1,0:T(8,128)(2,1)S(1)}, u32[]{:S(2)}, u32[]{:S(2)}) collective-permute-start(bf16[4,512,128]{2,1,0:T(8,128)(2,1)S(1)} %slice.40), channel_id=1, source_target_pairs={{0,8},{1,33},{2,10},{3,35},{4,12},{5,37},{6,14},{7,39},{8,16},{9,4... | collective-permute-start | bytes 1572872 | tf_op jit(solution)/shard_map/ppermute | solution.py:31
  29.4 8.4 %collective-permute-start.8 = (bf16[4,512,128]{2,1,0:T(8,128)(2,1)S(1)}, bf16[4,512,128]{2,1,0:T(8,128)(2,1)S(1)}, u32[]{:S(2)}, u32[]{:S(2)}) collective-permute-start(bf16[4,512,128]{2,1,0:T(8,128)(2,1)S(1)} %slice.41), channel_id=1, source_target_pairs={{0,24},{1,97},{2,26},{3,99},{4,28},{5,101},{6,30},{7,103},{8,0},{9... | collective-permute-start | bytes 1572872 | tf_op jit(solution)/shard_map/ppermute | solution.py:31
  31.0 12.5 %collective-permute-start.2 = (bf16[48,8192]{1,0:T(8,128)(2,1)S(1)}, bf16[48,8192]{1,0:T(8,128)(2,1)S(1)}, u32[]{:S(2)}, u32[]{:S(2)}) collective-permute-start(bf16[48,8192]{1,0:T(8,128)(2,1)S(1)} %broadcast_select_fusion), channel_id=1, source_target_pairs={{0,2},{1,7},{2,4},{3,1},{4,6},{5,3},{6,0},{7,5},{8,10},{9,15},{10,... | collective-permute-start | bytes 2359304 | tf_op jit(solution)/shard_map/ppermute | solution.py:31
  39.5 20.8 %collective-permute-start.9 = (bf16[12,512,128]{2,1,0:T(8,128)(2,1)S(1)}, bf16[12,512,128]{2,1,0:T(8,128)(2,1)S(1)}, u32[]{:S(2)}, u32[]{:S(2)}) collective-permute-start(bf16[12,512,128]{2,1,0:T(8,128)(2,1)S(1)} %get-tuple-element.13), channel_id=1, source_target_pairs={{0,32},{1,9},{2,34},{3,11},{4,36},{5,13},{6,38},{7,15},{8,40},{9,1... | collective-permute-start | bytes 4718600 | tf_op jit(solution)/shard_map/ppermute | solution.py:31
  40.8 19.7 %collective-permute-start.10 = (bf16[12,512,128]{2,1,0:T(8,128)(2,1)S(1)}, bf16[12,512,128]{2,1,0:T(8,128)(2,1)S(1)}, u32[]{:S(2)}, u32[]{:S(2)}) collective-permute-start(bf16[12,512,128]{2,1,0:T(8,128)(2,1)S(1)} %get-tuple-element.14), channel_id=1, source_target_pairs={{0,96},{1,25},{2,98},{3,27},{4,100},{5,29},{6,102},{7,31},{8,104},... | collective-permute-start | bytes 4718600 | tf_op jit(solution)/shard_map/ppermute | solution.py:31
  43.4 20.0 %copy-start.2 = (bf16[8192,128]{1,0:T(8,128)(2,1)S(1)}, bf16[8192,128]{1,0:T(8,128)(2,1)}, u32[]{:S(2)}) copy-start(bf16[8192,128]{1,0:T(8,128)(2,1)} %wk_hbm.1) | copy-start | bytes 6291460
  43.4 20.0 %copy-start.3 = (bf16[8192,128]{1,0:T(8,128)(2,1)S(1)}, bf16[8192,128]{1,0:T(8,128)(2,1)}, u32[]{:S(2)}) copy-start(bf16[8192,128]{1,0:T(8,128)(2,1)} %wv_hbm.1) | copy-start | bytes 6291460
  43.5 20.0 %collective-permute-start.4 = (bf16[48,8192]{1,0:T(8,128)(2,1)S(1)}, bf16[48,8192]{1,0:T(8,128)(2,1)S(1)}, u32[]{:S(2)}, u32[]{:S(2)}) collective-permute-start(bf16[48,8192]{1,0:T(8,128)(2,1)S(1)} %collective-permute-done.2.p3), channel_id=1, source_target_pairs={{0,1},{1,0},{2,3},{3,2},{4,5},{5,4},{6,7},{7,6},{8,9},{9,8},{10,11... | collective-permute-start | bytes 2359304 | tf_op jit(solution)/shard_map/ppermute | solution.py:31
  60.4 17.7 %collective-permute-start.11 = (bf16[4,512,128]{2,1,0:T(8,128)(2,1)S(1)}, bf16[4,512,128]{2,1,0:T(8,128)(2,1)S(1)}, u32[]{:S(2)}, u32[]{:S(2)}) collective-permute-start(bf16[4,512,128]{2,1,0:T(8,128)(2,1)S(1)} %slice.42), channel_id=1, source_target_pairs={{0,32},{1,9},{2,34},{3,11},{4,36},{5,13},{6,38},{7,15},{8,40},{9,1... | collective-permute-start | bytes 1572872 | tf_op jit(solution)/shard_map/ppermute | solution.py:31
  60.5 17.5 %collective-permute-start.12 = (bf16[4,512,128]{2,1,0:T(8,128)(2,1)S(1)}, bf16[4,512,128]{2,1,0:T(8,128)(2,1)S(1)}, u32[]{:S(2)}, u32[]{:S(2)}) collective-permute-start(bf16[4,512,128]{2,1,0:T(8,128)(2,1)S(1)} %slice.43), channel_id=1, source_target_pairs={{0,96},{1,25},{2,98},{3,27},{4,100},{5,29},{6,102},{7,31},{8,104},... | collective-permute-start | bytes 1572872 | tf_op jit(solution)/shard_map/ppermute | solution.py:31

commit v4 on v3

--- a/solution.py
+++ b/solution.py
@@ -51,19 +51,22 @@
     return move(value, lambda y, x, z, c: (y, x, z, 1 - c))
 
 
-def norm_kernel(tokens_ref, gain_ref, out_ref):
+def norm_kernel(tokens_ref, gain_ref, first_ref, out_ref):
     hidden = tokens_ref[...].astype(F32)
     scale = lax.rsqrt(jnp.mean(hidden * hidden, axis=-1, keepdims=True) + EPS)
     out_ref[...] = (hidden * scale * gain_ref[...].astype(F32)).astype(BF16)
 
 
-def normalise(tokens, gain):
+def normalise(tokens, gain, first):
+    vmem = pl.BlockSpec(memory_space=pltpu.VMEM)
     return pl.pallas_call(
         norm_kernel,
         out_shape=jax.ShapeDtypeStruct(tokens.shape, BF16),
+        in_specs=[vmem, vmem, pl.BlockSpec(memory_space=pl.ANY)],
+        out_specs=vmem,
         compiler_params=pltpu.CompilerParams(vmem_limit_bytes=8 * MIB),
         name="norm",
-    )(tokens, gain.reshape(1, -1))
+    )(tokens, gain.reshape(1, -1), first)
 
 
 def pick_kernel(index_ref, own, before, behind, k_far, v_far, up, down):
@@ -103,91 +106,93 @@
     return values * cosine + pltpu.roll(values, 64, 1) * sine
 
 
-def project_kernel(
-    place_ref, p0, p1, p2, p3, near, remote, wq_ref, wk_hbm, wv_hbm, cos_ref, sin_ref,
-    q_ref, nk_ref, nv_ref, x_buf, wk_buf, wv_buf, x_sems, w_sems,
-):
+def project_kernel(with_kv, *refs):
+    place_ref, p0, p1, p2, p3, near, remote = refs[:7]
+    if with_kv:
+        wq_ref, wk_hbm, wv_hbm, cos_ref, sin_ref, q_ref, nk_ref, nv_ref = refs[7:15]
+        x_buf, x_sems, wk_buf, wv_buf, w_sems = refs[15:]
+        k_copy = pltpu.make_async_copy(wk_hbm, wk_buf, w_sems.at[0])
+        v_copy = pltpu.make_async_copy(wv_hbm, wv_buf, w_sems.at[1])
+    else:
+        wq_ref, cos_ref, sin_ref, q_ref, x_buf, x_sems = refs[7:]
     step = pl.program_id(0)
     rows = p0.shape[0]
-    pieces = [p0, p1, p2, p3] + [ref.at[pl.ds(n * rows, rows)] for ref in (near, remote) for n in range(ref.shape[0] // rows)]
+    pieces = [p0, p1, p2, p3]
+    pieces += [ref.at[pl.ds(n * rows, rows)] for ref in (near, remote) for n in range(ref.shape[0] // rows)]
 
     def piece_copy(n):
         at = pl.multiple_of(place_ref[n] * rows, 16)
         return pltpu.make_async_copy(pieces[n], x_buf.at[pl.ds(at, rows)], x_sems.at[n])
-
-    k_copy = pltpu.make_async_copy(wk_hbm, wk_buf, w_sems.at[0])
-    v_copy = pltpu.make_async_copy(wv_hbm, wv_buf, w_sems.at[1])
 
     @pl.when(step == 0)
     def _():
         for n in range(8):
             piece_copy(n).start()
-        k_copy.start()
-        v_copy.start()
+        if with_kv:
+            k_copy.start()
+            v_copy.start()
         for n in range(8):
             piece_copy(n).wait()
 
     cosine = cos_ref[...]
     sine = sin_ref[...]
 
-    @pl.when(step < 4)
+    @pl.when(step < 2)
     def _():
         raw = jnp.dot(x_buf[...], wq_ref[...], preferred_element_type=F32)
         for h in range(2):
             q_ref[h] = rope(raw[:, h * 128 : (h + 1) * 128], cosine, sine).astype(BF16)
 
-    @pl.when(step == 4)
-    def _():
-        k_copy.wait()
-        v_copy.wait()
-        new_k = jnp.dot(x_buf[...], wk_buf[...], preferred_element_type=F32).astype(BF16)
-        nk_ref[...] = rope(new_k.astype(F32), cosine, sine).astype(BF16)
-        nv_ref[...] = jnp.dot(x_buf[...], wv_buf[...], preferred_element_type=F32).astype(BF16)
-
-
-def project(place, pieces, w_query, w_key, w_value, cosine, sine):
+    if with_kv:
+
+        @pl.when(step == 2)
+        def _():
+            k_copy.wait()
+            v_copy.wait()
+            new_k = jnp.dot(x_buf[...], wk_buf[...], preferred_element_type=F32).astype(BF16)
+            nk_ref[...] = rope(new_k.astype(F32), cosine, sine).astype(BF16)
+            nv_ref[...] = jnp.dot(x_buf[...], wv_buf[...], preferred_element_type=F32).astype(BF16)
+
+
+def project(place, pieces, half, w_query, w_kv, cosine, sine):
     rows, width = pieces[0].shape
     sel = 8 * rows
     any_spec = pl.BlockSpec(memory_space=pl.ANY)
     whole = pl.BlockSpec((sel, 128), lambda i: (0, 0))
-    last = lambda i: jnp.minimum(i, 3)
+    last = lambda i: jnp.minimum(i, 1)
+    new = [jax.ShapeDtypeStruct((sel, 128), BF16)] * len(w_kv)
+    scratch = [pltpu.VMEM((sel, width), BF16), pltpu.SemaphoreType.DMA((8,))]
+    if w_kv:
+        scratch += [pltpu.VMEM((width, 128), BF16)] * 2 + [pltpu.SemaphoreType.DMA((2,))]
     return pl.pallas_call(
-        project_kernel,
-        grid=(5,),
-        out_shape=[
-            jax.ShapeDtypeStruct((8, sel, 128), BF16),
-            jax.ShapeDtypeStruct((sel, 128), BF16),
-            jax.ShapeDtypeStruct((sel, 128), BF16),
-        ],
+        functools.partial(project_kernel, bool(w_kv)),
+        grid=(3 if w_kv else 2,),
+        out_shape=[jax.ShapeDtypeStruct((4, sel, 128), BF16)] + new,
         in_specs=[pl.BlockSpec(memory_space=pltpu.SMEM)]
         + [any_spec] * 6
-        + [pl.BlockSpec((width, 256), lambda i: (0, last(i))), any_spec, any_spec, whole, whole],
-        out_specs=[pl.BlockSpec((2, sel, 128), lambda i: (last(i), 0, 0)), whole, whole],
-        scratch_shapes=[
-            pltpu.VMEM((sel, width), BF16),
-            pltpu.VMEM((width, 128), BF16),
-            pltpu.VMEM((width, 128), BF16),
-            pltpu.SemaphoreType.DMA((8,)),
-            pltpu.SemaphoreType.DMA((2,)),
-        ],
+        + [pl.BlockSpec((width, 256), lambda i: (0, 2 * half + last(i)))]
+        + [any_spec] * len(w_kv)
+        + [whole, whole],
+        out_specs=[pl.BlockSpec((2, sel, 128), lambda i: (last(i), 0, 0))] + [whole] * len(w_kv),
+        scratch_shapes=scratch,
         compiler_params=pltpu.CompilerParams(vmem_limit_bytes=40 * MIB),
         cost_estimate=pl.CostEstimate(
-            flops=2 * sel * width * 1280, bytes_accessed=30 * MIB, transcendentals=0
+            flops=0, bytes_accessed=MIB, transcendentals=0
         ),
         name="project",
-    )(place, *pieces, w_query, w_key, w_value, cosine, sine)
+    )(place, *pieces, w_query, *w_kv, cosine, sine)
 
 
 def attend_kernel(
-    where_ref, count_ref, q_ref, nk_ref, nv_ref, qpos_ref, kpos_ref, npos_ref, cos_ref, sin_ref, far_cos_ref, far_sin_ref, *refs
+    where_ref, count_ref, low_ref, high_ref, nk_ref, nv_ref, qpos_ref, kpos_ref, npos_ref, cos_ref, sin_ref, far_cos_ref, far_sin_ref, *refs
 ):
     own, before, behind, k_far, v_far, up, down, k_last, v_last, out_ref = refs[:10]
-    k_buf, v_buf, nv_buf, s_buf, m_buf, acc, sems = refs[10:]
+    k_buf, v_buf, nv_buf, q_buf, s_buf, m_buf, acc, sems = refs[10:]
     keys = (own, before, behind, k_far, up, down, k_last)
     values = (own, before, behind, v_far, up, down, v_last)
     block = k_buf.shape[1]
     blocks = k_buf.shape[0]
-    heads, sel, dim = q_ref.shape
+    heads, sel, dim = 2 * low_ref.shape[0], *low_ref.shape[1:]
     ctx = block * blocks
     tall = heads * ROWS
     factor = 1.4426950408889634 / (dim ** 0.5)
@@ -238,7 +243,10 @@
 
     def tile(i, carry):
         rows = pl.ds(pl.multiple_of(i * ROWS, ROWS), ROWS)
-        queries = q_ref[:, rows, :].reshape(tall, dim)
+        half = tall // 2
+        q_buf[:half] = low_ref[:, rows, :].reshape(half, dim)
+        q_buf[half:] = high_ref[:, rows, :].reshape(half, dim)
+        queries = q_buf[...]
         query_pos = qpos_ref[rows, :]
         scores, most = masked_scores(queries, nk_ref[...], npos_ref[...], query_pos)
         s_buf[:, ctx:] = scores
@@ -248,7 +256,7 @@
 
         def first(j, carry):
             scores, most = masked_scores(
-                q_ref[:, rows, :].reshape(tall, dim),
+                q_buf[...],
                 k_buf[pl.ds(j * STEP, STEP)].reshape(span, dim),
                 jnp.concatenate([kpos_ref[pl.ds(j * STEP + n, 1), :] for n in range(STEP)], axis=1),
                 qpos_ref[rows, :],
@@ -280,8 +288,8 @@
     lax.fori_loop(0, sel // ROWS, tile, 0)
 
 
-def attend(where, count, queries, new_k, new_v, qpos, kpos, npos, angles, arrays):
-    heads, sel, dim = queries.shape
+def attend(where, count, low, high, new_k, new_v, qpos, kpos, npos, angles, arrays):
+    heads, sel, dim = 2 * low.shape[0], *low.shape[1:]
     _, block, _ = arrays[0].shape
     blocks = kpos.shape[0]
     ctx = block * blocks
@@ -292,12 +300,13 @@
     return pl.pallas_call(
         attend_kernel,
         out_shape=jax.ShapeDtypeStruct((sel, heads * dim), BF16),
-        in_specs=[smem] * 2 + [vmem] * 10 + [any_spec] * 9,
+        in_specs=[smem] * 2 + [vmem] * 11 + [any_spec] * 9,
         out_specs=vmem,
         scratch_shapes=[
             pltpu.VMEM((blocks, block, dim), BF16),
             pltpu.VMEM((ctx, 2 * dim), BF16),
             pltpu.VMEM((sel, 2 * dim), BF16),
+            pltpu.VMEM((tall, dim), BF16),
             pltpu.VMEM((tall, ctx + sel), F32),
             pltpu.VMEM((tall, 128), F32),
             pltpu.VMEM((tall, 2 * dim), F32),
@@ -308,7 +317,7 @@
             flops=4 * heads * sel * ctx * dim, bytes_accessed=8 * MIB, transcendentals=heads * sel * ctx
         ),
         name="attend",
-    )(where, count, queries, new_k, new_v, qpos, kpos, npos, *angles, *arrays)
+    )(where, count, low, high, new_k, new_v, qpos, kpos, npos, *angles, *arrays)
 
 
 def tables(positions):
@@ -335,9 +344,11 @@
         [store_keys.reshape(held, block, dim), store_values.reshape(held, block, dim)]
     )
     before, behind = first_axis(own, 1), first_axis(own, -1)
-    normed = normalise(tokens[0], norm_gain)
+    normed = normalise(tokens[0], norm_gain, own)
     z_before, z_behind = along_z(normed, 1), along_z(normed, -1)
-    k_far, v_far = first_axis(before[:held], 1), first_axis(behind[held:], -1)
+    k_half, v_half = before[:held], behind[held:]
+    k_far, v_far = first_axis(k_half, 1), first_axis(v_half, -1)
+    z_before, z_behind, _, _ = lax.optimization_barrier((z_before, z_behind, k_half, v_half))
     z_far = around_z(jnp.where(core == 0, z_before, z_behind))
     near = other_core(jnp.concatenate([normed, z_before, z_behind]))
     remote = other_core(z_far)
@@ -364,7 +375,6 @@
 
     up, down = pick(index, own, before, behind, k_far, v_far)
     up, down = second_axis(up, 1), second_axis(down, -1)
-    k_last, v_last = second_axis(up[8:], 1), second_axis(down[8:], -1)
 
     own_slots = jnp.sum(jnp.where((jnp.arange(requests) == req)[:, None], slots, 0), axis=0)
     store, local = own_slots // held, own_slots % held
@@ -392,9 +402,13 @@
         [((z + s + SIDE) % SIDE) * 2 + core for s in (0, -1, 1, 2)]
         + [((z + s + SIDE) % SIDE) * 2 + 1 - core for s in (0, -1, 1, 2)]
     ).astype(jnp.int32)
-    queries, new_k, new_v = project(place, [normed, z_before, z_behind, z_far, near, remote], w_query, w_key, w_value, q_cos, q_sin)
+    pieces = [normed, z_before, z_behind, z_far, near, remote]
+    low, new_k, new_v = project(place, pieces, 0, w_query, (w_key, w_value), q_cos, q_sin)
+    up_first, down_first, _ = lax.optimization_barrier((up, down, low))
+    k_last, v_last = second_axis(up_first[8:], 1), second_axis(down_first[8:], -1)
+    (high,) = project(place, pieces, 1, w_query, (), q_cos, q_sin)
     mixed = attend(
-        where, count, queries, new_k, new_v, qpos, kpos, positions[None], angles,
+        where, count, low, high, new_k, new_v, qpos, kpos, positions[None], angles,
         [own, before, behind, k_far, v_far, up, down, k_last, v_last],
     )
     return mixed[None]

time: 101 us -> 95.5 us (0.946)
  waiting for transfers between devices: 28.5 us -> 11.4 us
  Pallas kernels: 37.9 us -> 45.1 us
  local copies, waits for them, and re-layouts: 4.79 us -> 8.11 us
  other arithmetic: 5.68 us -> 8.06 us
    ppermute x13, waiting for transfers between devices: 28.5 us -> 11.4 us  [move(): return lax.ppermute(value, ('req', 'tp'), pairs)]
    pallas_call x1 -> x2, Pallas kernels: 14.6 us -> 20.7 us  [project(): pl.pallas_call(functools.partial(project_kernel, bool(w_kv)), grid=(3 if...]
    slice x4, local copies, waits for them, and re-layouts: 2.22 us -> 4.31 us  [the longest x2 2.15 us: on_device(): k_half, v_half = (before[:held], behind[held:])]
    pallas_call x1, Pallas kernels: 1.76 us -> 3.69 us  [pick(): pl.pallas_call(pick_kernel, out_shape=[jax.ShapeDtypeStruct((12, tokens,...]
    concatenate x1, other arithmetic: 0.16 us -> 1.58 us  [on_device(): near = other_core(jnp.concatenate([normed, z_before, z_behind]))]
    unnamed x13 -> x21, local copies, waits for them, and re-layouts: 1.22 us -> 2.51 us
  transfers between devices with their start and end apart: 13 -> 13, of which waited for: 4 -> 3; matrix products, arithmetic and copies ran while one was open for 8% -> 12% of each run, Pallas kernels for 16% -> 26%
where the time goes in v4:
time: 95.5 us; the launch traced here: 94.8 us
  Pallas kernels  45.1 us (47%)
  starting transfers between devices  21.7 us (23%)
  waiting for transfers between devices  11.4 us (12%)
  local copies, waits for them, and re-layouts  8.11 us (8%)
  other arithmetic  8.06 us (8%)
    ppermute x13, starting transfers between devices, move(): return lax.ppermute(value, ('req', 'tp'), pairs)  21.7 us
    pallas_call x2, Pallas kernels, project(): pl.pallas_call(functools.partial(project_kernel, bool(w_kv)), grid=(3 if...  20.7 us
    pallas_call x1, Pallas kernels, attend(): pl.pallas_call(attend_kernel, out_shape=jax.ShapeDtypeStruct((sel, heads...  20.2 us
    ppermute x13, waiting for transfers between devices, move(): return lax.ppermute(value, ('req', 'tp'), pairs)  11.4 us
    pallas_call x1, Pallas kernels, pick(): pl.pallas_call(pick_kernel, out_shape=[jax.ShapeDtypeStruct((12, tokens,...  3.69 us
    unnamed x21, local copies, waits for them, and re-layouts  2.51 us
    slice x2, local copies, waits for them, and re-layouts, on_device(): k_half, v_half = (before[:held], behind[held:])  2.15 us
  transfers between devices with their start and end apart: 13, of which 3 were waited for; matrix products, arithmetic and copies ran while one was open for 12% of the time, Pallas kernels for 26%

profile of v4, /device:TPU:1, one launch (start us, length us, event | category | flops | bytes accessed | tf_op | source)
XLA Modules:
  0.0 94.8 jit_solution(12160747312607706305)
XLA Ops:
  0.0 1.4 %pad_maximum_fusion.1.first_ref.own.refs_0_ = bf16[8,512,128]{2,1,0:T(8,128)(2,1)S(1)} fusion(bf16[4,512,128]{2,1,0:T(8,128)(2,1)} %bitcast.66, bf16[4,512,128]{2,1,0:T(8,128)(2,1)} %bitcast.67), kind=kLoop, calls=%fused_computation.3 | loop fusion | flops 524288 | bytes 2097152 | tf_op jit(solution)/shard_map/concatenate | solution.py:343
  1.4 2.2 %collective-permute-start.2 = (bf16[8,512,128]{2,1,0:T(8,128)(2,1)S(1)}, bf16[8,512,128]{2,1,0:T(8,128)(2,1)}, u32[]{:S(2)}, u32[]{:S(2)}) collective-permute-start(bf16[8,512,128]{2,1,0:T(8,128)(2,1)S(1)} %pad_maximum_fusion.1.first_ref.own.refs_0_), channel_id=1, source_target_pairs={{0,8},{1,33},{2,10},{3,35},{4,12},{5,37},{6,14},{7,39},{8,16},{9,4... | collective-permute-start | bytes 3145736 | tf_op jit(solution)/shard_map/ppermute | solution.py:31
  3.6 1.5 %collective-permute-start.3 = (bf16[8,512,128]{2,1,0:T(8,128)(2,1)S(1)}, bf16[8,512,128]{2,1,0:T(8,128)(2,1)}, u32[]{:S(2)}, u32[]{:S(2)}) collective-permute-start(bf16[8,512,128]{2,1,0:T(8,128)(2,1)S(1)} %pad_maximum_fusion.1.first_ref.own.refs_0_), channel_id=1, source_target_pairs={{0,24},{1,97},{2,26},{3,99},{4,28},{5,101},{6,30},{7,103},{8,0},{9... | collective-permute-start | bytes 3145736 | tf_op jit(solution)/shard_map/ppermute | solution.py:31
  6.4 1.7 %collective-permute-start = (bf16[48,8192]{1,0:T(8,128)(2,1)S(1)}, bf16[48,8192]{1,0:T(8,128)(2,1)S(1)}, u32[]{:S(2)}, u32[]{:S(2)}) collective-permute-start(bf16[48,8192]{1,0:T(8,128)(2,1)S(1)} %norm.1.refs_1_), channel_id=1, source_target_pairs={{0,2},{1,3},{2,4},{3,5},{4,6},{5,7},{6,0},{7,1},{8,10},{9,11},{10,... | collective-permute-start | bytes 2359304 | tf_op jit(solution)/shard_map/ppermute | solution.py:31
  8.1 2.2 %collective-permute-start.1 = (bf16[48,8192]{1,0:T(8,128)(2,1)S(1)}, bf16[48,8192]{1,0:T(8,128)(2,1)S(1)}, u32[]{:S(2)}, u32[]{:S(2)}) collective-permute-start(bf16[48,8192]{1,0:T(8,128)(2,1)S(1)} %norm.1.refs_1_), channel_id=1, source_target_pairs={{0,6},{1,7},{2,0},{3,1},{4,2},{5,3},{6,4},{7,5},{8,14},{9,15},{10,... | collective-permute-start | bytes 2359304 | tf_op jit(solution)/shard_map/ppermute | solution.py:31
  11.4 6.2 %collective-permute-done.2.before.refs_1_ = bf16[8,512,128]{2,1,0:T(8,128)(2,1)} collective-permute-done((bf16[8,512,128]{2,1,0:T(8,128)(2,1)S(1)}, bf16[8,512,128]{2,1,0:T(8,128)(2,1)}, u32[]{:S(2)}, u32[]{:S(2)}) %collective-permute-start.2) | collective-permute-done | bytes 1048608 | tf_op jit(solution)/shard_map/ppermute | solution.py:31
  17.6 1.1 %slice.40 = bf16[4,512,128]{2,1,0:T(8,128)(2,1)S(1)} slice(bf16[8,512,128]{2,1,0:T(8,128)(2,1)} %collective-permute-done.2.before.refs_1_), slice={[0:4], [0:512], [0:128]} | slice | bytes 1048576 | tf_op jit(solution)/shard_map/slice | solution.py:349
  18.8 1.1 %slice.41 = bf16[4,512,128]{2,1,0:T(8,128)(2,1)S(1)} slice(bf16[8,512,128]{2,1,0:T(8,128)(2,1)} %collective-permute-done.3.behind.refs_2_), slice={[4:8], [0:512], [0:128]} | slice | bytes 1048576 | tf_op jit(solution)/shard_map/slice | solution.py:349
  19.9 2.7 %collective-permute-start.8 = (bf16[4,512,128]{2,1,0:T(8,128)(2,1)S(1)}, bf16[4,512,128]{2,1,0:T(8,128)(2,1)S(1)}, u32[]{:S(2)}, u32[]{:S(2)}) collective-permute-start(bf16[4,512,128]{2,1,0:T(8,128)(2,1)S(1)} %slice.41), channel_id=1, source_target_pairs={{0,24},{1,97},{2,26},{3,99},{4,28},{5,101},{6,30},{7,103},{8,0},{9... | collective-permute-start | bytes 1572872 | tf_op jit(solution)/shard_map/ppermute | solution.py:31
  22.6 4.4 %collective-permute-done.refs_2_ = bf16[48,8192]{1,0:T(8,128)(2,1)S(1)} collective-permute-done((bf16[48,8192]{1,0:T(8,128)(2,1)S(1)}, bf16[48,8192]{1,0:T(8,128)(2,1)S(1)}, u32[]{:S(2)}, u32[]{:S(2)}) %collective-permute-start) | collective-permute-done | bytes 786464 | tf_op jit(solution)/shard_map/ppermute | solution.py:31
  27.0 1.6 %pad_maximum_fusion = bf16[144,8192]{1,0:T(8,128)(2,1)} fusion(bf16[48,8192]{1,0:T(8,128)(2,1)S(1)} %collective-permute-done.1.refs_3_, bf16[48,8192]{1,0:T(8,128)(2,1)S(1)} %collective-permute-done.refs_2_, bf16[48,8192]{1,0:T(8,128)(2,1)S(1)} %norm.1.refs_1_), kind=kLoop, calls=%fused_computation.2 | loop fusion | flops 7077888 | bytes 4718592 | tf_op jit(solution)/shard_map/concatenate | solution.py:353
  28.6 1.7 %collective-permute-start.5 = (bf16[144,8192]{1,0:T(8,128)(2,1)}, bf16[144,8192]{1,0:T(8,128)(2,1)}, u32[]{:S(2)}, u32[]{:S(2)}) collective-permute-start(bf16[144,8192]{1,0:T(8,128)(2,1)} %pad_maximum_fusion), channel_id=1, source_target_pairs={{0,1},{1,0},{2,3},{3,2},{4,5},{5,4},{6,7},{7,6},{8,9},{9,8},{10,11... | collective-permute-start | bytes 7077896 | tf_op jit(solution)/shard_map/ppermute | solution.py:31
  31.2 2.7 %collective-permute-start.4 = (bf16[48,8192]{1,0:T(8,128)(2,1)}, bf16[48,8192]{1,0:T(8,128)(2,1)}, u32[]{:S(2)}, u32[]{:S(2)}) collective-permute-start(bf16[48,8192]{1,0:T(8,128)(2,1)} %broadcast_select_fusion), channel_id=1, source_target_pairs={{0,2},{1,7},{2,4},{3,1},{4,6},{5,3},{6,0},{7,5},{8,10},{9,15},{10,... | collective-permute-start | bytes 2359304 | tf_op jit(solution)/shard_map/ppermute | solution.py:31
  34.0 3.7 %pick.1 = (bf16[12,512,128]{2,1,0:T(8,128)(2,1)}, bf16[12,512,128]{2,1,0:T(8,128)(2,1)}) custom-call(s32[12]{0:T(128)S(1)} %select_reduce_fusion.2.index_ref, bf16[8,512,128]{2,1,0:T(8,128)(2,1)S(1)} %pad_maximum_fusion.1.first_ref.own.refs_0_, bf16[8,512,128]{2,1,0:T(8,128)(2,1)} %collective-permute-done.2.before.refs_1_, ...), custom_call_target="tpu_custom_call" | custom-call | bytes 6291456 | tf_op jit(solution)/shard_map/pick/pallas_call | solution.py:94
  38.5 1.2 %collective-permute-start.9 = (bf16[12,512,128]{2,1,0:T(8,128)(2,1)}, bf16[12,512,128]{2,1,0:T(8,128)(2,1)}, u32[]{:S(2)}, u32[]{:S(2)}) collective-permute-start(bf16[12,512,128]{2,1,0:T(8,128)(2,1)} %get-tuple-element.19), channel_id=1, source_target_pairs={{0,32},{1,9},{2,34},{3,11},{4,36},{5,13},{6,38},{7,15},{8,40},{9,1... | collective-permute-start | bytes 4718600 | tf_op jit(solution)/shard_map/ppermute | solution.py:31
  39.7 1.5 %collective-permute-start.10 = (bf16[12,512,128]{2,1,0:T(8,128)(2,1)}, bf16[12,512,128]{2,1,0:T(8,128)(2,1)}, u32[]{:S(2)}, u32[]{:S(2)}) collective-permute-start(bf16[12,512,128]{2,1,0:T(8,128)(2,1)} %get-tuple-element.20), channel_id=1, source_target_pairs={{0,96},{1,25},{2,98},{3,27},{4,100},{5,29},{6,102},{7,31},{8,104},... | collective-permute-start | bytes 4718600 | tf_op jit(solution)/shard_map/ppermute | solution.py:31
  43.4 1.3 %collective-permute-start.6 = (bf16[48,8192]{1,0:T(8,128)(2,1)}, bf16[48,8192]{1,0:T(8,128)(2,1)S(1)}, u32[]{:S(2)}, u32[]{:S(2)}) collective-permute-start(bf16[48,8192]{1,0:T(8,128)(2,1)} %collective-permute-done.4.refs_4_), channel_id=1, source_target_pairs={{0,1},{1,0},{2,3},{3,2},{4,5},{5,4},{6,7},{7,6},{8,9},{9,8},{10,11... | collective-permute-start | bytes 2359304 | tf_op jit(solution)/shard_map/ppermute | solution.py:31
  46.9 1.6 %copy-done.1 = bf16[8192,128]{1,0:T(8,128)(2,1)S(1)} copy-done((bf16[8192,128]{1,0:T(8,128)(2,1)S(1)}, bf16[8192,128]{1,0:T(8,128)(2,1)}, u32[]{:S(2)}) %copy-start.1) | copy-done | bytes 2097176
  48.5 12.0 %project.2 = (bf16[4,384,128]{2,1,0:T(8,128)(2,1)S(1)}, bf16[384,128]{1,0:T(8,128)(2,1)S(1)}, bf16[384,128]{1,0:T(8,128)(2,1)S(1)}) custom-call(s32[8]{0:T(128)S(1)} %stack.82.refs_0_, bf16[48,8192]{1,0:T(8,128)(2,1)S(1)} %norm.1.refs_1_, bf16[48,8192]{1,0:T(8,128)(2,1)S(1)} %collective-permute-done.refs_2_, ...), custom_call_target="tpu_custom_call" | custom-call | bytes 1048576 | tf_op jit(solution)/shard_map/project/pallas_call | solution.py:167
  60.5 1.1 %slice.38 = bf16[4,512,128]{2,1,0:T(8,128)(2,1)S(1)} slice(bf16[12,512,128]{2,1,0:T(8,128)(2,1)} %collective-permute-done.9.refs_5_), slice={[8:12], [0:512], [0:128]} | slice | bytes 1048576 | tf_op jit(solution)/shard_map/slice | solution.py:408
  61.6 1.3 %collective-permute-start.11 = (bf16[4,512,128]{2,1,0:T(8,128)(2,1)S(1)}, bf16[4,512,128]{2,1,0:T(8,128)(2,1)S(1)}, u32[]{:S(2)}, u32[]{:S(2)}) collective-permute-start(bf16[4,512,128]{2,1,0:T(8,128)(2,1)S(1)} %slice.38), channel_id=1, source_target_pairs={{0,32},{1,9},{2,34},{3,11},{4,36},{5,13},{6,38},{7,15},{8,40},{9,1... | collective-permute-start | bytes 1572872 | tf_op jit(solution)/shard_map/ppermute | solution.py:31
  64.0 1.5 %collective-permute-start.12 = (bf16[4,512,128]{2,1,0:T(8,128)(2,1)S(1)}, bf16[4,512,128]{2,1,0:T(8,128)(2,1)S(1)}, u32[]{:S(2)}, u32[]{:S(2)}) collective-permute-start(bf16[4,512,128]{2,1,0:T(8,128)(2,1)S(1)} %slice.39), channel_id=1, source_target_pairs={{0,96},{1,25},{2,98},{3,27},{4,100},{5,29},{6,102},{7,31},{8,104},... | collective-permute-start | bytes 1572872 | tf_op jit(solution)/shard_map/ppermute | solution.py:31
  65.5 8.7 %project.3.high_ref = bf16[4,384,128]{2,1,0:T(8,128)(2,1)S(1)} custom-call(s32[8]{0:T(128)S(1)} %stack.82.refs_0_, bf16[48,8192]{1,0:T(8,128)(2,1)S(1)} %norm.1.refs_1_, bf16[48,8192]{1,0:T(8,128)(2,1)S(1)} %collective-permute-done.refs_2_, bf16[48,8192]{1,0:T(8,128)(2,1)S(1)} %collective-permute-done.1.refs_3_, ...), custom_call_target="tpu_custom_call" | custom-call | bytes 1048576 | tf_op jit(solution)/shard_map/project/pallas_call | solution.py:167
  74.4 20.2 %attend.1 = bf16[384,1024]{1,0:T(8,128)(2,1)} custom-call(s32[4,8]{1,0:T(4,128)S(1)} %pad_add_fusion.where_ref, s32[3]{0:T(128)S(1)} %fusion.10.count_ref, bf16[4,384,128]{2,1,0:T(8,128)(2,1)S(1)} %get-tuple-element.16.low_ref, bf16[4,384,128]{2,1,0:T(8,128)(2,1)S(1)} %project.3.high_ref, bf16[384,128]{1,0:T(8,128)(2,1)S(1)} %get-tuple-element.17.nk_ref, ...), custom_call_target="tpu_custom_call" | custom-call | flops 6442450944 | bytes 8388608 | tf_op jit(solution)/shard_map/attend/pallas_call | solution.py:300
  (65 shorter events, 9.7 us)
Async XLA Ops:
  0.0 5.8 %copy-start.2 = (bf16[1,48,8192]{2,1,0:T(8,128)(2,1)S(1)}, bf16[1,48,8192]{2,1,0:T(8,128)(2,1)}, u32[]{:S(2)}) copy-start(bf16[1,48,8192]{2,1,0:T(8,128)(2,1)} %param.10) | copy-start | bytes 2359300
  0.0 10.3 %copy-start.8 = (s32[16,8]{0,1:T(8,128)S(1)}, s32[16,8]{0,1:T(8,128)}, u32[]{:S(2)}) copy-start(s32[16,8]{0,1:T(8,128)} %param.18) | copy-start | bytes 1540
  0.0 10.3 %copy-start.7 = (s32[1,384]{1,0:T(1,128)S(1)}, s32[1,384]{1,0:T(1,128)}, u32[]{:S(2)}) copy-start(s32[1,384]{1,0:T(1,128)} %npos_ref.1) | copy-start | bytes 4612
  0.0 10.4 %copy-start.9 = (s32[64]{0:T(128)S(1)}, s32[64]{0:T(128)}, u32[]{:S(2)}) copy-start(s32[64]{0:T(128)} %param.17) | copy-start | bytes 772
  1.4 16.2 %collective-permute-start.2 = (bf16[8,512,128]{2,1,0:T(8,128)(2,1)S(1)}, bf16[8,512,128]{2,1,0:T(8,128)(2,1)}, u32[]{:S(2)}, u32[]{:S(2)}) collective-permute-start(bf16[8,512,128]{2,1,0:T(8,128)(2,1)S(1)} %pad_maximum_fusion.1.first_ref.own.refs_0_), channel_id=1, source_target_pairs={{0,8},{1,33},{2,10},{3,35},{4,12},{5,37},{6,14},{7,39},{8,16},{9,4... | collective-permute-start | bytes 3145736 | tf_op jit(solution)/shard_map/ppermute | solution.py:31
  3.6 15.2 %collective-permute-start.3 = (bf16[8,512,128]{2,1,0:T(8,128)(2,1)S(1)}, bf16[8,512,128]{2,1,0:T(8,128)(2,1)}, u32[]{:S(2)}, u32[]{:S(2)}) collective-permute-start(bf16[8,512,128]{2,1,0:T(8,128)(2,1)S(1)} %pad_maximum_fusion.1.first_ref.own.refs_0_), channel_id=1, source_target_pairs={{0,24},{1,97},{2,26},{3,99},{4,28},{5,101},{6,30},{7,103},{8,0},{9... | collective-permute-start | bytes 3145736 | tf_op jit(solution)/shard_map/ppermute | solution.py:31
  6.4 20.6 %collective-permute-start = (bf16[48,8192]{1,0:T(8,128)(2,1)S(1)}, bf16[48,8192]{1,0:T(8,128)(2,1)S(1)}, u32[]{:S(2)}, u32[]{:S(2)}) collective-permute-start(bf16[48,8192]{1,0:T(8,128)(2,1)S(1)} %norm.1.refs_1_), channel_id=1, source_target_pairs={{0,2},{1,3},{2,4},{3,5},{4,6},{5,7},{6,0},{7,1},{8,10},{9,11},{10,... | collective-permute-start | bytes 2359304 | tf_op jit(solution)/shard_map/ppermute | solution.py:31
  8.1 18.9 %collective-permute-start.1 = (bf16[48,8192]{1,0:T(8,128)(2,1)S(1)}, bf16[48,8192]{1,0:T(8,128)(2,1)S(1)}, u32[]{:S(2)}, u32[]{:S(2)}) collective-permute-start(bf16[48,8192]{1,0:T(8,128)(2,1)S(1)} %norm.1.refs_1_), channel_id=1, source_target_pairs={{0,6},{1,7},{2,0},{3,1},{4,2},{5,3},{6,4},{7,5},{8,14},{9,15},{10,... | collective-permute-start | bytes 2359304 | tf_op jit(solution)/shard_map/ppermute | solution.py:31
  18.7 15.3 %collective-permute-start.7 = (bf16[4,512,128]{2,1,0:T(8,128)(2,1)S(1)}, bf16[4,512,128]{2,1,0:T(8,128)(2,1)S(1)}, u32[]{:S(2)}, u32[]{:S(2)}) collective-permute-start(bf16[4,512,128]{2,1,0:T(8,128)(2,1)S(1)} %slice.40), channel_id=1, source_target_pairs={{0,8},{1,33},{2,10},{3,35},{4,12},{5,37},{6,14},{7,39},{8,16},{9,4... | collective-permute-start | bytes 1572872 | tf_op jit(solution)/shard_map/ppermute | solution.py:31
  19.9 14.1 %collective-permute-start.8 = (bf16[4,512,128]{2,1,0:T(8,128)(2,1)S(1)}, bf16[4,512,128]{2,1,0:T(8,128)(2,1)S(1)}, u32[]{:S(2)}, u32[]{:S(2)}) collective-permute-start(bf16[4,512,128]{2,1,0:T(8,128)(2,1)S(1)} %slice.41), channel_id=1, source_target_pairs={{0,24},{1,97},{2,26},{3,99},{4,28},{5,101},{6,30},{7,103},{8,0},{9... | collective-permute-start | bytes 1572872 | tf_op jit(solution)/shard_map/ppermute | solution.py:31
  28.6 18.3 %collective-permute-start.5 = (bf16[144,8192]{1,0:T(8,128)(2,1)}, bf16[144,8192]{1,0:T(8,128)(2,1)}, u32[]{:S(2)}, u32[]{:S(2)}) collective-permute-start(bf16[144,8192]{1,0:T(8,128)(2,1)} %pad_maximum_fusion), channel_id=1, source_target_pairs={{0,1},{1,0},{2,3},{3,2},{4,5},{5,4},{6,7},{7,6},{8,9},{9,8},{10,11... | collective-permute-start | bytes 7077896 | tf_op jit(solution)/shard_map/ppermute | solution.py:31
  31.2 12.2 %collective-permute-start.4 = (bf16[48,8192]{1,0:T(8,128)(2,1)}, bf16[48,8192]{1,0:T(8,128)(2,1)}, u32[]{:S(2)}, u32[]{:S(2)}) collective-permute-start(bf16[48,8192]{1,0:T(8,128)(2,1)} %broadcast_select_fusion), channel_id=1, source_target_pairs={{0,2},{1,7},{2,4},{3,1},{4,6},{5,3},{6,0},{7,5},{8,10},{9,15},{10,... | collective-permute-start | bytes 2359304 | tf_op jit(solution)/shard_map/ppermute | solution.py:31
  34.0 3.7 %copy-start.5 = (bf16[4,512,128]{2,1,0:T(8,128)(2,1)}, bf16[4,512,128]{2,1,0:T(8,128)(2,1)S(1)}, u32[]{:S(2)}) copy-start(bf16[4,512,128]{2,1,0:T(8,128)(2,1)S(1)} %collective-permute-done.8.v_far.refs_4_) | copy-start | bytes 1572868
  37.7 0.8 copy-start.3
  38.5 22.0 %collective-permute-start.9 = (bf16[12,512,128]{2,1,0:T(8,128)(2,1)}, bf16[12,512,128]{2,1,0:T(8,128)(2,1)}, u32[]{:S(2)}, u32[]{:S(2)}) collective-permute-start(bf16[12,512,128]{2,1,0:T(8,128)(2,1)} %get-tuple-element.19), channel_id=1, source_target_pairs={{0,32},{1,9},{2,34},{3,11},{4,36},{5,13},{6,38},{7,15},{8,40},{9,1... | collective-permute-start | bytes 4718600 | tf_op jit(solution)/shard_map/ppermute | solution.py:31
  39.7 20.8 %collective-permute-start.10 = (bf16[12,512,128]{2,1,0:T(8,128)(2,1)}, bf16[12,512,128]{2,1,0:T(8,128)(2,1)}, u32[]{:S(2)}, u32[]{:S(2)}) collective-permute-start(bf16[12,512,128]{2,1,0:T(8,128)(2,1)} %get-tuple-element.20), channel_id=1, source_target_pairs={{0,96},{1,25},{2,98},{3,27},{4,100},{5,29},{6,102},{7,31},{8,104},... | collective-permute-start | bytes 4718600 | tf_op jit(solution)/shard_map/ppermute | solution.py:31
  42.4 4.4 %copy-start = (bf16[8192,128]{1,0:T(8,128)(2,1)S(1)}, bf16[8192,128]{1,0:T(8,128)(2,1)}, u32[]{:S(2)}) copy-start(bf16[8192,128]{1,0:T(8,128)(2,1)} %refs_8_.1) | copy-start | bytes 6291460
  43.4 3.4 %collective-permute-start.6 = (bf16[48,8192]{1,0:T(8,128)(2,1)}, bf16[48,8192]{1,0:T(8,128)(2,1)S(1)}, u32[]{:S(2)}, u32[]{:S(2)}) collective-permute-start(bf16[48,8192]{1,0:T(8,128)(2,1)} %collective-permute-done.4.refs_4_), channel_id=1, source_target_pairs={{0,1},{1,0},{2,3},{3,2},{4,5},{5,4},{6,7},{7,6},{8,9},{9,8},{10,11... | collective-permute-start | bytes 2359304 | tf_op jit(solution)/shard_map/ppermute | solution.py:31
  46.9 1.6 %copy-start.1 = (bf16[8192,128]{1,0:T(8,128)(2,1)S(1)}, bf16[8192,128]{1,0:T(8,128)(2,1)}, u32[]{:S(2)}) copy-start(bf16[8192,128]{1,0:T(8,128)(2,1)} %refs_9_.1) | copy-start | bytes 6291460
  61.6 12.7 %collective-permute-start.11 = (bf16[4,512,128]{2,1,0:T(8,128)(2,1)S(1)}, bf16[4,512,128]{2,1,0:T(8,128)(2,1)S(1)}, u32[]{:S(2)}, u32[]{:S(2)}) collective-permute-start(bf16[4,512,128]{2,1,0:T(8,128)(2,1)S(1)} %slice.38), channel_id=1, source_target_pairs={{0,32},{1,9},{2,34},{3,11},{4,36},{5,13},{6,38},{7,15},{8,40},{9,1... | collective-permute-start | bytes 1572872 | tf_op jit(solution)/shard_map/ppermute | solution.py:31
  64.0 10.3 %collective-permute-start.12 = (bf16[4,512,128]{2,1,0:T(8,128)(2,1)S(1)}, bf16[4,512,128]{2,1,0:T(8,128)(2,1)S(1)}, u32[]{:S(2)}, u32[]{:S(2)}) collective-permute-start(bf16[4,512,128]{2,1,0:T(8,128)(2,1)S(1)} %slice.39), channel_id=1, source_target_pairs={{0,96},{1,25},{2,98},{3,27},{4,100},{5,29},{6,102},{7,31},{8,104},... | collective-permute-start | bytes 1572872 | tf_op jit(solution)/shard_map/ppermute | solution.py:31
  65.5 8.9 %copy-start.4 = (bf16[4,512,128]{2,1,0:T(8,128)(2,1)S(1)}, bf16[4,512,128]{2,1,0:T(8,128)(2,1)}, u32[]{:S(2)}) copy-start(bf16[4,512,128]{2,1,0:T(8,128)(2,1)} %copy-done.3) | copy-start | bytes 1572868
  65.5 8.9 %copy-start.6 = (bf16[4,512,128]{2,1,0:T(8,128)(2,1)S(1)}, bf16[4,512,128]{2,1,0:T(8,128)(2,1)}, u32[]{:S(2)}) copy-start(bf16[4,512,128]{2,1,0:T(8,128)(2,1)} %copy-done.5) | copy-start | bytes 1572868

commit v5 on v4

--- a/solution.py
+++ b/solution.py
@@ -54,7 +54,7 @@
 def norm_kernel(tokens_ref, gain_ref, first_ref, out_ref):
     hidden = tokens_ref[...].astype(F32)
     scale = lax.rsqrt(jnp.mean(hidden * hidden, axis=-1, keepdims=True) + EPS)
-    out_ref[...] = (hidden * scale * gain_ref[...].astype(F32)).astype(BF16)
+    out_ref[...] = (hidden * scale * gain_ref[...].astype(F32)[None, :]).astype(BF16)
 
 
 def normalise(tokens, gain, first):
@@ -66,7 +66,7 @@
         out_specs=vmem,
         compiler_params=pltpu.CompilerParams(vmem_limit_bytes=8 * MIB),
         name="norm",
-    )(tokens, gain.reshape(1, -1), first)
+    )(tokens, gain, first)
 
 
 def pick_kernel(index_ref, own, before, behind, k_far, v_far, up, down):
@@ -209,10 +209,7 @@
             @pl.when(where_ref[0, j] == n)
             def _():
                 pltpu.make_async_copy(keys[n].at[where_ref[1, j]], k_dest(j), sems.at[0, j]).start()
-
-            @pl.when(where_ref[2, j] == n)
-            def _():
-                pltpu.make_async_copy(values[n].at[where_ref[3, j]], v_dest(j), sems.at[1, j]).start()
+                pltpu.make_async_copy(values[n].at[where_ref[2, j]], v_dest(j), sems.at[1, j]).start()
 
     v_buf[:, dim:] = jnp.ones((ctx, dim), BF16)
     nv_buf[:, dim:] = jnp.ones((sel, dim), BF16)
@@ -251,21 +248,31 @@
         scores, most = masked_scores(queries, nk_ref[...], npos_ref[...], query_pos)
         s_buf[:, ctx:] = scores
         m_buf[...] = most
-        count = (count_ref[i] + STEP - 1) // STEP
-        span = STEP * block
-
-        def first(j, carry):
+        count = count_ref[i]
+
+        def first(at, blocks_now):
+            span = blocks_now * block
             scores, most = masked_scores(
                 q_buf[...],
-                k_buf[pl.ds(j * STEP, STEP)].reshape(span, dim),
-                jnp.concatenate([kpos_ref[pl.ds(j * STEP + n, 1), :] for n in range(STEP)], axis=1),
+                k_buf[pl.ds(at, blocks_now)].reshape(span, dim),
+                jnp.concatenate([kpos_ref[pl.ds(at + n, 1), :] for n in range(blocks_now)], axis=1),
                 qpos_ref[rows, :],
             )
-            s_buf[:, pl.ds(pl.multiple_of(j * span, span), span)] = scores
+            s_buf[:, pl.ds(pl.multiple_of(at * block, block), span)] = scores
             m_buf[...] = jnp.maximum(m_buf[...], most)
-            return carry
-
-        lax.fori_loop(0, count, first, 0)
+
+        def over_blocks(body):
+            def some(j, carry):
+                body(j * STEP, STEP)
+                return carry
+
+            lax.fori_loop(0, count // STEP, some, 0)
+
+            @pl.when(count % STEP == 1)
+            def _():
+                body(count - 1, 1)
+
+        over_blocks(first)
         m_buf[...] = jnp.broadcast_to(jnp.max(m_buf[...], axis=1, keepdims=True), (tall, 128))
 
         def expos(scores):
@@ -274,12 +281,11 @@
 
         acc[...] = jnp.dot(expos(s_buf[:, ctx:]), nv_buf[...], preferred_element_type=F32)
 
-        def second(j, carry):
-            at = pl.ds(pl.multiple_of(j * span, span), span)
-            acc[...] += jnp.dot(expos(s_buf[:, at]), v_buf[at, :], preferred_element_type=F32)
-            return carry
-
-        lax.fori_loop(0, count, second, 0)
+        def second(at, blocks_now):
+            span = pl.ds(pl.multiple_of(at * block, block), blocks_now * block)
+            acc[...] += jnp.dot(expos(s_buf[:, span]), v_buf[span, :], preferred_element_type=F32)
+
+        over_blocks(second)
         result = (acc[:, :dim] / acc[:, dim:]).astype(BF16)
         for h in range(heads):
             out_ref[rows, h * dim : (h + 1) * dim] = result[h * ROWS : (h + 1) * ROWS]
@@ -385,7 +391,7 @@
     entry = jnp.where(two == 0, local, one)
     offset = jnp.where(two == 0, held, 4)
     shared = (array != 3) & (array != 6)
-    where = jnp.stack([array, entry, array, jnp.where(shared, entry + offset, entry)]).astype(jnp.int32)
+    where = jnp.stack([array, entry, jnp.where(shared, entry + offset, entry)]).astype(jnp.int32)
 
     positions = sel_index[0]
     sel = positions.shape[0]

time: 95.5 us -> 94.5 us (0.990)
    unnamed x21 -> x23, local copies, waits for them, and re-layouts: 2.51 us -> 3.24 us
  transfers between devices with their start and end apart: 13 -> 13, of which waited for: 3 -> 3; matrix products, arithmetic and copies ran while one was open for 12% -> 11% of each run, Pallas kernels for 26% -> 26%
where the time goes in v5:
time: 94.5 us; the launch traced here: 94.4 us
  Pallas kernels  44.7 us (47%)
  starting transfers between devices  21.7 us (23%)
  waiting for transfers between devices  11.4 us (12%)
  local copies, waits for them, and re-layouts  8.11 us (9%)
  other arithmetic  8.05 us (9%)
    ppermute x13, starting transfers between devices, move(): return lax.ppermute(value, ('req', 'tp'), pairs)  21.7 us
    pallas_call x2, Pallas kernels, project(): pl.pallas_call(functools.partial(project_kernel, bool(w_kv)), grid=(3 if...  20.7 us
    pallas_call x1, Pallas kernels, attend(): pl.pallas_call(attend_kernel, out_shape=jax.ShapeDtypeStruct((sel, heads...  19.8 us
    ppermute x13, waiting for transfers between devices, move(): return lax.ppermute(value, ('req', 'tp'), pairs)  11.4 us
    pallas_call x1, Pallas kernels, pick(): pl.pallas_call(pick_kernel, out_shape=[jax.ShapeDtypeStruct((12, tokens,...  3.68 us
    unnamed x23, local copies, waits for them, and re-layouts  3.24 us
    slice x2, local copies, waits for them, and re-layouts, on_device(): k_half, v_half = (before[:held], behind[held:])  2.15 us
  transfers between devices with their start and end apart: 13, of which 3 were waited for; matrix products, arithmetic and copies ran while one was open for 11% of the time, Pallas kernels for 26%

profile of v5, /device:TPU:1, one launch (start us, length us, event | category | flops | bytes accessed | tf_op | source)
XLA Modules:
  0.0 94.4 jit_solution(9572276293249549009)
XLA Ops:
  0.0 1.4 %pad_maximum_fusion.1.first_ref.own.refs_0_ = bf16[8,512,128]{2,1,0:T(8,128)(2,1)S(1)} fusion(bf16[4,512,128]{2,1,0:T(8,128)(2,1)} %bitcast.66, bf16[4,512,128]{2,1,0:T(8,128)(2,1)} %bitcast.67), kind=kLoop, calls=%fused_computation.3 | loop fusion | flops 524288 | bytes 2097152 | tf_op jit(solution)/shard_map/concatenate | solution.py:349
  1.4 2.2 %collective-permute-start.2 = (bf16[8,512,128]{2,1,0:T(8,128)(2,1)S(1)}, bf16[8,512,128]{2,1,0:T(8,128)(2,1)}, u32[]{:S(2)}, u32[]{:S(2)}) collective-permute-start(bf16[8,512,128]{2,1,0:T(8,128)(2,1)S(1)} %pad_maximum_fusion.1.first_ref.own.refs_0_), channel_id=1, source_target_pairs={{0,8},{1,33},{2,10},{3,35},{4,12},{5,37},{6,14},{7,39},{8,16},{9,4... | collective-permute-start | bytes 3145736 | tf_op jit(solution)/shard_map/ppermute | solution.py:31
  3.6 1.5 %collective-permute-start.3 = (bf16[8,512,128]{2,1,0:T(8,128)(2,1)S(1)}, bf16[8,512,128]{2,1,0:T(8,128)(2,1)}, u32[]{:S(2)}, u32[]{:S(2)}) collective-permute-start(bf16[8,512,128]{2,1,0:T(8,128)(2,1)S(1)} %pad_maximum_fusion.1.first_ref.own.refs_0_), channel_id=1, source_target_pairs={{0,24},{1,97},{2,26},{3,99},{4,28},{5,101},{6,30},{7,103},{8,0},{9... | collective-permute-start | bytes 3145736 | tf_op jit(solution)/shard_map/ppermute | solution.py:31
  6.3 1.7 %collective-permute-start = (bf16[48,8192]{1,0:T(8,128)(2,1)S(1)}, bf16[48,8192]{1,0:T(8,128)(2,1)S(1)}, u32[]{:S(2)}, u32[]{:S(2)}) collective-permute-start(bf16[48,8192]{1,0:T(8,128)(2,1)S(1)} %norm.1.refs_1_), channel_id=1, source_target_pairs={{0,2},{1,3},{2,4},{3,5},{4,6},{5,7},{6,0},{7,1},{8,10},{9,11},{10,... | collective-permute-start | bytes 2359304 | tf_op jit(solution)/shard_map/ppermute | solution.py:31
  8.0 2.2 %collective-permute-start.1 = (bf16[48,8192]{1,0:T(8,128)(2,1)S(1)}, bf16[48,8192]{1,0:T(8,128)(2,1)S(1)}, u32[]{:S(2)}, u32[]{:S(2)}) collective-permute-start(bf16[48,8192]{1,0:T(8,128)(2,1)S(1)} %norm.1.refs_1_), channel_id=1, source_target_pairs={{0,6},{1,7},{2,0},{3,1},{4,2},{5,3},{6,4},{7,5},{8,14},{9,15},{10,... | collective-permute-start | bytes 2359304 | tf_op jit(solution)/shard_map/ppermute | solution.py:31
  11.3 6.3 %collective-permute-done.2.before.refs_1_ = bf16[8,512,128]{2,1,0:T(8,128)(2,1)} collective-permute-done((bf16[8,512,128]{2,1,0:T(8,128)(2,1)S(1)}, bf16[8,512,128]{2,1,0:T(8,128)(2,1)}, u32[]{:S(2)}, u32[]{:S(2)}) %collective-permute-start.2) | collective-permute-done | bytes 1048608 | tf_op jit(solution)/shard_map/ppermute | solution.py:31
  17.6 1.1 %slice.40 = bf16[4,512,128]{2,1,0:T(8,128)(2,1)S(1)} slice(bf16[8,512,128]{2,1,0:T(8,128)(2,1)} %collective-permute-done.2.before.refs_1_), slice={[0:4], [0:512], [0:128]} | slice | bytes 1048576 | tf_op jit(solution)/shard_map/slice | solution.py:355
  18.8 1.1 %slice.41 = bf16[4,512,128]{2,1,0:T(8,128)(2,1)S(1)} slice(bf16[8,512,128]{2,1,0:T(8,128)(2,1)} %collective-permute-done.3.behind.refs_2_), slice={[4:8], [0:512], [0:128]} | slice | bytes 1048576 | tf_op jit(solution)/shard_map/slice | solution.py:355
  19.9 2.7 %collective-permute-start.8 = (bf16[4,512,128]{2,1,0:T(8,128)(2,1)S(1)}, bf16[4,512,128]{2,1,0:T(8,128)(2,1)S(1)}, u32[]{:S(2)}, u32[]{:S(2)}) collective-permute-start(bf16[4,512,128]{2,1,0:T(8,128)(2,1)S(1)} %slice.41), channel_id=1, source_target_pairs={{0,24},{1,97},{2,26},{3,99},{4,28},{5,101},{6,30},{7,103},{8,0},{9... | collective-permute-start | bytes 1572872 | tf_op jit(solution)/shard_map/ppermute | solution.py:31
  22.6 4.3 %collective-permute-done.refs_2_ = bf16[48,8192]{1,0:T(8,128)(2,1)S(1)} collective-permute-done((bf16[48,8192]{1,0:T(8,128)(2,1)S(1)}, bf16[48,8192]{1,0:T(8,128)(2,1)S(1)}, u32[]{:S(2)}, u32[]{:S(2)}) %collective-permute-start) | collective-permute-done | bytes 786464 | tf_op jit(solution)/shard_map/ppermute | solution.py:31
  26.9 1.6 %pad_maximum_fusion = bf16[144,8192]{1,0:T(8,128)(2,1)} fusion(bf16[48,8192]{1,0:T(8,128)(2,1)S(1)} %collective-permute-done.1.refs_3_, bf16[48,8192]{1,0:T(8,128)(2,1)S(1)} %collective-permute-done.refs_2_, bf16[48,8192]{1,0:T(8,128)(2,1)S(1)} %norm.1.refs_1_), kind=kLoop, calls=%fused_computation.2 | loop fusion | flops 7077888 | bytes 4718592 | tf_op jit(solution)/shard_map/concatenate | solution.py:359
  28.5 1.7 %collective-permute-start.5 = (bf16[144,8192]{1,0:T(8,128)(2,1)}, bf16[144,8192]{1,0:T(8,128)(2,1)}, u32[]{:S(2)}, u32[]{:S(2)}) collective-permute-start(bf16[144,8192]{1,0:T(8,128)(2,1)} %pad_maximum_fusion), channel_id=1, source_target_pairs={{0,1},{1,0},{2,3},{3,2},{4,5},{5,4},{6,7},{7,6},{8,9},{9,8},{10,11... | collective-permute-start | bytes 7077896 | tf_op jit(solution)/shard_map/ppermute | solution.py:31
  31.2 2.7 %collective-permute-start.4 = (bf16[48,8192]{1,0:T(8,128)(2,1)}, bf16[48,8192]{1,0:T(8,128)(2,1)}, u32[]{:S(2)}, u32[]{:S(2)}) collective-permute-start(bf16[48,8192]{1,0:T(8,128)(2,1)} %broadcast_select_fusion), channel_id=1, source_target_pairs={{0,2},{1,7},{2,4},{3,1},{4,6},{5,3},{6,0},{7,5},{8,10},{9,15},{10,... | collective-permute-start | bytes 2359304 | tf_op jit(solution)/shard_map/ppermute | solution.py:31
  33.9 3.7 %pick.1 = (bf16[12,512,128]{2,1,0:T(8,128)(2,1)}, bf16[12,512,128]{2,1,0:T(8,128)(2,1)}) custom-call(s32[12]{0:T(128)S(1)} %select_reduce_fusion.2.index_ref, bf16[8,512,128]{2,1,0:T(8,128)(2,1)S(1)} %pad_maximum_fusion.1.first_ref.own.refs_0_, bf16[8,512,128]{2,1,0:T(8,128)(2,1)} %collective-permute-done.2.before.refs_1_, ...), custom_call_target="tpu_custom_call" | custom-call | bytes 6291456 | tf_op jit(solution)/shard_map/pick/pallas_call | solution.py:94
  38.5 1.2 %collective-permute-start.9 = (bf16[12,512,128]{2,1,0:T(8,128)(2,1)}, bf16[12,512,128]{2,1,0:T(8,128)(2,1)}, u32[]{:S(2)}, u32[]{:S(2)}) collective-permute-start(bf16[12,512,128]{2,1,0:T(8,128)(2,1)} %get-tuple-element.19), channel_id=1, source_target_pairs={{0,32},{1,9},{2,34},{3,11},{4,36},{5,13},{6,38},{7,15},{8,40},{9,1... | collective-permute-start | bytes 4718600 | tf_op jit(solution)/shard_map/ppermute | solution.py:31
  39.7 1.5 %collective-permute-start.10 = (bf16[12,512,128]{2,1,0:T(8,128)(2,1)}, bf16[12,512,128]{2,1,0:T(8,128)(2,1)}, u32[]{:S(2)}, u32[]{:S(2)}) collective-permute-start(bf16[12,512,128]{2,1,0:T(8,128)(2,1)} %get-tuple-element.20), channel_id=1, source_target_pairs={{0,96},{1,25},{2,98},{3,27},{4,100},{5,29},{6,102},{7,31},{8,104},... | collective-permute-start | bytes 4718600 | tf_op jit(solution)/shard_map/ppermute | solution.py:31
  43.4 1.3 %collective-permute-start.6 = (bf16[48,8192]{1,0:T(8,128)(2,1)}, bf16[48,8192]{1,0:T(8,128)(2,1)S(1)}, u32[]{:S(2)}, u32[]{:S(2)}) collective-permute-start(bf16[48,8192]{1,0:T(8,128)(2,1)} %collective-permute-done.4.refs_4_), channel_id=1, source_target_pairs={{0,1},{1,0},{2,3},{3,2},{4,5},{5,4},{6,7},{7,6},{8,9},{9,8},{10,11... | collective-permute-start | bytes 2359304 | tf_op jit(solution)/shard_map/ppermute | solution.py:31
  46.8 1.6 %copy-done.1 = bf16[8192,128]{1,0:T(8,128)(2,1)S(1)} copy-done((bf16[8192,128]{1,0:T(8,128)(2,1)S(1)}, bf16[8192,128]{1,0:T(8,128)(2,1)}, u32[]{:S(2)}) %copy-start.1) | copy-done | bytes 2097176
  48.4 12.0 %project.2 = (bf16[4,384,128]{2,1,0:T(8,128)(2,1)S(1)}, bf16[384,128]{1,0:T(8,128)(2,1)S(1)}, bf16[384,128]{1,0:T(8,128)(2,1)S(1)}) custom-call(s32[8]{0:T(128)S(1)} %stack.81.refs_0_, bf16[48,8192]{1,0:T(8,128)(2,1)S(1)} %norm.1.refs_1_, bf16[48,8192]{1,0:T(8,128)(2,1)S(1)} %collective-permute-done.refs_2_, ...), custom_call_target="tpu_custom_call" | custom-call | bytes 1048576 | tf_op jit(solution)/shard_map/project/pallas_call | solution.py:167
  60.5 1.1 %slice.38 = bf16[4,512,128]{2,1,0:T(8,128)(2,1)S(1)} slice(bf16[12,512,128]{2,1,0:T(8,128)(2,1)} %collective-permute-done.9.refs_5_), slice={[8:12], [0:512], [0:128]} | slice | bytes 1048576 | tf_op jit(solution)/shard_map/slice | solution.py:414
  61.5 1.3 %collective-permute-start.11 = (bf16[4,512,128]{2,1,0:T(8,128)(2,1)S(1)}, bf16[4,512,128]{2,1,0:T(8,128)(2,1)S(1)}, u32[]{:S(2)}, u32[]{:S(2)}) collective-permute-start(bf16[4,512,128]{2,1,0:T(8,128)(2,1)S(1)} %slice.38), channel_id=1, source_target_pairs={{0,32},{1,9},{2,34},{3,11},{4,36},{5,13},{6,38},{7,15},{8,40},{9,1... | collective-permute-start | bytes 1572872 | tf_op jit(solution)/shard_map/ppermute | solution.py:31
  63.9 1.5 %collective-permute-start.12 = (bf16[4,512,128]{2,1,0:T(8,128)(2,1)S(1)}, bf16[4,512,128]{2,1,0:T(8,128)(2,1)S(1)}, u32[]{:S(2)}, u32[]{:S(2)}) collective-permute-start(bf16[4,512,128]{2,1,0:T(8,128)(2,1)S(1)} %slice.39), channel_id=1, source_target_pairs={{0,96},{1,25},{2,98},{3,27},{4,100},{5,29},{6,102},{7,31},{8,104},... | collective-permute-start | bytes 1572872 | tf_op jit(solution)/shard_map/ppermute | solution.py:31
  65.5 8.7 %project.3.high_ref = bf16[4,384,128]{2,1,0:T(8,128)(2,1)S(1)} custom-call(s32[8]{0:T(128)S(1)} %stack.81.refs_0_, bf16[48,8192]{1,0:T(8,128)(2,1)S(1)} %norm.1.refs_1_, bf16[48,8192]{1,0:T(8,128)(2,1)S(1)} %collective-permute-done.refs_2_, bf16[48,8192]{1,0:T(8,128)(2,1)S(1)} %collective-permute-done.1.refs_3_, ...), custom_call_target="tpu_custom_call" | custom-call | bytes 1048576 | tf_op jit(solution)/shard_map/project/pallas_call | solution.py:167
  74.4 19.8 %attend.1 = bf16[384,1024]{1,0:T(8,128)(2,1)} custom-call(s32[3,8]{1,0:T(4,128)S(1)} %pad_add_fusion.where_ref, s32[3]{0:T(128)S(1)} %fusion.10.count_ref, bf16[4,384,128]{2,1,0:T(8,128)(2,1)S(1)} %get-tuple-element.16.low_ref, bf16[4,384,128]{2,1,0:T(8,128)(2,1)S(1)} %project.3.high_ref, bf16[384,128]{1,0:T(8,128)(2,1)S(1)} %get-tuple-element.17.nk_ref, ...), custom_call_target="tpu_custom_call" | custom-call | flops 6442450944 | bytes 8388608 | tf_op jit(solution)/shard_map/attend/pallas_call | solution.py:306
  (66 shorter events, 9.7 us)
Async XLA Ops:
  0.0 5.1 %copy-start.2 = (bf16[1,48,8192]{2,1,0:T(8,128)(2,1)S(1)}, bf16[1,48,8192]{2,1,0:T(8,128)(2,1)}, u32[]{:S(2)}) copy-start(bf16[1,48,8192]{2,1,0:T(8,128)(2,1)} %param.10) | copy-start | bytes 2359300
  0.0 10.2 %copy-start.9 = (s32[16,8]{0,1:T(8,128)S(1)}, s32[16,8]{0,1:T(8,128)}, u32[]{:S(2)}) copy-start(s32[16,8]{0,1:T(8,128)} %param.18) | copy-start | bytes 1540
  0.0 10.3 %copy-start.8 = (s32[1,384]{1,0:T(1,128)S(1)}, s32[1,384]{1,0:T(1,128)}, u32[]{:S(2)}) copy-start(s32[1,384]{1,0:T(1,128)} %npos_ref.1) | copy-start | bytes 4612
  0.0 10.3 %copy-start.10 = (s32[64]{0:T(128)S(1)}, s32[64]{0:T(128)}, u32[]{:S(2)}) copy-start(s32[64]{0:T(128)} %param.17) | copy-start | bytes 772
  1.4 16.2 %collective-permute-start.2 = (bf16[8,512,128]{2,1,0:T(8,128)(2,1)S(1)}, bf16[8,512,128]{2,1,0:T(8,128)(2,1)}, u32[]{:S(2)}, u32[]{:S(2)}) collective-permute-start(bf16[8,512,128]{2,1,0:T(8,128)(2,1)S(1)} %pad_maximum_fusion.1.first_ref.own.refs_0_), channel_id=1, source_target_pairs={{0,8},{1,33},{2,10},{3,35},{4,12},{5,37},{6,14},{7,39},{8,16},{9,4... | collective-permute-start | bytes 3145736 | tf_op jit(solution)/shard_map/ppermute | solution.py:31
  3.6 15.2 %collective-permute-start.3 = (bf16[8,512,128]{2,1,0:T(8,128)(2,1)S(1)}, bf16[8,512,128]{2,1,0:T(8,128)(2,1)}, u32[]{:S(2)}, u32[]{:S(2)}) collective-permute-start(bf16[8,512,128]{2,1,0:T(8,128)(2,1)S(1)} %pad_maximum_fusion.1.first_ref.own.refs_0_), channel_id=1, source_target_pairs={{0,24},{1,97},{2,26},{3,99},{4,28},{5,101},{6,30},{7,103},{8,0},{9... | collective-permute-start | bytes 3145736 | tf_op jit(solution)/shard_map/ppermute | solution.py:31
  5.1 0.7 copy-start.7
  6.3 20.6 %collective-permute-start = (bf16[48,8192]{1,0:T(8,128)(2,1)S(1)}, bf16[48,8192]{1,0:T(8,128)(2,1)S(1)}, u32[]{:S(2)}, u32[]{:S(2)}) collective-permute-start(bf16[48,8192]{1,0:T(8,128)(2,1)S(1)} %norm.1.refs_1_), channel_id=1, source_target_pairs={{0,2},{1,3},{2,4},{3,5},{4,6},{5,7},{6,0},{7,1},{8,10},{9,11},{10,... | collective-permute-start | bytes 2359304 | tf_op jit(solution)/shard_map/ppermute | solution.py:31
  8.0 18.9 %collective-permute-start.1 = (bf16[48,8192]{1,0:T(8,128)(2,1)S(1)}, bf16[48,8192]{1,0:T(8,128)(2,1)S(1)}, u32[]{:S(2)}, u32[]{:S(2)}) collective-permute-start(bf16[48,8192]{1,0:T(8,128)(2,1)S(1)} %norm.1.refs_1_), channel_id=1, source_target_pairs={{0,6},{1,7},{2,0},{3,1},{4,2},{5,3},{6,4},{7,5},{8,14},{9,15},{10,... | collective-permute-start | bytes 2359304 | tf_op jit(solution)/shard_map/ppermute | solution.py:31
  18.7 15.3 %collective-permute-start.7 = (bf16[4,512,128]{2,1,0:T(8,128)(2,1)S(1)}, bf16[4,512,128]{2,1,0:T(8,128)(2,1)S(1)}, u32[]{:S(2)}, u32[]{:S(2)}) collective-permute-start(bf16[4,512,128]{2,1,0:T(8,128)(2,1)S(1)} %slice.40), channel_id=1, source_target_pairs={{0,8},{1,33},{2,10},{3,35},{4,12},{5,37},{6,14},{7,39},{8,16},{9,4... | collective-permute-start | bytes 1572872 | tf_op jit(solution)/shard_map/ppermute | solution.py:31
  19.9 14.1 %collective-permute-start.8 = (bf16[4,512,128]{2,1,0:T(8,128)(2,1)S(1)}, bf16[4,512,128]{2,1,0:T(8,128)(2,1)S(1)}, u32[]{:S(2)}, u32[]{:S(2)}) collective-permute-start(bf16[4,512,128]{2,1,0:T(8,128)(2,1)S(1)} %slice.41), channel_id=1, source_target_pairs={{0,24},{1,97},{2,26},{3,99},{4,28},{5,101},{6,30},{7,103},{8,0},{9... | collective-permute-start | bytes 1572872 | tf_op jit(solution)/shard_map/ppermute | solution.py:31
  28.5 18.3 %collective-permute-start.5 = (bf16[144,8192]{1,0:T(8,128)(2,1)}, bf16[144,8192]{1,0:T(8,128)(2,1)}, u32[]{:S(2)}, u32[]{:S(2)}) collective-permute-start(bf16[144,8192]{1,0:T(8,128)(2,1)} %pad_maximum_fusion), channel_id=1, source_target_pairs={{0,1},{1,0},{2,3},{3,2},{4,5},{5,4},{6,7},{7,6},{8,9},{9,8},{10,11... | collective-permute-start | bytes 7077896 | tf_op jit(solution)/shard_map/ppermute | solution.py:31
  31.2 12.2 %collective-permute-start.4 = (bf16[48,8192]{1,0:T(8,128)(2,1)}, bf16[48,8192]{1,0:T(8,128)(2,1)}, u32[]{:S(2)}, u32[]{:S(2)}) collective-permute-start(bf16[48,8192]{1,0:T(8,128)(2,1)} %broadcast_select_fusion), channel_id=1, source_target_pairs={{0,2},{1,7},{2,4},{3,1},{4,6},{5,3},{6,0},{7,5},{8,10},{9,15},{10,... | collective-permute-start | bytes 2359304 | tf_op jit(solution)/shard_map/ppermute | solution.py:31
  33.9 3.7 %copy-start.5 = (bf16[4,512,128]{2,1,0:T(8,128)(2,1)}, bf16[4,512,128]{2,1,0:T(8,128)(2,1)S(1)}, u32[]{:S(2)}) copy-start(bf16[4,512,128]{2,1,0:T(8,128)(2,1)S(1)} %collective-permute-done.8.v_far.refs_4_) | copy-start | bytes 1572868
  37.6 0.8 copy-start.3
  38.5 22.0 %collective-permute-start.9 = (bf16[12,512,128]{2,1,0:T(8,128)(2,1)}, bf16[12,512,128]{2,1,0:T(8,128)(2,1)}, u32[]{:S(2)}, u32[]{:S(2)}) collective-permute-start(bf16[12,512,128]{2,1,0:T(8,128)(2,1)} %get-tuple-element.19), channel_id=1, source_target_pairs={{0,32},{1,9},{2,34},{3,11},{4,36},{5,13},{6,38},{7,15},{8,40},{9,1... | collective-permute-start | bytes 4718600 | tf_op jit(solution)/shard_map/ppermute | solution.py:31
  39.7 20.8 %collective-permute-start.10 = (bf16[12,512,128]{2,1,0:T(8,128)(2,1)}, bf16[12,512,128]{2,1,0:T(8,128)(2,1)}, u32[]{:S(2)}, u32[]{:S(2)}) collective-permute-start(bf16[12,512,128]{2,1,0:T(8,128)(2,1)} %get-tuple-element.20), channel_id=1, source_target_pairs={{0,96},{1,25},{2,98},{3,27},{4,100},{5,29},{6,102},{7,31},{8,104},... | collective-permute-start | bytes 4718600 | tf_op jit(solution)/shard_map/ppermute | solution.py:31
  42.4 4.4 %copy-start = (bf16[8192,128]{1,0:T(8,128)(2,1)S(1)}, bf16[8192,128]{1,0:T(8,128)(2,1)}, u32[]{:S(2)}) copy-start(bf16[8192,128]{1,0:T(8,128)(2,1)} %refs_8_.1) | copy-start | bytes 6291460
  43.4 3.4 %collective-permute-start.6 = (bf16[48,8192]{1,0:T(8,128)(2,1)}, bf16[48,8192]{1,0:T(8,128)(2,1)S(1)}, u32[]{:S(2)}, u32[]{:S(2)}) collective-permute-start(bf16[48,8192]{1,0:T(8,128)(2,1)} %collective-permute-done.4.refs_4_), channel_id=1, source_target_pairs={{0,1},{1,0},{2,3},{3,2},{4,5},{5,4},{6,7},{7,6},{8,9},{9,8},{10,11... | collective-permute-start | bytes 2359304 | tf_op jit(solution)/shard_map/ppermute | solution.py:31
  46.8 1.6 %copy-start.1 = (bf16[8192,128]{1,0:T(8,128)(2,1)S(1)}, bf16[8192,128]{1,0:T(8,128)(2,1)}, u32[]{:S(2)}) copy-start(bf16[8192,128]{1,0:T(8,128)(2,1)} %refs_9_.1) | copy-start | bytes 6291460
  61.5 12.7 %collective-permute-start.11 = (bf16[4,512,128]{2,1,0:T(8,128)(2,1)S(1)}, bf16[4,512,128]{2,1,0:T(8,128)(2,1)S(1)}, u32[]{:S(2)}, u32[]{:S(2)}) collective-permute-start(bf16[4,512,128]{2,1,0:T(8,128)(2,1)S(1)} %slice.38), channel_id=1, source_target_pairs={{0,32},{1,9},{2,34},{3,11},{4,36},{5,13},{6,38},{7,15},{8,40},{9,1... | collective-permute-start | bytes 1572872 | tf_op jit(solution)/shard_map/ppermute | solution.py:31
  63.9 10.3 %collective-permute-start.12 = (bf16[4,512,128]{2,1,0:T(8,128)(2,1)S(1)}, bf16[4,512,128]{2,1,0:T(8,128)(2,1)S(1)}, u32[]{:S(2)}, u32[]{:S(2)}) collective-permute-start(bf16[4,512,128]{2,1,0:T(8,128)(2,1)S(1)} %slice.39), channel_id=1, source_target_pairs={{0,96},{1,25},{2,98},{3,27},{4,100},{5,29},{6,102},{7,31},{8,104},... | collective-permute-start | bytes 1572872 | tf_op jit(solution)/shard_map/ppermute | solution.py:31
  65.5 8.9 %copy-start.4 = (bf16[4,512,128]{2,1,0:T(8,128)(2,1)S(1)}, bf16[4,512,128]{2,1,0:T(8,128)(2,1)}, u32[]{:S(2)}) copy-start(bf16[4,512,128]{2,1,0:T(8,128)(2,1)} %copy-done.3) | copy-start | bytes 1572868
  65.5 8.9 %copy-start.6 = (bf16[4,512,128]{2,1,0:T(8,128)(2,1)S(1)}, bf16[4,512,128]{2,1,0:T(8,128)(2,1)}, u32[]{:S(2)}) copy-start(bf16[4,512,128]{2,1,0:T(8,128)(2,1)} %copy-done.5) | copy-start | bytes 1572868

commit v6 on v5

--- a/solution.py
+++ b/solution.py
@@ -11,7 +11,7 @@
 F32 = jnp.float32
 SIDE = 4
 ROWS = 128
-STEP = 2
+STEP = 4
 THETA = 500000.0
 EPS = 1e-05
 HIDDEN_POS = 1 << 30
@@ -268,7 +268,11 @@
 
             lax.fori_loop(0, count // STEP, some, 0)
 
-            @pl.when(count % STEP == 1)
+            @pl.when(count % STEP >= 2)
+            def _():
+                body(count // STEP * STEP, 2)
+
+            @pl.when(count % 2 == 1)
             def _():
                 body(count - 1, 1)
 

time: 94.5 us -> 93.2 us (0.986)
  Pallas kernels: 44.7 us -> 43 us
    pallas_call x1, Pallas kernels: 19.8 us -> 18.1 us  [attend(): pl.pallas_call(attend_kernel, out_shape=jax.ShapeDtypeStruct((sel, heads...]
  transfers between devices with their start and end apart: 13 -> 13, of which waited for: 3 -> 3; matrix products, arithmetic and copies ran while one was open for 11% -> 11% of each run, Pallas kernels for 26% -> 27%
where the time goes in v6:
time: 93.2 us; the launch traced here: 92.7 us
  Pallas kernels  43 us (46%)
  starting transfers between devices  21.7 us (23%)
  waiting for transfers between devices  11.4 us (12%)
  local copies, waits for them, and re-layouts  8.11 us (9%)
  other arithmetic  8.05 us (9%)
    ppermute x13, starting transfers between devices, move(): return lax.ppermute(value, ('req', 'tp'), pairs)  21.7 us
    pallas_call x2, Pallas kernels, project(): pl.pallas_call(functools.partial(project_kernel, bool(w_kv)), grid=(3 if...  20.7 us
    pallas_call x1, Pallas kernels, attend(): pl.pallas_call(attend_kernel, out_shape=jax.ShapeDtypeStruct((sel, heads...  18.1 us
    ppermute x13, waiting for transfers between devices, move(): return lax.ppermute(value, ('req', 'tp'), pairs)  11.4 us
    pallas_call x1, Pallas kernels, pick(): pl.pallas_call(pick_kernel, out_shape=[jax.ShapeDtypeStruct((12, tokens,...  3.68 us
    unnamed x23, local copies, waits for them, and re-layouts  3.24 us
    slice x2, local copies, waits for them, and re-layouts, on_device(): k_half, v_half = (before[:held], behind[held:])  2.15 us
    neg x3, other arithmetic, tables(): -sine  1.87 us
  transfers between devices with their start and end apart: 13, of which 3 were waited for; matrix products, arithmetic and copies ran while one was open for 11% of the time, Pallas kernels for 27%

profile of v6, /device:TPU:1, one launch (start us, length us, event | category | flops | bytes accessed | tf_op | source)
XLA Modules:
  0.0 92.7 jit_solution(17039340564256939094)
XLA Ops:
  0.0 1.4 %pad_maximum_fusion.1.first_ref.own.refs_0_ = bf16[8,512,128]{2,1,0:T(8,128)(2,1)S(1)} fusion(bf16[4,512,128]{2,1,0:T(8,128)(2,1)} %bitcast.66, bf16[4,512,128]{2,1,0:T(8,128)(2,1)} %bitcast.67), kind=kLoop, calls=%fused_computation.3 | loop fusion | flops 524288 | bytes 2097152 | tf_op jit(solution)/shard_map/concatenate | solution.py:353
  1.4 2.2 %collective-permute-start.2 = (bf16[8,512,128]{2,1,0:T(8,128)(2,1)S(1)}, bf16[8,512,128]{2,1,0:T(8,128)(2,1)}, u32[]{:S(2)}, u32[]{:S(2)}) collective-permute-start(bf16[8,512,128]{2,1,0:T(8,128)(2,1)S(1)} %pad_maximum_fusion.1.first_ref.own.refs_0_), channel_id=1, source_target_pairs={{0,8},{1,33},{2,10},{3,35},{4,12},{5,37},{6,14},{7,39},{8,16},{9,4... | collective-permute-start | bytes 3145736 | tf_op jit(solution)/shard_map/ppermute | solution.py:31
  3.6 1.5 %collective-permute-start.3 = (bf16[8,512,128]{2,1,0:T(8,128)(2,1)S(1)}, bf16[8,512,128]{2,1,0:T(8,128)(2,1)}, u32[]{:S(2)}, u32[]{:S(2)}) collective-permute-start(bf16[8,512,128]{2,1,0:T(8,128)(2,1)S(1)} %pad_maximum_fusion.1.first_ref.own.refs_0_), channel_id=1, source_target_pairs={{0,24},{1,97},{2,26},{3,99},{4,28},{5,101},{6,30},{7,103},{8,0},{9... | collective-permute-start | bytes 3145736 | tf_op jit(solution)/shard_map/ppermute | solution.py:31
  6.3 1.7 %collective-permute-start = (bf16[48,8192]{1,0:T(8,128)(2,1)S(1)}, bf16[48,8192]{1,0:T(8,128)(2,1)S(1)}, u32[]{:S(2)}, u32[]{:S(2)}) collective-permute-start(bf16[48,8192]{1,0:T(8,128)(2,1)S(1)} %norm.1.refs_1_), channel_id=1, source_target_pairs={{0,2},{1,3},{2,4},{3,5},{4,6},{5,7},{6,0},{7,1},{8,10},{9,11},{10,... | collective-permute-start | bytes 2359304 | tf_op jit(solution)/shard_map/ppermute | solution.py:31
  8.0 2.2 %collective-permute-start.1 = (bf16[48,8192]{1,0:T(8,128)(2,1)S(1)}, bf16[48,8192]{1,0:T(8,128)(2,1)S(1)}, u32[]{:S(2)}, u32[]{:S(2)}) collective-permute-start(bf16[48,8192]{1,0:T(8,128)(2,1)S(1)} %norm.1.refs_1_), channel_id=1, source_target_pairs={{0,6},{1,7},{2,0},{3,1},{4,2},{5,3},{6,4},{7,5},{8,14},{9,15},{10,... | collective-permute-start | bytes 2359304 | tf_op jit(solution)/shard_map/ppermute | solution.py:31
  11.3 6.3 %collective-permute-done.2.before.refs_1_ = bf16[8,512,128]{2,1,0:T(8,128)(2,1)} collective-permute-done((bf16[8,512,128]{2,1,0:T(8,128)(2,1)S(1)}, bf16[8,512,128]{2,1,0:T(8,128)(2,1)}, u32[]{:S(2)}, u32[]{:S(2)}) %collective-permute-start.2) | collective-permute-done | bytes 1048608 | tf_op jit(solution)/shard_map/ppermute | solution.py:31
  17.6 1.1 %slice.40 = bf16[4,512,128]{2,1,0:T(8,128)(2,1)S(1)} slice(bf16[8,512,128]{2,1,0:T(8,128)(2,1)} %collective-permute-done.2.before.refs_1_), slice={[0:4], [0:512], [0:128]} | slice | bytes 1048576 | tf_op jit(solution)/shard_map/slice | solution.py:359
  18.8 1.1 %slice.41 = bf16[4,512,128]{2,1,0:T(8,128)(2,1)S(1)} slice(bf16[8,512,128]{2,1,0:T(8,128)(2,1)} %collective-permute-done.3.behind.refs_2_), slice={[4:8], [0:512], [0:128]} | slice | bytes 1048576 | tf_op jit(solution)/shard_map/slice | solution.py:359
  19.9 2.7 %collective-permute-start.8 = (bf16[4,512,128]{2,1,0:T(8,128)(2,1)S(1)}, bf16[4,512,128]{2,1,0:T(8,128)(2,1)S(1)}, u32[]{:S(2)}, u32[]{:S(2)}) collective-permute-start(bf16[4,512,128]{2,1,0:T(8,128)(2,1)S(1)} %slice.41), channel_id=1, source_target_pairs={{0,24},{1,97},{2,26},{3,99},{4,28},{5,101},{6,30},{7,103},{8,0},{9... | collective-permute-start | bytes 1572872 | tf_op jit(solution)/shard_map/ppermute | solution.py:31
  22.6 4.3 %collective-permute-done.refs_2_ = bf16[48,8192]{1,0:T(8,128)(2,1)S(1)} collective-permute-done((bf16[48,8192]{1,0:T(8,128)(2,1)S(1)}, bf16[48,8192]{1,0:T(8,128)(2,1)S(1)}, u32[]{:S(2)}, u32[]{:S(2)}) %collective-permute-start) | collective-permute-done | bytes 786464 | tf_op jit(solution)/shard_map/ppermute | solution.py:31
  26.9 1.6 %pad_maximum_fusion = bf16[144,8192]{1,0:T(8,128)(2,1)} fusion(bf16[48,8192]{1,0:T(8,128)(2,1)S(1)} %collective-permute-done.1.refs_3_, bf16[48,8192]{1,0:T(8,128)(2,1)S(1)} %collective-permute-done.refs_2_, bf16[48,8192]{1,0:T(8,128)(2,1)S(1)} %norm.1.refs_1_), kind=kLoop, calls=%fused_computation.2 | loop fusion | flops 7077888 | bytes 4718592 | tf_op jit(solution)/shard_map/concatenate | solution.py:363
  28.5 1.7 %collective-permute-start.5 = (bf16[144,8192]{1,0:T(8,128)(2,1)}, bf16[144,8192]{1,0:T(8,128)(2,1)}, u32[]{:S(2)}, u32[]{:S(2)}) collective-permute-start(bf16[144,8192]{1,0:T(8,128)(2,1)} %pad_maximum_fusion), channel_id=1, source_target_pairs={{0,1},{1,0},{2,3},{3,2},{4,5},{5,4},{6,7},{7,6},{8,9},{9,8},{10,11... | collective-permute-start | bytes 7077896 | tf_op jit(solution)/shard_map/ppermute | solution.py:31
  31.2 2.7 %collective-permute-start.4 = (bf16[48,8192]{1,0:T(8,128)(2,1)}, bf16[48,8192]{1,0:T(8,128)(2,1)}, u32[]{:S(2)}, u32[]{:S(2)}) collective-permute-start(bf16[48,8192]{1,0:T(8,128)(2,1)} %broadcast_select_fusion), channel_id=1, source_target_pairs={{0,2},{1,7},{2,4},{3,1},{4,6},{5,3},{6,0},{7,5},{8,10},{9,15},{10,... | collective-permute-start | bytes 2359304 | tf_op jit(solution)/shard_map/ppermute | solution.py:31
  33.9 3.7 %pick.1 = (bf16[12,512,128]{2,1,0:T(8,128)(2,1)}, bf16[12,512,128]{2,1,0:T(8,128)(2,1)}) custom-call(s32[12]{0:T(128)S(1)} %select_reduce_fusion.2.index_ref, bf16[8,512,128]{2,1,0:T(8,128)(2,1)S(1)} %pad_maximum_fusion.1.first_ref.own.refs_0_, bf16[8,512,128]{2,1,0:T(8,128)(2,1)} %collective-permute-done.2.before.refs_1_, ...), custom_call_target="tpu_custom_call" | custom-call | bytes 6291456 | tf_op jit(solution)/shard_map/pick/pallas_call | solution.py:94
  38.5 1.2 %collective-permute-start.9 = (bf16[12,512,128]{2,1,0:T(8,128)(2,1)}, bf16[12,512,128]{2,1,0:T(8,128)(2,1)}, u32[]{:S(2)}, u32[]{:S(2)}) collective-permute-start(bf16[12,512,128]{2,1,0:T(8,128)(2,1)} %get-tuple-element.19), channel_id=1, source_target_pairs={{0,32},{1,9},{2,34},{3,11},{4,36},{5,13},{6,38},{7,15},{8,40},{9,1... | collective-permute-start | bytes 4718600 | tf_op jit(solution)/shard_map/ppermute | solution.py:31
  39.7 1.5 %collective-permute-start.10 = (bf16[12,512,128]{2,1,0:T(8,128)(2,1)}, bf16[12,512,128]{2,1,0:T(8,128)(2,1)}, u32[]{:S(2)}, u32[]{:S(2)}) collective-permute-start(bf16[12,512,128]{2,1,0:T(8,128)(2,1)} %get-tuple-element.20), channel_id=1, source_target_pairs={{0,96},{1,25},{2,98},{3,27},{4,100},{5,29},{6,102},{7,31},{8,104},... | collective-permute-start | bytes 4718600 | tf_op jit(solution)/shard_map/ppermute | solution.py:31
  43.4 1.3 %collective-permute-start.6 = (bf16[48,8192]{1,0:T(8,128)(2,1)}, bf16[48,8192]{1,0:T(8,128)(2,1)S(1)}, u32[]{:S(2)}, u32[]{:S(2)}) collective-permute-start(bf16[48,8192]{1,0:T(8,128)(2,1)} %collective-permute-done.4.refs_4_), channel_id=1, source_target_pairs={{0,1},{1,0},{2,3},{3,2},{4,5},{5,4},{6,7},{7,6},{8,9},{9,8},{10,11... | collective-permute-start | bytes 2359304 | tf_op jit(solution)/shard_map/ppermute | solution.py:31
  46.8 1.6 %copy-done.1 = bf16[8192,128]{1,0:T(8,128)(2,1)S(1)} copy-done((bf16[8192,128]{1,0:T(8,128)(2,1)S(1)}, bf16[8192,128]{1,0:T(8,128)(2,1)}, u32[]{:S(2)}) %copy-start.1) | copy-done | bytes 2097176
  48.4 12.0 %project.2 = (bf16[4,384,128]{2,1,0:T(8,128)(2,1)S(1)}, bf16[384,128]{1,0:T(8,128)(2,1)S(1)}, bf16[384,128]{1,0:T(8,128)(2,1)S(1)}) custom-call(s32[8]{0:T(128)S(1)} %stack.81.refs_0_, bf16[48,8192]{1,0:T(8,128)(2,1)S(1)} %norm.1.refs_1_, bf16[48,8192]{1,0:T(8,128)(2,1)S(1)} %collective-permute-done.refs_2_, ...), custom_call_target="tpu_custom_call" | custom-call | bytes 1048576 | tf_op jit(solution)/shard_map/project/pallas_call | solution.py:167
  60.5 1.1 %slice.38 = bf16[4,512,128]{2,1,0:T(8,128)(2,1)S(1)} slice(bf16[12,512,128]{2,1,0:T(8,128)(2,1)} %collective-permute-done.9.refs_5_), slice={[8:12], [0:512], [0:128]} | slice | bytes 1048576 | tf_op jit(solution)/shard_map/slice | solution.py:418
  61.5 1.3 %collective-permute-start.11 = (bf16[4,512,128]{2,1,0:T(8,128)(2,1)S(1)}, bf16[4,512,128]{2,1,0:T(8,128)(2,1)S(1)}, u32[]{:S(2)}, u32[]{:S(2)}) collective-permute-start(bf16[4,512,128]{2,1,0:T(8,128)(2,1)S(1)} %slice.38), channel_id=1, source_target_pairs={{0,32},{1,9},{2,34},{3,11},{4,36},{5,13},{6,38},{7,15},{8,40},{9,1... | collective-permute-start | bytes 1572872 | tf_op jit(solution)/shard_map/ppermute | solution.py:31
  63.9 1.5 %collective-permute-start.12 = (bf16[4,512,128]{2,1,0:T(8,128)(2,1)S(1)}, bf16[4,512,128]{2,1,0:T(8,128)(2,1)S(1)}, u32[]{:S(2)}, u32[]{:S(2)}) collective-permute-start(bf16[4,512,128]{2,1,0:T(8,128)(2,1)S(1)} %slice.39), channel_id=1, source_target_pairs={{0,96},{1,25},{2,98},{3,27},{4,100},{5,29},{6,102},{7,31},{8,104},... | collective-permute-start | bytes 1572872 | tf_op jit(solution)/shard_map/ppermute | solution.py:31
  65.5 8.7 %project.3.high_ref = bf16[4,384,128]{2,1,0:T(8,128)(2,1)S(1)} custom-call(s32[8]{0:T(128)S(1)} %stack.81.refs_0_, bf16[48,8192]{1,0:T(8,128)(2,1)S(1)} %norm.1.refs_1_, bf16[48,8192]{1,0:T(8,128)(2,1)S(1)} %collective-permute-done.refs_2_, bf16[48,8192]{1,0:T(8,128)(2,1)S(1)} %collective-permute-done.1.refs_3_, ...), custom_call_target="tpu_custom_call" | custom-call | bytes 1048576 | tf_op jit(solution)/shard_map/project/pallas_call | solution.py:167
  74.4 18.1 %attend.1 = bf16[384,1024]{1,0:T(8,128)(2,1)} custom-call(s32[3,8]{1,0:T(4,128)S(1)} %pad_add_fusion.where_ref, s32[3]{0:T(128)S(1)} %fusion.10.count_ref, bf16[4,384,128]{2,1,0:T(8,128)(2,1)S(1)} %get-tuple-element.16.low_ref, bf16[4,384,128]{2,1,0:T(8,128)(2,1)S(1)} %project.3.high_ref, bf16[384,128]{1,0:T(8,128)(2,1)S(1)} %get-tuple-element.17.nk_ref, ...), custom_call_target="tpu_custom_call" | custom-call | flops 6442450944 | bytes 8388608 | tf_op jit(solution)/shard_map/attend/pallas_call | solution.py:310
  (66 shorter events, 9.7 us)
Async XLA Ops:
  0.0 5.1 %copy-start.2 = (bf16[1,48,8192]{2,1,0:T(8,128)(2,1)S(1)}, bf16[1,48,8192]{2,1,0:T(8,128)(2,1)}, u32[]{:S(2)}) copy-start(bf16[1,48,8192]{2,1,0:T(8,128)(2,1)} %param.10) | copy-start | bytes 2359300
  0.0 10.2 %copy-start.9 = (s32[16,8]{0,1:T(8,128)S(1)}, s32[16,8]{0,1:T(8,128)}, u32[]{:S(2)}) copy-start(s32[16,8]{0,1:T(8,128)} %param.18) | copy-start | bytes 1540
  0.0 10.3 %copy-start.8 = (s32[1,384]{1,0:T(1,128)S(1)}, s32[1,384]{1,0:T(1,128)}, u32[]{:S(2)}) copy-start(s32[1,384]{1,0:T(1,128)} %npos_ref.1) | copy-start | bytes 4612
  0.0 10.3 %copy-start.10 = (s32[64]{0:T(128)S(1)}, s32[64]{0:T(128)}, u32[]{:S(2)}) copy-start(s32[64]{0:T(128)} %param.17) | copy-start | bytes 772
  1.4 16.2 %collective-permute-start.2 = (bf16[8,512,128]{2,1,0:T(8,128)(2,1)S(1)}, bf16[8,512,128]{2,1,0:T(8,128)(2,1)}, u32[]{:S(2)}, u32[]{:S(2)}) collective-permute-start(bf16[8,512,128]{2,1,0:T(8,128)(2,1)S(1)} %pad_maximum_fusion.1.first_ref.own.refs_0_), channel_id=1, source_target_pairs={{0,8},{1,33},{2,10},{3,35},{4,12},{5,37},{6,14},{7,39},{8,16},{9,4... | collective-permute-start | bytes 3145736 | tf_op jit(solution)/shard_map/ppermute | solution.py:31
  3.6 15.2 %collective-permute-start.3 = (bf16[8,512,128]{2,1,0:T(8,128)(2,1)S(1)}, bf16[8,512,128]{2,1,0:T(8,128)(2,1)}, u32[]{:S(2)}, u32[]{:S(2)}) collective-permute-start(bf16[8,512,128]{2,1,0:T(8,128)(2,1)S(1)} %pad_maximum_fusion.1.first_ref.own.refs_0_), channel_id=1, source_target_pairs={{0,24},{1,97},{2,26},{3,99},{4,28},{5,101},{6,30},{7,103},{8,0},{9... | collective-permute-start | bytes 3145736 | tf_op jit(solution)/shard_map/ppermute | solution.py:31
  5.1 0.7 copy-start.7
  6.3 20.6 %collective-permute-start = (bf16[48,8192]{1,0:T(8,128)(2,1)S(1)}, bf16[48,8192]{1,0:T(8,128)(2,1)S(1)}, u32[]{:S(2)}, u32[]{:S(2)}) collective-permute-start(bf16[48,8192]{1,0:T(8,128)(2,1)S(1)} %norm.1.refs_1_), channel_id=1, source_target_pairs={{0,2},{1,3},{2,4},{3,5},{4,6},{5,7},{6,0},{7,1},{8,10},{9,11},{10,... | collective-permute-start | bytes 2359304 | tf_op jit(solution)/shard_map/ppermute | solution.py:31
  8.0 18.9 %collective-permute-start.1 = (bf16[48,8192]{1,0:T(8,128)(2,1)S(1)}, bf16[48,8192]{1,0:T(8,128)(2,1)S(1)}, u32[]{:S(2)}, u32[]{:S(2)}) collective-permute-start(bf16[48,8192]{1,0:T(8,128)(2,1)S(1)} %norm.1.refs_1_), channel_id=1, source_target_pairs={{0,6},{1,7},{2,0},{3,1},{4,2},{5,3},{6,4},{7,5},{8,14},{9,15},{10,... | collective-permute-start | bytes 2359304 | tf_op jit(solution)/shard_map/ppermute | solution.py:31
  18.7 15.3 %collective-permute-start.7 = (bf16[4,512,128]{2,1,0:T(8,128)(2,1)S(1)}, bf16[4,512,128]{2,1,0:T(8,128)(2,1)S(1)}, u32[]{:S(2)}, u32[]{:S(2)}) collective-permute-start(bf16[4,512,128]{2,1,0:T(8,128)(2,1)S(1)} %slice.40), channel_id=1, source_target_pairs={{0,8},{1,33},{2,10},{3,35},{4,12},{5,37},{6,14},{7,39},{8,16},{9,4... | collective-permute-start | bytes 1572872 | tf_op jit(solution)/shard_map/ppermute | solution.py:31
  19.9 14.1 %collective-permute-start.8 = (bf16[4,512,128]{2,1,0:T(8,128)(2,1)S(1)}, bf16[4,512,128]{2,1,0:T(8,128)(2,1)S(1)}, u32[]{:S(2)}, u32[]{:S(2)}) collective-permute-start(bf16[4,512,128]{2,1,0:T(8,128)(2,1)S(1)} %slice.41), channel_id=1, source_target_pairs={{0,24},{1,97},{2,26},{3,99},{4,28},{5,101},{6,30},{7,103},{8,0},{9... | collective-permute-start | bytes 1572872 | tf_op jit(solution)/shard_map/ppermute | solution.py:31
  28.5 18.3 %collective-permute-start.5 = (bf16[144,8192]{1,0:T(8,128)(2,1)}, bf16[144,8192]{1,0:T(8,128)(2,1)}, u32[]{:S(2)}, u32[]{:S(2)}) collective-permute-start(bf16[144,8192]{1,0:T(8,128)(2,1)} %pad_maximum_fusion), channel_id=1, source_target_pairs={{0,1},{1,0},{2,3},{3,2},{4,5},{5,4},{6,7},{7,6},{8,9},{9,8},{10,11... | collective-permute-start | bytes 7077896 | tf_op jit(solution)/shard_map/ppermute | solution.py:31
  31.2 12.2 %collective-permute-start.4 = (bf16[48,8192]{1,0:T(8,128)(2,1)}, bf16[48,8192]{1,0:T(8,128)(2,1)}, u32[]{:S(2)}, u32[]{:S(2)}) collective-permute-start(bf16[48,8192]{1,0:T(8,128)(2,1)} %broadcast_select_fusion), channel_id=1, source_target_pairs={{0,2},{1,7},{2,4},{3,1},{4,6},{5,3},{6,0},{7,5},{8,10},{9,15},{10,... | collective-permute-start | bytes 2359304 | tf_op jit(solution)/shard_map/ppermute | solution.py:31
  33.9 3.7 %copy-start.5 = (bf16[4,512,128]{2,1,0:T(8,128)(2,1)}, bf16[4,512,128]{2,1,0:T(8,128)(2,1)S(1)}, u32[]{:S(2)}) copy-start(bf16[4,512,128]{2,1,0:T(8,128)(2,1)S(1)} %collective-permute-done.8.v_far.refs_4_) | copy-start | bytes 1572868
  37.6 0.8 copy-start.3
  38.5 22.0 %collective-permute-start.9 = (bf16[12,512,128]{2,1,0:T(8,128)(2,1)}, bf16[12,512,128]{2,1,0:T(8,128)(2,1)}, u32[]{:S(2)}, u32[]{:S(2)}) collective-permute-start(bf16[12,512,128]{2,1,0:T(8,128)(2,1)} %get-tuple-element.19), channel_id=1, source_target_pairs={{0,32},{1,9},{2,34},{3,11},{4,36},{5,13},{6,38},{7,15},{8,40},{9,1... | collective-permute-start | bytes 4718600 | tf_op jit(solution)/shard_map/ppermute | solution.py:31
  39.7 20.8 %collective-permute-start.10 = (bf16[12,512,128]{2,1,0:T(8,128)(2,1)}, bf16[12,512,128]{2,1,0:T(8,128)(2,1)}, u32[]{:S(2)}, u32[]{:S(2)}) collective-permute-start(bf16[12,512,128]{2,1,0:T(8,128)(2,1)} %get-tuple-element.20), channel_id=1, source_target_pairs={{0,96},{1,25},{2,98},{3,27},{4,100},{5,29},{6,102},{7,31},{8,104},... | collective-permute-start | bytes 4718600 | tf_op jit(solution)/shard_map/ppermute | solution.py:31
  42.4 4.4 %copy-start = (bf16[8192,128]{1,0:T(8,128)(2,1)S(1)}, bf16[8192,128]{1,0:T(8,128)(2,1)}, u32[]{:S(2)}) copy-start(bf16[8192,128]{1,0:T(8,128)(2,1)} %refs_8_.1) | copy-start | bytes 6291460
  43.4 3.4 %collective-permute-start.6 = (bf16[48,8192]{1,0:T(8,128)(2,1)}, bf16[48,8192]{1,0:T(8,128)(2,1)S(1)}, u32[]{:S(2)}, u32[]{:S(2)}) collective-permute-start(bf16[48,8192]{1,0:T(8,128)(2,1)} %collective-permute-done.4.refs_4_), channel_id=1, source_target_pairs={{0,1},{1,0},{2,3},{3,2},{4,5},{5,4},{6,7},{7,6},{8,9},{9,8},{10,11... | collective-permute-start | bytes 2359304 | tf_op jit(solution)/shard_map/ppermute | solution.py:31
  46.8 1.6 %copy-start.1 = (bf16[8192,128]{1,0:T(8,128)(2,1)S(1)}, bf16[8192,128]{1,0:T(8,128)(2,1)}, u32[]{:S(2)}) copy-start(bf16[8192,128]{1,0:T(8,128)(2,1)} %refs_9_.1) | copy-start | bytes 6291460
  61.5 12.7 %collective-permute-start.11 = (bf16[4,512,128]{2,1,0:T(8,128)(2,1)S(1)}, bf16[4,512,128]{2,1,0:T(8,128)(2,1)S(1)}, u32[]{:S(2)}, u32[]{:S(2)}) collective-permute-start(bf16[4,512,128]{2,1,0:T(8,128)(2,1)S(1)} %slice.38), channel_id=1, source_target_pairs={{0,32},{1,9},{2,34},{3,11},{4,36},{5,13},{6,38},{7,15},{8,40},{9,1... | collective-permute-start | bytes 1572872 | tf_op jit(solution)/shard_map/ppermute | solution.py:31
  63.9 10.3 %collective-permute-start.12 = (bf16[4,512,128]{2,1,0:T(8,128)(2,1)S(1)}, bf16[4,512,128]{2,1,0:T(8,128)(2,1)S(1)}, u32[]{:S(2)}, u32[]{:S(2)}) collective-permute-start(bf16[4,512,128]{2,1,0:T(8,128)(2,1)S(1)} %slice.39), channel_id=1, source_target_pairs={{0,96},{1,25},{2,98},{3,27},{4,100},{5,29},{6,102},{7,31},{8,104},... | collective-permute-start | bytes 1572872 | tf_op jit(solution)/shard_map/ppermute | solution.py:31
  65.5 8.9 %copy-start.4 = (bf16[4,512,128]{2,1,0:T(8,128)(2,1)S(1)}, bf16[4,512,128]{2,1,0:T(8,128)(2,1)}, u32[]{:S(2)}) copy-start(bf16[4,512,128]{2,1,0:T(8,128)(2,1)} %copy-done.3) | copy-start | bytes 1572868
  65.5 8.9 %copy-start.6 = (bf16[4,512,128]{2,1,0:T(8,128)(2,1)S(1)}, bf16[4,512,128]{2,1,0:T(8,128)(2,1)}, u32[]{:S(2)}) copy-start(bf16[4,512,128]{2,1,0:T(8,128)(2,1)} %copy-done.5) | copy-start | bytes 1572868
